TPU v7x, 32 devices: a whole 2x2x4 slice. The times are simulated.
32 devices in a mesh: batch: 4 (over y, x), rows: 8 (over z, core).
Axes of the slice: x: 2, y: 2, z: 4, core: 2. Of those that a mesh axis runs over, the one named last changes fastest.
Arguments:
- image_in: float32 [4, 128, 16, 512], P('batch', 'rows'), may hold values from -40 to 40
- cotangent: float32 [4, 128, 16, 512], P('batch', 'rows'), may hold values from -6 to 6
- slot_rows: int32 [6144], replicated, may hold values from 0 to 6143, as said below
- master: float32 [6144, 512], P(('batch', 'rows')), may hold values from -2 to 2
- first_moment: float32 [6144, 512], P(('batch', 'rows')), may hold values from -1025 to 1025
- second_moment: float32 [6144, 512], P(('batch', 'rows')), may hold values from 0 to 8192, as said below
Outputs:
- block_out: float32 [4, 128, 16, 512], P('batch', 'rows')
- grad_in: float32 [4, 128, 16, 512], P('batch', 'rows')
- grad_slots: float32 [6144, 512], P(('batch', 'rows'))
- new_first: float32 [6144, 512], P(('batch', 'rows'))
- new_second: float32 [6144, 512], P(('batch', 'rows'))
- new_master: float32 [6144, 512], P(('batch', 'rows'))
- new_copy: bfloat16 [6144, 512], P(('batch', 'rows'))
Inputs may be any that keep to these rules, and one draw needn't show every extreme that they name: `slot_rows`: A permutation: each table row is held by exactly one owner slot; slot s is on device s // 192 of batch+rows (batch slowest). `second_moment`: Positive.
All inputs are finite; a program needn't handle non-finite values.
Results may differ from a plain program's by a relative error of at most 0.012.
Values may be sent and summed in bfloat16 or wider, within the bound.
A program may use at most 192 MiB of HBM per device.

v0:
```python
import jax
import jax.numpy as jnp
from jax import lax
from jax.sharding import PartitionSpec as P

C = 512
FF = 2048
KL = 31
KS = 5
STEP = 10


norm_eps = 1e-05
beta_one = 0.9
beta_two = 0.999
adam_eps = 1e-08
decay_rate = 0.05
matrix_rate = 0.05
norm_rate = 0.5
highest = lax.Precision.HIGHEST


def with_halo(cells, sides, width):
    for axis, dim in sides:
        count = lax.axis_size(axis)
        ends = count - 1
        head = lax.slice_in_dim(cells, 0, width, axis=dim)
        tail = lax.slice_in_dim(cells, cells.shape[dim] - width, cells.shape[dim], axis=dim)
        cells = jnp.concatenate(
            [
                lax.ppermute(tail, axis, [(i, (i + 1) % count) for i in range(ends)]),
                cells,
                lax.ppermute(head, axis, [((i + 1) % count, i) for i in range(ends)]),
            ],
            axis=dim,
        )
    return cells


def passed_along(value, axis, steps):
    count = lax.axis_size(axis)
    leading, last = (max(0, -steps), min(count, count - steps))
    return lax.ppermute(value, axis, [(source, source + steps) for source in range(leading, last)])


def count_all(row_count):
    return row_count * lax.axis_size("batch") * lax.axis_size("rows")


def moments(values):
    every = count_all(values.shape[0])
    sum_one = lax.psum(jnp.sum(values, axis=0), ("batch", "rows"))
    centre = sum_one / every
    shifted = values - centre
    sum_two = lax.psum(jnp.sum(shifted * shifted, axis=0), ("batch", "rows"))
    spread = sum_two / every
    inv_std = lax.rsqrt(spread + norm_eps)
    return (shifted * inv_std, inv_std)


def batch_norm(values, gain_row, bias_row):
    normed, inv_std = moments(values)
    return (normed * gain_row + bias_row, normed, inv_std)


def norm_back(grad_out, normed, gain_row, inv_std):
    every = count_all(grad_out.shape[0])
    bias_part = jnp.sum(grad_out, axis=0)
    gain_part = jnp.sum(grad_out * normed, axis=0)
    sum_bias, sum_gain = lax.psum((bias_part, gain_part), ("batch", "rows"))
    grad_input = gain_row * inv_std * (grad_out - sum_bias / every - normed * (sum_gain / every))
    return (grad_input, gain_part, bias_part)


def depth_conv(padded_u, kernel_large, kernel_small, exact):
    reach_large = (kernel_large.shape[0] - 1) // 2
    reach_small = (kernel_small.shape[0] - 1) // 2
    rows_here = padded_u.shape[1] - 2 * reach_large
    channels = padded_u.shape[3]
    layout_names = ("NHWC", "HWIO", "NHWC")
    inner_rows = lax.slice_in_dim(
        padded_u, reach_large - reach_small, reach_large + rows_here + reach_small, axis=1
    )
    if exact:
        large_out = lax.conv_general_dilated(
            padded_u,
            kernel_large[:, :, None, :],
            (1, 1),
            ((0, 0), (reach_large, reach_large)),
            dimension_numbers=layout_names,
            feature_group_count=channels,
            precision=highest,
        )
        small_out = lax.conv_general_dilated(
            inner_rows,
            kernel_small[:, :, None, :],
            (1, 1),
            ((0, 0), (reach_small, reach_small)),
            dimension_numbers=layout_names,
            feature_group_count=channels,
            precision=highest,
        )
    else:
        large_out = lax.conv_general_dilated(
            padded_u,
            kernel_large[:, :, None, :],
            (1, 1),
            ((0, 0), (reach_large, reach_large)),
            dimension_numbers=layout_names,
            feature_group_count=channels,
            preferred_element_type=jnp.float32,
        )
        small_out = lax.conv_general_dilated(
            inner_rows,
            kernel_small[:, :, None, :],
            (1, 1),
            ((0, 0), (reach_small, reach_small)),
            dimension_numbers=layout_names,
            feature_group_count=channels,
            preferred_element_type=jnp.float32,
        )
    return jnp.concatenate([large_out, small_out], axis=3)


def depth_exact(padded_u, kernel_large, kernel_small):
    return depth_conv(padded_u, kernel_large, kernel_small, True)


def body(image_in, cotangent, slot_rows, master, first_moment, second_moment):
    batch_here = image_in.shape[0]
    rows_here = image_in.shape[1]
    cols_here = image_in.shape[2]
    pixels = batch_here * rows_here * cols_here
    own_copy = master.astype(jnp.bfloat16)
    gathered = lax.all_gather(own_copy, ("batch", "rows"), axis=0, tiled=True)
    ordered = jnp.zeros_like(gathered).at[slot_rows].set(gathered)
    w_in = ordered[0:C]
    w_out = ordered[C : 2 * C]
    w_up = ordered[2 * C : 2 * C + FF].reshape(C, FF)
    w_down = ordered[2 * C + FF : 2 * C + 2 * FF]
    offset = 2 * C + 2 * FF
    k_large = ordered[offset : offset + KL * KL].reshape(KL, KL, C)
    offset = offset + KL * KL
    k_small = ordered[offset : offset + KS * KS].reshape(KS, KS, C)
    offset = offset + KS * KS
    norm_start = offset
    norm_rows = ordered[offset : offset + 10].astype(jnp.float32)
    offset = offset + 10
    mid_gain = ordered[offset : offset + FF // C].astype(jnp.float32).reshape(FF)
    mid_bias = ordered[offset + FF // C : offset + 2 * (FF // C)].astype(jnp.float32).reshape(FF)
    x_flat = image_in.reshape(pixels, C)
    pre_out, pre_hat, pre_inv = batch_norm(x_flat, norm_rows[0], norm_rows[1])
    pre_low = pre_out.astype(jnp.bfloat16)
    z_first = jnp.dot(pre_low, w_in, preferred_element_type=jnp.float32)
    u_val, gelu_first = jax.vjp(jax.nn.gelu, z_first)
    u_low = u_val.astype(jnp.bfloat16).reshape(batch_here, rows_here, cols_here, C)
    rim_width = (KL - 1) // 2
    place = lax.axis_index("rows")
    row_ids = lax.broadcasted_iota(jnp.int32, (1, rows_here + 2 * rim_width, 1, 1), 1)
    upper_cut = (row_ids < rim_width) & (place == 0)
    lower_cut = (row_ids >= rows_here + rim_width) & (place == lax.axis_size("rows") - 1)
    cut_rows = upper_cut | lower_cut
    keep_rows = jnp.where(cut_rows, 0.0, 1.0).astype(jnp.float32)
    padded = with_halo(u_low, (("rows", 1),), rim_width)
    wide_low = jnp.where(cut_rows, jnp.zeros((), jnp.bfloat16), padded)
    pair_out = depth_conv(wide_low, k_large, k_small, False)
    pair_flat = pair_out.reshape(pixels, 2 * C)
    pair_gain = jnp.concatenate([norm_rows[2], norm_rows[4]])
    pair_bias = jnp.concatenate([norm_rows[3], norm_rows[5]])
    pair_norm, pair_hat, pair_inv = batch_norm(pair_flat, pair_gain, pair_bias)
    s_val = pair_norm[:, :C] + pair_norm[:, C:]
    t_val, gelu_second = jax.vjp(jax.nn.gelu, s_val)
    t_low = t_val.astype(jnp.bfloat16)
    p_val = jnp.dot(t_low, w_out, preferred_element_type=jnp.float32)
    proj_out, proj_hat, proj_inv = batch_norm(p_val, norm_rows[6], norm_rows[7])
    mid_sum = x_flat + proj_out
    ffn_out, ffn_hat, ffn_inv = batch_norm(mid_sum, norm_rows[8], norm_rows[9])
    ffn_low = ffn_out.astype(jnp.bfloat16)
    hidden = jnp.dot(ffn_low, w_up, preferred_element_type=jnp.float32)
    hid_out, hid_hat, hid_inv = batch_norm(hidden, mid_gain, mid_bias)
    act_val, gelu_third = jax.vjp(jax.nn.gelu, hid_out)
    act_low = act_val.astype(jnp.bfloat16)
    result = mid_sum + jnp.dot(act_low, w_down, preferred_element_type=jnp.float32)
    grad_y = cotangent.reshape(pixels, C)
    grad_low = grad_y.astype(jnp.bfloat16)
    g_down = jnp.einsum("pf,pc->fc", act_low, grad_low, preferred_element_type=jnp.float32)
    grad_act = jnp.einsum("pc,fc->pf", grad_low, w_down, preferred_element_type=jnp.float32)
    grad_hid = gelu_third(grad_act)[0]
    grad_hidden, g_mid_gain, g_mid_bias = norm_back(grad_hid, hid_hat, mid_gain, hid_inv)
    hidden_low = grad_hidden.astype(jnp.bfloat16)
    g_up = jnp.einsum("pc,pf->cf", ffn_low, hidden_low, preferred_element_type=jnp.float32)
    grad_ffn = jnp.einsum("pf,cf->pc", hidden_low, w_up, preferred_element_type=jnp.float32)
    grad_mid_in, g_ffn_gain, g_ffn_bias = norm_back(grad_ffn, ffn_hat, norm_rows[8], ffn_inv)
    grad_mid = grad_y + grad_mid_in
    grad_p, g_proj_gain, g_proj_bias = norm_back(grad_mid, proj_hat, norm_rows[6], proj_inv)
    p_low = grad_p.astype(jnp.bfloat16)
    g_out = jnp.einsum("pc,pd->cd", t_low, p_low, preferred_element_type=jnp.float32)
    grad_t = jnp.einsum("pd,cd->pc", p_low, w_out, preferred_element_type=jnp.float32)
    grad_s = gelu_second(grad_t)[0]
    grad_pair, g_pair_gain, g_pair_bias = norm_back(
        jnp.concatenate([grad_s, grad_s], axis=1), pair_hat, pair_gain, pair_inv
    )
    unused_out, conv_pull = jax.vjp(
        depth_exact,
        wide_low.astype(jnp.float32),
        k_large.astype(jnp.float32),
        k_small.astype(jnp.float32),
    )
    grad_wide, g_large, g_small = conv_pull(
        grad_pair.reshape(batch_here, rows_here, cols_here, 2 * C)
    )
    grad_wide = grad_wide * keep_rows
    from_next = passed_along(grad_wide[:, :rim_width].astype(jnp.bfloat16), "rows", -1).astype(
        jnp.float32
    )
    from_prev = passed_along(
        grad_wide[:, rows_here + rim_width :].astype(jnp.bfloat16), "rows", 1
    ).astype(jnp.float32)
    grad_u = grad_wide[:, rim_width : rim_width + rows_here]
    grad_u = grad_u.at[:, rows_here - rim_width :].add(from_next)
    grad_u = grad_u.at[:, :rim_width].add(from_prev)
    grad_z = gelu_first(grad_u.reshape(pixels, C))[0]
    z_low = grad_z.astype(jnp.bfloat16)
    g_in = jnp.einsum("pc,pd->cd", pre_low, z_low, preferred_element_type=jnp.float32)
    grad_pre = jnp.einsum("pd,cd->pc", z_low, w_in, preferred_element_type=jnp.float32)
    grad_x_in, g_pre_gain, g_pre_bias = norm_back(grad_pre, pre_hat, norm_rows[0], pre_inv)
    grad_x = grad_mid + grad_x_in
    norm_grads = jnp.stack(
        [
            g_pre_gain,
            g_pre_bias,
            g_pair_gain[:C],
            g_pair_bias[:C],
            g_pair_gain[C:],
            g_pair_bias[C:],
            g_proj_gain,
            g_proj_bias,
            g_ffn_gain,
            g_ffn_bias,
        ]
    )
    grads_flat = jnp.concatenate(
        [
            g_in,
            g_out,
            g_up.reshape(FF, C),
            g_down,
            g_large.reshape(KL * KL, C),
            g_small.reshape(KS * KS, C),
            norm_grads,
            g_mid_gain.reshape(FF // C, C),
            g_mid_bias.reshape(FF // C, C),
        ],
        axis=0,
    )
    grads_flat = jnp.pad(grads_flat, ((0, gathered.shape[0] - grads_flat.shape[0]), (0, 0)))
    slot_grads = grads_flat[slot_rows]
    reduced = lax.psum_scatter(slot_grads, ("batch", "rows"), scatter_dimension=0, tiled=True)
    own_count = master.shape[0]
    device_pos = lax.axis_index("batch") * lax.axis_size("rows") + lax.axis_index("rows")
    own_rows = lax.dynamic_slice_in_dim(slot_rows, device_pos * own_count, own_count)
    rates = jnp.where(own_rows >= norm_start, norm_rate, matrix_rate)[:, None]
    new_first = beta_one * first_moment + (1.0 - beta_one) * reduced
    new_second = beta_two * second_moment + (1.0 - beta_two) * reduced * reduced
    first_hat = new_first / (1.0 - beta_one**STEP)
    second_hat = new_second / (1.0 - beta_two**STEP)
    new_master = master - rates * (
        first_hat / (jnp.sqrt(second_hat) + adam_eps) + decay_rate * master
    )
    new_copy = new_master.astype(jnp.bfloat16)
    return (
        result.reshape(image_in.shape),
        grad_x.reshape(image_in.shape),
        reduced,
        new_first,
        new_second,
        new_master,
        new_copy,
    )


def solution(mesh):
    in_specs = (
        P("batch", "rows", None, None),
        P("batch", "rows", None, None),
        P(),
        P(("batch", "rows"), None),
        P(("batch", "rows"), None),
        P(("batch", "rows"), None),
    )
    out_specs = (
        P("batch", "rows", None, None),
        P("batch", "rows", None, None),
        P(("batch", "rows"), None),
        P(("batch", "rows"), None),
        P(("batch", "rows"), None),
        P(("batch", "rows"), None),
        P(("batch", "rows"), None),
    )
    return jax.shard_map(body, mesh=mesh, in_specs=in_specs, out_specs=out_specs, check_vma=False)
```

profile of v0, /device:TPU:0, one launch (start us, length us, event | category | flops | bytes accessed | tf_op | source)
XLA Modules:
  0.0 1953.4 jit_solution(5641123091714643962)
XLA Ops:
  10.2 42.3 %psum.140 = f32[512]{0:T(512)S(1)} all-reduce(f32[512]{0:T(512)S(1)} %reduce_sum.188), channel_id=1, replica_groups=mesh['batch'=4,'rows'=8] {'batch','rows'}, use_global_device_ids=true, to_apply=%region_1.0 | all-reduce | flops 512 | bytes 4096 | tf_op jit(solution)/shard_map/psum | solution.py:52
  53.6 40.8 %psum.141 = f32[512]{0:T(512)S(1)} all-reduce(f32[512]{0:T(512)S(1)} %multiply_reduce_fusion.8), channel_id=1, replica_groups=mesh['batch'=4,'rows'=8] {'batch','rows'}, use_global_device_ids=true, to_apply=%region_3.0 | all-reduce | flops 512 | bytes 4096 | tf_op jit(solution)/shard_map/psum | solution.py:55
  96.4 31.1 %scatter_custom_fusion = bf16[6144,512]{1,0:T(8,128)(2,1)} fusion(s32[6144]{0:T(1024)S(1)} %get-tuple-element.81, bf16[6144,512]{1,0:T(8,128)(2,1)} %all-gather.2.cloned.1.call-done, bf16[]{:T(256)} %constant.138.clone.1), kind=kCustom, calls=%fused_computation.2 | custom fusion | bytes 6291968 | tf_op jit(solution)/shard_map/scatter | solution.py:136
  170.6 389.8 %fusion.81 = f32[1,16,16,512]{3,0,2,1:T(1,128)S(1)} fusion(bf16[1,46,16,512]{3,0,2,1:T(2,128)(2,1)S(1)} %broadcast_select_fusion, bf16[31,31,1,512]{3,2,1,0:T(2,128)(2,1)S(1)} %broadcast_in_dim_reshape.10), kind=kOutput, calls=%fused_computation.159 | convolution fusion | flops 130023424 | bytes 2262016 | tf_op jit(solution)/shard_map/conv_general_dilated | solution.py:104
  560.6 42.4 %psum.142 = f32[1024]{0:T(1024)S(1)} all-reduce(f32[1024]{0:T(1024)S(1)} %reduce_sum.190), channel_id=1, replica_groups=mesh['batch'=4,'rows'=8] {'batch','rows'}, use_global_device_ids=true, to_apply=%region_6.7 | all-reduce | flops 1024 | bytes 8192 | tf_op jit(solution)/shard_map/psum | solution.py:52
  603.1 39.3 %psum.143 = f32[1024]{0:T(1024)S(1)} all-reduce(f32[1024]{0:T(1024)S(1)} %multiply_reduce_fusion.2), channel_id=1, replica_groups=mesh['batch'=4,'rows'=8] {'batch','rows'}, use_global_device_ids=true, to_apply=%region_8.9 | all-reduce | flops 1024 | bytes 8192 | tf_op jit(solution)/shard_map/psum | solution.py:55
  645.1 40.8 %psum.144 = f32[512]{0:T(512)S(1)} all-reduce(f32[512]{0:T(512)S(1)} %get-tuple-element.99), channel_id=1, replica_groups=mesh['batch'=4,'rows'=8] {'batch','rows'}, use_global_device_ids=true, to_apply=%region_10.11 | all-reduce | flops 512 | bytes 4096 | tf_op jit(solution)/shard_map/psum | solution.py:52
  686.0 39.3 %psum.145 = f32[512]{0:T(512)S(1)} all-reduce(f32[512]{0:T(512)S(1)} %multiply_reduce_fusion.7), channel_id=1, replica_groups=mesh['batch'=4,'rows'=8] {'batch','rows'}, use_global_device_ids=true, to_apply=%region_12.13 | all-reduce | flops 512 | bytes 4096 | tf_op jit(solution)/shard_map/psum | solution.py:55
  726.0 40.8 %psum.146 = f32[512]{0:T(512)S(1)} all-reduce(f32[512]{0:T(512)S(1)} %get-tuple-element.56), channel_id=1, replica_groups=mesh['batch'=4,'rows'=8] {'batch','rows'}, use_global_device_ids=true, to_apply=%region_14.15 | all-reduce | flops 512 | bytes 4096 | tf_op jit(solution)/shard_map/psum | solution.py:52
  766.8 39.4 %psum.147 = f32[512]{0:T(512)S(1)} all-reduce(f32[512]{0:T(512)S(1)} %multiply_reduce_fusion.6), channel_id=1, replica_groups=mesh['batch'=4,'rows'=8] {'batch','rows'}, use_global_device_ids=true, to_apply=%region_16.17 | all-reduce | flops 512 | bytes 4096 | tf_op jit(solution)/shard_map/psum | solution.py:55
  809.4 40.8 %psum.148 = f32[2048]{0:T(1024)S(1)} all-reduce(f32[2048]{0:T(1024)S(1)} %get-tuple-element.101), channel_id=1, replica_groups=mesh['batch'=4,'rows'=8] {'batch','rows'}, use_global_device_ids=true, to_apply=%region_18.19 | all-reduce | flops 2048 | bytes 16384 | tf_op jit(solution)/shard_map/psum | solution.py:52
  850.4 39.3 %psum.149 = f32[2048]{0:T(1024)S(1)} all-reduce(f32[2048]{0:T(1024)S(1)} %multiply_reduce_fusion.1), channel_id=1, replica_groups=mesh['batch'=4,'rows'=8] {'batch','rows'}, use_global_device_ids=true, to_apply=%region_20.21 | all-reduce | flops 2048 | bytes 16384 | tf_op jit(solution)/shard_map/psum | solution.py:55
  894.9 40.9 %all-reduce.5 = (f32[2048]{0:T(1024)S(1)}, f32[2048]{0:T(1024)}) all-reduce(f32[2048]{0:T(1024)S(1)} %get-tuple-element.32, f32[2048]{0:T(1024)S(1)} %get-tuple-element.31), channel_id=1, replica_groups=mesh['batch'=4,'rows'=8] {'batch','rows'}, use_global_device_ids=true, to_apply=%region_24.25 | all-reduce | flops 4096 | bytes 32768 | tf_op jit(solution)/shard_map/psum | solution.py:70
  940.6 39.8 %all-reduce.4 = (f32[512]{0:T(512)S(1)}, f32[512]{0:T(512)S(1)}) all-reduce(f32[512]{0:T(512)S(1)} %get-tuple-element.38, f32[512]{0:T(512)S(1)} %get-tuple-element.37), channel_id=1, replica_groups=mesh['batch'=4,'rows'=8] {'batch','rows'}, use_global_device_ids=true, to_apply=%region_28.29 | all-reduce | flops 1024 | bytes 8192 | tf_op jit(solution)/shard_map/psum | solution.py:70
  983.0 40.7 %all-reduce.3 = (f32[512]{0:T(512)S(1)}, f32[512]{0:T(512)S(1)}) all-reduce(f32[512]{0:T(512)S(1)} %get-tuple-element.36, f32[512]{0:T(512)S(1)} %get-tuple-element.35), channel_id=1, replica_groups=mesh['batch'=4,'rows'=8] {'batch','rows'}, use_global_device_ids=true, to_apply=%region_32.33 | all-reduce | flops 1024 | bytes 8192 | tf_op jit(solution)/shard_map/psum | solution.py:70
  1028.8 39.7 %all-reduce.2 = (f32[1024]{0:T(1024)S(1)}, f32[1024]{0:T(1024)S(1)}) all-reduce(f32[1024]{0:T(1024)S(1)} %fusion.18, f32[1024]{0:T(1024)S(1)} %maximum_reduce_fusion), channel_id=1, replica_groups=mesh['batch'=4,'rows'=8] {'batch','rows'}, use_global_device_ids=true, to_apply=%region_36.37 | all-reduce | flops 2048 | bytes 16384 | tf_op jit(solution)/shard_map/psum | solution.py:70
  1077.6 11.6 convolution_reduce_fusion.1
  1090.1 434.6 %convolution_reduce_fusion = f32[31,31,512]{2,1,0:T(8,128)} fusion(bf16[1,46,16,512]{3,0,2,1:T(2,128)(2,1)} %copy-done.16, f32[1,16,16,512]{3,2,1,0:T(8,128)S(1)} %get-tuple-element.66), kind=kOutput, calls=%fused_computation.23 | convolution fusion | flops 780140544 | bytes 3246080 | tf_op jit(solution)/shard_map/transpose(jvp())/conv_general_dilated | solution.py:85
  1533.7 152.5 %fusion.80 = (bf16[1,46,16,512]{3,0,2,1:T(2,128)(2,1)S(1)}, f32[1,46,16,512]{3,0,2,1:T(1,128)S(1)}) fusion(f32[46]{0:T(128)S(1)} %copy-done.40, f32[1,46,16,512]{3,0,2,1:T(1,128)S(1)} %fusion.53, f32[31,31,512,1]{2,3,1,0:T(1,128)S(1)} %copy-done.14, f32[1,16,16,512]{3,2,1,0:T(8,128)S(1)} %get-tuple-element.66), kind=kOutput, calls=%fused_computation.158 | convolution fusion | flops 781271040 | bytes 6260920 | tf_op jit(solution)/shard_map/transpose(jvp())/conv_general_dilated | solution.py:85
  1706.5 36.7 %concatenate.67 = f32[6124,512]{1,0:T(8,128)} concatenate(f32[512,512]{1,0:T(8,128)} %fusion.83, f32[512,512]{1,0:T(8,128)} %fusion.84, f32[2048,512]{1,0:T(8,128)} %reshape.398, f32[2048,512]{1,0:T(8,128)} %fusion.64, f32[961,512]{1,0:T(8,128)} %reshape.399, f32[25,512]{1,0:T(8,128)S(1)} %reshape.400, f32[1,512]{1,0:T(1,128)S(1)} %bitcast.108, f32[1,512]{1,0:T(1,128)S(1)} %bitcast.107, ...), dimensions={0} | concatenate | bytes 25083904 | tf_op jit(solution)/shard_map/concatenate | solution.py:242
  1743.2 10.6 pad.12
  1753.8 31.1 %gather_fusion = f32[6144,512]{1,0:T(8,128)} fusion(f32[6144,512]{1,0:T(8,128)} %pad.12, s32[6144]{0:T(1024)S(1)} %get-tuple-element.80), kind=kCustom, calls=%fused_computation | custom fusion | bytes 25190400 | tf_op jit(solution)/shard_map/gather | solution.py:257
  1789.5 43.0 %all-reduce.1 = (f32[512]{0:T(512)S(1)}, f32[512]{0:T(512)S(1)}) all-reduce(f32[512]{0:T(512)S(1)} %get-tuple-element.34, f32[512]{0:T(512)S(1)} %get-tuple-element.33), channel_id=1, replica_groups=mesh['batch'=4,'rows'=8] {'batch','rows'}, use_global_device_ids=true, to_apply=%region_40.41 | all-reduce | flops 1024 | bytes 8192 | tf_op jit(solution)/shard_map/psum | solution.py:70
  1834.7 109.4 %reduce-scatter.2.cloned.1.call-done = f32[192,512]{1,0:T(8,128)} async-done(((f32[6144,512]{1,0:T(8,128)}), f32[192,512]{1,0:T(8,128)}) %reduce-scatter.2.cloned.1.call-update) | async-done | bytes 393232 | tf_op jit(solution)/shard_map/reduce_scatter | solution.py:258
  (189 shorter events, 122.0 us)
Async XLA Ops:
  7.2 88.5 %copy-start.13 = (f32[1,16,16,512]{3,2,1,0:T(8,128)S(1)}, f32[1,16,16,512]{3,2,1,0:T(8,128)}, u32[]{:S(2)}) copy-start(f32[1,16,16,512]{3,2,1,0:T(8,128)} %param.11) | copy-start | bytes 1572868
  7.2 89.3 %all-gather.2.cloned.1.call-start = ((), (), s32[]{:S(2)}) async-start(), calls=%async_computation.1 | async-start | bytes 6488064 | tf_op jit(solution)/shard_map/all_gather | solution.py:135
  9.0 1935.1 %reduce-scatter.2.cloned.1.call-start = ((), (), s32[]{:S(2)}) async-start(), calls=%async_computation.2 | async-start | bytes 12976128 | tf_op jit(solution)/shard_map/reduce_scatter | solution.py:258
  134.0 755.8 %copy-start.36 = (f32[1,4,4,128]{3,1,2,0:T(4,128)}, f32[1,4,4,128]{3,1,2,0:T(4,128)S(1)}, u32[]{:S(2)}) copy-start(f32[1,4,4,128]{3,1,2,0:T(4,128)S(1)} %copy.40) | copy-start | bytes 24580
  139.4 21.9 %collective-permute-start = (bf16[1,15,16,512]{3,0,2,1:T(2,128)(2,1)}, bf16[1,15,16,512]{3,0,2,1:T(2,128)(2,1)}, u32[]{:S(2)}, u32[]{:S(2)}) collective-permute-start(bf16[1,15,16,512]{3,0,2,1:T(2,128)(2,1)} %get-tuple-element.68), channel_id=1, source_target_pairs={{0,1},{1,2},{2,3},{3,4},{4,5},{5,6},{6,7},{8,9},{9,10},{10,11},{11... | collective-permute-start | bytes 737288 | tf_op jit(solution)/shard_map/ppermute | solution.py:31
  141.5 19.8 %collective-permute-start.1 = (bf16[1,15,16,512]{3,0,2,1:T(2,128)(2,1)}, bf16[1,15,16,512]{3,0,2,1:T(2,128)(2,1)}, u32[]{:S(2)}, u32[]{:S(2)}) collective-permute-start(bf16[1,15,16,512]{3,0,2,1:T(2,128)(2,1)} %get-tuple-element.69), channel_id=1, source_target_pairs={{1,0},{2,1},{3,2},{4,3},{5,4},{6,5},{7,6},{9,8},{10,9},{11,10},{12... | collective-permute-start | bytes 737288 | tf_op jit(solution)/shard_map/ppermute | solution.py:33
  645.1 161.8 %copy-start.6 = (f32[256,512]{1,0:T(8,128)}, f32[256,512]{1,0:T(8,128)S(1)}, u32[]{:S(2)}) copy-start(f32[256,512]{1,0:T(8,128)S(1)} %get-tuple-element.100) | copy-start | bytes 1572868
  726.0 80.9 %copy-start.2 = (f32[256,512]{1,0:T(8,128)}, f32[256,512]{1,0:T(8,128)S(1)}, u32[]{:S(2)}) copy-start(f32[256,512]{1,0:T(8,128)S(1)} %get-tuple-element.57) | copy-start | bytes 1572868
  939.0 41.5 %copy-start.39 = (f32[512]{0:T(512)S(1)}, f32[512]{0:T(512)}, u32[]{:S(2)}) copy-start(f32[512]{0:T(512)} %get-tuple-element.95) | copy-start | bytes 6148
  940.5 84.5 %copy-start.28 = (f32[512]{0:T(512)}, f32[512]{0:T(512)S(1)}, u32[]{:S(2)}) copy-start(f32[512]{0:T(512)S(1)} %get-tuple-element.38) | copy-start | bytes 6148
  940.5 86.6 %copy-start.26 = (f32[512]{0:T(512)}, f32[512]{0:T(512)S(1)}, u32[]{:S(2)}) copy-start(f32[512]{0:T(512)S(1)} %get-tuple-element.37) | copy-start | bytes 6148
  940.6 83.2 %copy-start.35 = (f32[512]{0:T(512)S(1)}, f32[512]{0:T(512)}, u32[]{:S(2)}) copy-start(f32[512]{0:T(512)} %get-tuple-element.93) | copy-start | bytes 6148
  1025.1 44.0 %copy-start.37 = (f32[1,4,4,128]{3,1,2,0:T(4,128)S(1)}, f32[1,4,4,128]{3,1,2,0:T(4,128)}, u32[]{:S(2)}) copy-start(f32[1,4,4,128]{3,1,2,0:T(4,128)} %copy-done.36) | copy-start | bytes 24580
  1069.0 4.5 copy-start.12
  1527.5 6.1 copy-start.14
  1527.5 6.1 copy-start.40
  1686.2 5.3 copy-start.22
  1688.2 12.3 collective-permute-start.3
  1690.3 8.2 collective-permute-start.2
  1692.0 5.3 copy-start.21
  1786.0 46.5 %copy-start.30 = (f32[512]{0:T(512)S(1)}, f32[512]{0:T(512)}, u32[]{:S(2)}) copy-start(f32[512]{0:T(512)} %get-tuple-element.91) | copy-start | bytes 6148
  1789.5 154.5 %copy-start.15 = (f32[192,512]{1,0:T(8,128)S(1)}, f32[192,512]{1,0:T(8,128)}, u32[]{:S(2)}) copy-start(f32[192,512]{1,0:T(8,128)} %param.13) | copy-start | bytes 1179652
  1789.5 154.5 %copy-start.24 = (f32[192,512]{1,0:T(8,128)S(1)}, f32[192,512]{1,0:T(8,128)}, u32[]{:S(2)}) copy-start(f32[192,512]{1,0:T(8,128)} %param.15) | copy-start | bytes 1179652
  1789.5 154.5 %copy-start.25 = (f32[192,512]{1,0:T(8,128)S(1)}, f32[192,512]{1,0:T(8,128)}, u32[]{:S(2)}) copy-start(f32[192,512]{1,0:T(8,128)} %param.14) | copy-start | bytes 1179652
  (23 other events, 62.1 us)
Sparse Core Ops, SparseCore 0:
  11.6 72.9 all-gather.1
  1785.1 158.9 reduce-scatter.1
where the time goes:
time: 1960 us; the launch traced here: 1950 us
  matrix products  1030 us (53%)
  blocking collectives  609 us (31%)
  local copies, waits for them, and re-layouts  147 us (8%)
  waiting for transfers between devices  109 us (6%)
  other arithmetic  38.5 us (2%)
    conv_general_dilated x3, matrix products, depth_conv(): lax.conv_general_dilated(padded_u, kernel_large[:, :, None, :], (1, 1), (...  977 us
    psum x5, blocking collectives, moments(): sum_one = lax.psum(jnp.sum(values, axis=0), ('batch', 'rows'))  207 us
    psum x5, blocking collectives, norm_back(): sum_bias, sum_gain = lax.psum((bias_part, gain_part), ('batch', 'rows'))  204 us
    psum x5, blocking collectives, moments(): sum_two = lax.psum(jnp.sum(shifted * shifted, axis=0), ('batch', 'rows'))  198 us
    reduce_scatter x1, waiting for transfers between devices, body(): lax.psum_scatter(slot_grads, ('batch', 'rows'), scatter_dimension=0, tile...  109 us
  transfers between devices with their start and end apart: 6, of which 1 were waited for; matrix products, arithmetic and copies ran while one was open for 2% of the time, Pallas kernels for 0%

commit v1 on v0

v1 whole, which is shorter than its diff:
```python
import functools

import jax
import jax.numpy as jnp
import numpy as np
from jax import lax
from jax.sharding import PartitionSpec as P

C = 512
FF = 2048
KL = 31
KS = 5
STEP = 10

norm_eps = 1e-05
beta_one = 0.9
beta_two = 0.999
adam_eps = 1e-08
decay_rate = 0.05
matrix_rate = 0.05
norm_rate = 0.5

TH = 16
TW = 16
NY = 47
NX = 31
NF = 768
REACH = (KL - 1) // 2
AXES = ("batch", "rows")
f32 = jnp.float32
bf16 = jnp.bfloat16


@functools.lru_cache(None)
def tables():
    freqs = [(ky, 0) for ky in range((NY + 1) // 2)]
    freqs += [(ky, kx) for kx in range(1, (NX + 1) // 2) for ky in range(NY)]
    ky = np.array([f[0] for f in freqs], np.int64)[:, None]
    kx = np.array([f[1] for f in freqs], np.int64)[:, None]
    pad = NF - len(freqs)

    def angle(rows, cols):
        ty = (ky * rows.reshape(1, -1)) % NY
        tx = (kx * cols.reshape(1, -1)) % NX
        return 2 * np.pi * (ty / NY + tx / NX)

    def grid(rows, cols):
        r, c = np.meshgrid(rows, cols, indexing="ij")
        return r.reshape(-1), c.reshape(-1)

    def stack(re, im):
        z = np.zeros((pad, re.shape[1]))
        return np.concatenate([re, z, im, z], axis=0)

    r, c = grid(np.arange(-TH, 2 * TH), np.arange(TW))
    used = ((r + REACH >= 0) & (r + REACH < NY - 1)).astype(np.float64)[None]
    t = angle(r + REACH, c)
    a = stack(np.cos(t) * used, -np.sin(t) * used)
    i, j = grid(np.arange(KL), np.arange(KL))
    t = angle(i, j - REACH)
    b = stack(np.cos(t), -np.sin(t))
    lead = REACH - (KS - 1) // 2
    small = ((i >= lead) & (i < lead + KS) & (j >= lead) & (j < lead + KS)).nonzero()[0]
    bs = b[:, small]
    y, x = grid(np.arange(TH), np.arange(TW))
    t = angle(y, x)
    w = np.full((len(freqs), 1), 2.0)
    w[0] = 1.0
    w /= NY * NX
    c = stack(w * np.cos(t), -w * np.sin(t)).T

    def split(m):
        hi = m.astype(np.float32).astype(bf16)
        lo = (m - hi.astype(np.float64)).astype(np.float32).astype(bf16)
        return hi, lo

    return tuple(split(m) for m in (a, b, bs, c))


def dot(a, b, dims=(1, 0)):
    return lax.dot_general(a, b, (((dims[0],), (dims[1],)), ((), ())), preferred_element_type=f32)


def split(v):
    hi = v.astype(bf16)
    lo = (v - hi.astype(f32)).astype(bf16)
    return hi, lo


def dot_exact(pair, low, dims=(1, 0)):
    return dot(pair[0], low, dims) + dot(pair[1], low, dims)


def dot_pair(pair, v, dims=(1, 0)):
    hi, lo = split(v)
    return dot(pair[0], hi, dims) + dot(pair[1], hi, dims) + dot(pair[0], lo, dims)


def times_conj(u, k):
    ur, ui, kr, ki = u[:NF], u[NF:], k[:NF], k[NF:]
    return jnp.concatenate([ur * kr + ui * ki, ui * kr - ur * ki], axis=0)


def times(g, k):
    gr, gi, kr, ki = g[:NF], g[NF:], k[:NF], k[NF:]
    return jnp.concatenate([gr * kr - gi * ki, gr * ki + gi * kr], axis=0)


def exchange(rows):
    return lax.all_gather(jnp.stack(rows), AXES, axis=0)


def local_stats(v):
    m = jnp.mean(v, axis=0)
    d = v - m
    return m, jnp.sum(d * d, axis=0)


def combine(means, seconds, n):
    m = jnp.mean(means, axis=0)
    d = means - m
    total = jnp.sum(seconds, axis=0) + n * jnp.sum(d * d, axis=0)
    return m, total / (n * means.shape[0])


def combine_cross(means_a, means_b, cross, n):
    da = means_a - jnp.mean(means_a, axis=0)
    db = means_b - jnp.mean(means_b, axis=0)
    return (jnp.sum(cross, axis=0) + n * jnp.sum(da * db, axis=0)) / (n * cross.shape[0])


def gelu_grad(v):
    a = np.float32(np.sqrt(2 / np.pi))
    t = jnp.tanh(a * (v + 0.044715 * (v * v * v)))
    return 0.5 * (1 + t) + 0.5 * v * (1 - t * t) * (a * (1 + 3 * 0.044715 * v * v))


def gelu(v):
    a = np.float32(np.sqrt(2 / np.pi))
    return 0.5 * v * (1 + jnp.tanh(a * (v + 0.044715 * (v * v * v))))


def body(image_in, cotangent, slot_rows, master, first_moment, second_moment):
    n = image_in.shape[0] * image_in.shape[1] * image_in.shape[2]
    devices = lax.axis_size("batch") * lax.axis_size("rows")
    every = n * devices
    ta, tb, tbs, tc = tables()
    own_copy = master.astype(bf16)
    gathered = lax.all_gather(own_copy, AXES, axis=0, tiled=True)
    ordered = jnp.zeros_like(gathered).at[slot_rows].set(gathered)
    w_in = ordered[0:C]
    w_out = ordered[C : 2 * C]
    w_up = ordered[2 * C : 2 * C + FF].reshape(C, FF)
    w_down = ordered[2 * C + FF : 2 * C + 2 * FF]
    offset = 2 * C + 2 * FF
    k_large = ordered[offset : offset + KL * KL]
    offset = offset + KL * KL
    k_small = ordered[offset : offset + KS * KS]
    offset = offset + KS * KS
    norm_start = offset
    rows = ordered[offset : offset + 10].astype(f32)
    offset = offset + 10
    mid_gain = ordered[offset : offset + FF // C].astype(f32).reshape(FF)
    mid_bias = ordered[offset + FF // C : offset + 2 * (FF // C)].astype(f32).reshape(FF)

    x = image_in.reshape(n, C)
    cot = cotangent.reshape(n, C)
    all_one = exchange(local_stats(x))
    m_x, q_x = combine(all_one[:, 0], all_one[:, 1], n)
    inv_x = lax.rsqrt(q_x + norm_eps)
    pre_hat = (x - m_x) * inv_x
    pre_low = (pre_hat * rows[0] + rows[1]).astype(bf16)
    z = dot(pre_low, w_in)
    u_low = gelu(z).astype(bf16)
    count = lax.axis_size("rows")
    above = lax.ppermute(u_low, "rows", [(i, i + 1) for i in range(count - 1)])
    below = lax.ppermute(u_low, "rows", [(i + 1, i) for i in range(count - 1)])
    wide = jnp.concatenate([above, u_low, below], axis=0)
    spec_l = dot_exact(tb, k_large)
    spec_s = dot_exact(tbs, k_small)
    spec_u = dot_exact(ta, wide)
    d_l = dot_pair(tc, times_conj(spec_u, spec_l))
    d_s = dot_pair(tc, times_conj(spec_u, spec_s))
    all_two = exchange(local_stats(d_l) + local_stats(d_s))
    m_l, q_l = combine(all_two[:, 0], all_two[:, 1], n)
    m_s, q_s = combine(all_two[:, 2], all_two[:, 3], n)
    inv_l, inv_s = lax.rsqrt(q_l + norm_eps), lax.rsqrt(q_s + norm_eps)
    hat_l, hat_s = (d_l - m_l) * inv_l, (d_s - m_s) * inv_s
    s_val = hat_l * rows[2] + rows[3] + hat_s * rows[4] + rows[5]
    t_low = gelu(s_val).astype(bf16)
    p = dot(t_low, w_out)
    mean_p, second_p = local_stats(p)
    cross = jnp.sum((p - mean_p) * (x - jnp.mean(x, axis=0)), axis=0)
    all_three = exchange((mean_p, second_p, cross))
    m_p, q_p = combine(all_three[:, 0], all_three[:, 1], n)
    cov = combine_cross(all_one[:, 0], all_three[:, 0], all_three[:, 2], n)
    inv_p = lax.rsqrt(q_p + norm_eps)
    proj_hat = (p - m_p) * inv_p
    mid = x + (proj_hat * rows[6] + rows[7])
    slope = rows[6] * inv_p
    m_f = m_x + rows[7]
    q_f = jnp.maximum(q_x + 2 * slope * cov + slope * slope * q_p, 0.0)
    inv_f = lax.rsqrt(q_f + norm_eps)
    ffn_hat = (mid - m_f) * inv_f
    hats = inv_f * inv_p * (cov + slope * q_p)
    c_low = (ffn_hat * rows[8] + rows[9]).astype(bf16)
    hidden = dot(c_low, w_up)
    all_four = exchange(local_stats(hidden))
    m_h, q_h = combine(all_four[:, 0], all_four[:, 1], n)
    inv_h = lax.rsqrt(q_h + norm_eps)
    hid_hat = (hidden - m_h) * inv_h
    hid_out = hid_hat * mid_gain + mid_bias
    a_low = gelu(hid_out).astype(bf16)
    result = mid + dot(a_low, w_down)

    gy_low = cot.astype(bf16)
    g_down = dot(a_low, gy_low, (0, 0))
    g_hid = dot(gy_low, w_down, (1, 1)) * gelu_grad(hid_out)
    b_mid, g_mid_gain = jnp.sum(g_hid, axis=0), jnp.sum(g_hid * hid_hat, axis=0)
    tot = jnp.sum(exchange((b_mid, g_mid_gain)), axis=0) / every
    gh_low = (mid_gain * inv_h * (g_hid - tot[0] - hid_hat * tot[1])).astype(bf16)
    g_up = dot(c_low, gh_low, (0, 0))
    g_ffn = dot(gh_low, w_up, (1, 1))
    b_ffn, g_ffn_gain = jnp.sum(g_ffn, axis=0), jnp.sum(g_ffn * ffn_hat, axis=0)
    tot = jnp.sum(
        exchange((b_ffn, g_ffn_gain, jnp.sum(g_ffn * proj_hat, axis=0), jnp.sum(cot, axis=0), jnp.sum(cot * proj_hat, axis=0))),
        axis=0,
    ) / every
    scale_f = rows[8] * inv_f
    g_mid = cot + scale_f * (g_ffn - tot[0] - ffn_hat * tot[1])
    mean_mid = tot[3]
    mean_mid_hat = tot[4] + scale_f * (tot[2] - tot[1] * hats)
    b_proj, g_proj = jnp.sum(g_mid, axis=0), jnp.sum(g_mid * proj_hat, axis=0)
    gp_low = (slope * (g_mid - mean_mid - proj_hat * mean_mid_hat)).astype(bf16)
    g_out = dot(t_low, gp_low, (0, 0))
    g_s = dot(gp_low, w_out, (1, 1)) * gelu_grad(s_val)
    b_pair, g_l_gain, g_s_gain = jnp.sum(g_s, axis=0), jnp.sum(g_s * hat_l, axis=0), jnp.sum(g_s * hat_s, axis=0)
    tot = jnp.sum(exchange((b_pair, g_l_gain, g_s_gain)), axis=0) / every
    gl = rows[2] * inv_l * (g_s - tot[0] - hat_l * tot[1])
    gs = rows[4] * inv_s * (g_s - tot[0] - hat_s * tot[2])
    spec_gl = dot_pair(tc, gl, (0, 0))
    spec_gs = dot_pair(tc, gs, (0, 0))
    grad_wide = dot_pair(ta, times(spec_gl, spec_l) + times(spec_gs, spec_s), (0, 0))
    from_below = lax.ppermute(grad_wide[:n].astype(bf16), "rows", [(i + 1, i) for i in range(count - 1)])
    from_above = lax.ppermute(grad_wide[2 * n :].astype(bf16), "rows", [(i, i + 1) for i in range(count - 1)])
    g_u = grad_wide[n : 2 * n] + from_below.astype(f32) + from_above.astype(f32)
    flip = times_conj(spec_u, spec_gl)
    g_k_l = dot_pair(tb, flip, (0, 0))
    flip = times_conj(spec_u, spec_gs)
    g_k_s = dot_pair(tbs, flip, (0, 0))
    gz_low = (g_u * gelu_grad(z)).astype(bf16)
    g_in = dot(pre_low, gz_low, (0, 0))
    g_pre = dot(gz_low, w_in, (1, 1))
    b_pre, g_pre_gain = jnp.sum(g_pre, axis=0), jnp.sum(g_pre * pre_hat, axis=0)
    tot = jnp.sum(exchange((b_pre, g_pre_gain)), axis=0) / every
    grad_x = g_mid + rows[0] * inv_x * (g_pre - tot[0] - pre_hat * tot[1])

    norm_grads = jnp.stack(
        [g_pre_gain, b_pre, g_l_gain, b_pair, g_s_gain, b_pair, g_proj, b_proj, g_ffn_gain, b_ffn]
    )
    grads = jnp.concatenate(
        [
            g_in,
            g_out,
            g_up.reshape(FF, C),
            g_down,
            g_k_l,
            g_k_s,
            norm_grads,
            g_mid_gain.reshape(FF // C, C),
            b_mid.reshape(FF // C, C),
        ],
        axis=0,
    )
    grads = jnp.pad(grads, ((0, gathered.shape[0] - grads.shape[0]), (0, 0)))
    slot_grads = grads[slot_rows]
    reduced = lax.psum_scatter(slot_grads, AXES, scatter_dimension=0, tiled=True)
    own_count = master.shape[0]
    place = lax.axis_index("batch") * lax.axis_size("rows") + lax.axis_index("rows")
    own_rows = lax.dynamic_slice_in_dim(slot_rows, place * own_count, own_count)
    rates = jnp.where(own_rows >= norm_start, norm_rate, matrix_rate)[:, None]
    new_first = beta_one * first_moment + (1.0 - beta_one) * reduced
    new_second = beta_two * second_moment + (1.0 - beta_two) * reduced * reduced
    first_hat = new_first / (1.0 - beta_one**STEP)
    second_hat = new_second / (1.0 - beta_two**STEP)
    new_master = master - rates * (
        first_hat / (jnp.sqrt(second_hat) + adam_eps) + decay_rate * master
    )
    return (
        result.reshape(image_in.shape),
        grad_x.reshape(image_in.shape),
        reduced,
        new_first,
        new_second,
        new_master,
        new_master.astype(bf16),
    )


def solution(mesh):
    image = P("batch", "rows", None, None)
    owner = P(AXES, None)
    return jax.shard_map(
        body,
        mesh=mesh,
        in_specs=(image, image, P(), owner, owner, owner),
        out_specs=(image, image, owner, owner, owner, owner, owner),
        check_vma=False,
    )
```

time: 1960 us -> 749 us (0.38)
  matrix products: 1030 us -> 76.7 us
  blocking collectives: 609 us -> 328 us
  waiting for transfers between devices: 109 us -> 134 us
    conv_general_dilated x5 -> x0, matrix products: 991 us -> none  [the longest x3 977 us: depth_conv(): lax.conv_general_dilated(padded_u, kernel_large[:, :, None, :], (1, 1), (...]
    psum x15 -> x0, blocking collectives: 609 us -> none  [the longest x5 207 us: moments(): sum_one = lax.psum(jnp.sum(values, axis=0), ('batch', 'rows'))]
    all_gather x0 -> x8, blocking collectives: none -> 328 us  [exchange(): return lax.all_gather(jnp.stack(rows), AXES, axis=0)]
    dot_general x12 -> x43, matrix products: 30.3 us -> 76.7 us  [dot(): lax.dot_general(a, b, (((dims[0],), (dims[1],)), ((), ())), preferred_ele...]
    all_gather x1, waiting for transfers between devices: 0.01 us -> 25.7 us  [body(): gathered = lax.all_gather(own_copy, AXES, axis=0, tiled=True)]
  transfers between devices with their start and end apart: 6 -> 6, of which waited for: 1 -> 2; matrix products, arithmetic and copies ran while one was open for 2% -> 7% of each run, Pallas kernels for 0% -> 0%
where the time goes in v1:
time: 749 us; the launch traced here: 740 us
  blocking collectives  328 us (44%)
  waiting for transfers between devices  134 us (18%)
  local copies, waits for them, and re-layouts  132 us (18%)
  matrix products  76.7 us (10%)
  other arithmetic  44.3 us (6%)
  between operations  16.2 us (2%)
  starting transfers between devices  9.62 us (1%)
    all_gather x8, blocking collectives, exchange(): return lax.all_gather(jnp.stack(rows), AXES, axis=0)  328 us
    reduce_scatter x1, waiting for transfers between devices, body(): lax.psum_scatter(slot_grads, AXES, scatter_dimension=0, tiled=True)  108 us
    dot_general x43, matrix products, dot(): lax.dot_general(a, b, (((dims[0],), (dims[1],)), ((), ())), preferred_ele...  76.7 us
    concatenate x1, local copies, waits for them, and re-layouts, body(): jnp.concatenate([g_in, g_out, g_up.reshape(FF, C), g_down, g_k_l, g_k_s,...  34.8 us
    gather x1, local copies, waits for them, and re-layouts, body(): slot_grads = grads[slot_rows]  31.2 us
    scatter x1, local copies, waits for them, and re-layouts, body(): ordered = jnp.zeros_like(gathered).at[slot_rows].set(gathered)  31.1 us
    all_gather x1, waiting for transfers between devices, body(): gathered = lax.all_gather(own_copy, AXES, axis=0, tiled=True)  25.7 us
  transfers between devices with their start and end apart: 6, of which 2 were waited for; matrix products, arithmetic and copies ran while one was open for 7% of the time, Pallas kernels for 0%

profile of v1, /device:TPU:0, one launch (start us, length us, event | category | flops | bytes accessed | tf_op | source)
XLA Modules:
  0.0 740.3 jit_solution(9908303840955701488)
XLA Ops:
  11.3 44.3 %all-gather.8 = f32[32,2,512]{2,1,0:T(2,128)S(1)} all-gather(f32[1,2,512]{2,1,0:T(2,128)S(1)} %maximum_bitcast_fusion.5), channel_id=2, replica_groups=mesh['batch'=4,'rows'=8] {'batch','rows'}, dimensions={0}, use_global_device_ids=true | all-gather | bytes 135168 | tf_op jit(solution)/shard_map/all_gather | solution.py:110
  58.3 25.7 %all-gather.18.cloned.1.call-done = bf16[6144,512]{1,0:T(8,128)(2,1)} async-done(((bf16[192,512]{1,0:T(8,128)(2,1)}), bf16[6144,512]{1,0:T(8,128)(2,1)}) %all-gather.18.cloned.1.call-update) | async-done | bytes 6291472 | tf_op jit(solution)/shard_map/all_gather | solution.py:149
  84.0 31.1 %scatter_custom_fusion = bf16[6144,512]{1,0:T(8,128)(2,1)} fusion(s32[6144]{0:T(1024)S(1)} %get-tuple-element.93, bf16[6144,512]{1,0:T(8,128)(2,1)} %all-gather.18.cloned.1.call-done, bf16[]{:T(256)} %constant.42.clone.1), kind=kCustom, calls=%fused_computation.30 | custom fusion | bytes 6291968 | tf_op jit(solution)/shard_map/scatter | solution.py:150
  120.2 3.8 collective-permute-start
  124.0 5.5 fusion.39
  129.5 3.3 fusion.152
  138.2 5.1 fusion.7
  160.5 40.3 %all-gather.9 = f32[32,4,512]{2,1,0:T(4,128)S(1)} all-gather(f32[1,4,512]{2,1,0:T(4,128)S(1)} %maximum_bitcast_fusion.2), channel_id=3, replica_groups=mesh['batch'=4,'rows'=8] {'batch','rows'}, dimensions={0}, use_global_device_ids=true | all-gather | bytes 270336 | tf_op jit(solution)/shard_map/all_gather | solution.py:110
  202.2 38.0 %all-gather.10 = f32[32,3,512]{2,1,0:T(4,128)S(1)} all-gather(f32[1,3,512]{2,1,0:T(4,128)S(1)} %maximum_bitcast_fusion.3), channel_id=4, replica_groups=mesh['batch'=4,'rows'=8] {'batch','rows'}, dimensions={0}, use_global_device_ids=true | all-gather | bytes 202752 | tf_op jit(solution)/shard_map/all_gather | solution.py:110
  243.3 40.1 %all-gather.11 = f32[32,2,2048]{2,1,0:T(2,128)S(1)} all-gather(f32[1,2,2048]{2,1,0:T(2,128)S(1)} %maximum_bitcast_fusion), channel_id=5, replica_groups=mesh['batch'=4,'rows'=8] {'batch','rows'}, dimensions={0}, use_global_device_ids=true | all-gather | bytes 540672 | tf_op jit(solution)/shard_map/all_gather | solution.py:110
  284.7 3.3 fusion.131
  288.6 41.5 %all-gather.12 = f32[32,2,2048]{2,1,0:T(2,128)} all-gather(f32[1,2,2048]{2,1,0:T(2,128)S(1)} %maximum_bitcast_fusion.1), channel_id=6, replica_groups=mesh['batch'=4,'rows'=8] {'batch','rows'}, dimensions={0}, use_global_device_ids=true | all-gather | bytes 540672 | tf_op jit(solution)/shard_map/all_gather | solution.py:110
  340.9 3.3 fusion.130
  345.5 42.9 %all-gather.13 = f32[32,5,512]{2,1,0:T(8,128)} all-gather(f32[1,5,512]{2,1,0:T(8,128)} %bitcast.279), channel_id=7, replica_groups=mesh['batch'=4,'rows'=8] {'batch','rows'}, dimensions={0}, use_global_device_ids=true | all-gather | bytes 337920 | tf_op jit(solution)/shard_map/all_gather | solution.py:110
  398.4 40.7 %all-gather.14 = f32[32,3,512]{2,1,0:T(4,128)} all-gather(f32[1,3,512]{2,1,0:T(4,128)S(1)} %maximum_bitcast_fusion.4), channel_id=8, replica_groups=mesh['batch'=4,'rows'=8] {'batch','rows'}, dimensions={0}, use_global_device_ids=true | all-gather | bytes 202752 | tf_op jit(solution)/shard_map/all_gather | solution.py:110
  457.3 3.1 fusion.29
  479.9 5.3 reshape.311
  488.9 4.0 add_bitcast_fusion
  498.7 34.8 %concatenate.31 = f32[6124,512]{1,0:T(8,128)} concatenate(f32[512,512]{1,0:T(8,128)} %fusion.158, f32[512,512]{1,0:T(8,128)} %fusion.159, f32[2048,512]{1,0:T(8,128)} %reshape.311, f32[2048,512]{1,0:T(8,128)} %fusion.130, f32[961,512]{1,0:T(8,128)S(1)} %add_bitcast_fusion, f32[25,512]{1,0:T(8,128)S(1)} %copy-done.68, f32[1,512]{1,0:T(1,128)S(1)} %bitcast.304, ...), dimensions={0} | concatenate | bytes 25083904 | tf_op jit(solution)/shard_map/concatenate | solution.py:261
  533.4 10.7 %pad.4 = f32[6144,512]{1,0:T(8,128)} pad(f32[6124,512]{1,0:T(8,128)} %concatenate.31, f32[]{:T(128)} %constant.36.clone.1), padding=0_20x0_0 | pad | bytes 25124868 | tf_op jit(solution)/shard_map/jit(_pad)/pad | solution.py:275
  544.1 31.2 %gather_fusion = f32[6144,512]{1,0:T(8,128)} fusion(f32[6144,512]{1,0:T(8,128)} %pad.4, s32[6144]{0:T(1024)S(1)} %copy-done.74), kind=kCustom, calls=%fused_computation | custom fusion | bytes 25190400 | tf_op jit(solution)/shard_map/gather | solution.py:276
  577.0 3.5 fusion.31
  580.5 39.8 %all-gather.15 = f32[32,2,512]{2,1,0:T(2,128)S(1)} all-gather(f32[1,2,512]{2,1,0:T(2,128)S(1)} %maximum_bitcast_fusion.6), channel_id=9, replica_groups=mesh['batch'=4,'rows'=8] {'batch','rows'}, dimensions={0}, use_global_device_ids=true | all-gather | bytes 135168 | tf_op jit(solution)/shard_map/all_gather | solution.py:110
  622.6 108.1 %reduce-scatter.2.cloned.1.call-done = f32[192,512]{1,0:T(8,128)} async-done(((f32[6144,512]{1,0:T(8,128)}), f32[192,512]{1,0:T(8,128)}) %reduce-scatter.2.cloned.1.call-update) | async-done | bytes 393232 | tf_op jit(solution)/shard_map/reduce_scatter | solution.py:277
  (409 shorter events, 114.8 us)
Async XLA Ops:
  7.2 48.6 %copy-start.42 = (f32[1,16,16,512]{3,2,1,0:T(8,128)S(1)}, f32[1,16,16,512]{3,2,1,0:T(8,128)}, u32[]{:S(2)}) copy-start(f32[1,16,16,512]{3,2,1,0:T(8,128)} %param.15) | copy-start | bytes 1572868
  7.2 50.5 %copy-start.106 = (s32[6144]{0:T(1024)S(1)}, s32[6144]{0:T(1024)}, u32[]{:S(2)}) copy-start(s32[6144]{0:T(1024)} %param.16) | copy-start | bytes 73732
  7.2 76.8 %all-gather.18.cloned.1.call-start = ((), (), s32[]{:S(2)}) async-start(), calls=%async_computation.1 | async-start | bytes 6488064 | tf_op jit(solution)/shard_map/all_gather | solution.py:149
  9.0 721.7 %reduce-scatter.2.cloned.1.call-start = ((), (), s32[]{:S(2)}) async-start(), calls=%async_computation.2 | async-start | bytes 12976128 | tf_op jit(solution)/shard_map/reduce_scatter | solution.py:277
  55.7 59.4 %copy-start.63 = (f32[32,1,512]{2,1,0:T(1,128)}, f32[32,1,512]{2,1,0:T(1,128)S(1)}, u32[]{:S(2)}) copy-start(f32[32,1,512]{2,1,0:T(1,128)S(1)} %get-tuple-element.76) | copy-start | bytes 196612
  57.6 58.8 %copy-start.95 = (f32[512]{0:T(512)}, f32[512]{0:T(512)S(1)}, u32[]{:S(2)}) copy-start(f32[512]{0:T(512)S(1)} %get-tuple-element.46) | copy-start | bytes 6148
  119.0 27.9 %collective-permute-start.1 = (bf16[256,512]{1,0:T(8,128)(2,1)}, bf16[256,512]{1,0:T(8,128)(2,1)}, u32[]{:S(2)}, u32[]{:S(2)}) collective-permute-start(bf16[256,512]{1,0:T(8,128)(2,1)} %get-tuple-element.105), channel_id=1, source_target_pairs={{1,0},{2,1},{3,2},{4,3},{5,4},{6,5},{7,6},{9,8},{10,9},{11,10},{12... | collective-permute-start | bytes 786440 | tf_op jit(solution)/shard_map/ppermute | solution.py:177
  120.2 30.0 %collective-permute-start = (bf16[256,512]{1,0:T(8,128)(2,1)}, bf16[256,512]{1,0:T(8,128)(2,1)}, u32[]{:S(2)}, u32[]{:S(2)}) collective-permute-start(bf16[256,512]{1,0:T(8,128)(2,1)} %get-tuple-element.105), channel_id=1, source_target_pairs={{0,1},{1,2},{2,3},{3,4},{4,5},{5,6},{6,7},{8,9},{9,10},{10,11},{11... | collective-permute-start | bytes 786440 | tf_op jit(solution)/shard_map/ppermute | solution.py:176
  138.2 146.5 %copy-start.128 = (f32[1,4,4,128]{3,1,2,0:T(4,128)}, f32[1,4,4,128]{3,1,2,0:T(4,128)S(1)}, u32[]{:S(2)}) copy-start(f32[1,4,4,128]{3,1,2,0:T(4,128)S(1)} %copy.41) | copy-start | bytes 24580
  138.2 146.5 %copy-start.101 = (f32[1,4,4,128]{3,1,2,0:T(4,128)}, f32[1,4,4,128]{3,1,2,0:T(4,128)S(1)}, u32[]{:S(2)}) copy-start(f32[1,4,4,128]{3,1,2,0:T(4,128)S(1)} %copy.40) | copy-start | bytes 24580
  158.9 42.7 %slice-start = ((s8[6291456]{0:T(1024)(128)(4,1)}), s8[4194304]{0:T(1024)(128)(4,1)S(1)}, s32[]{:S(2)}) async-start(s8[6291456]{0:T(1024)(128)(4,1)} %bitcast.260), calls=%async_computation.3 | async-start | bytes 8388608
  159.6 42.0 %slice-start.1 = ((s8[6291456]{0:T(1024)(128)(4,1)}), s8[2097152]{0:T(1024)(128)(4,1)S(1)}, s32[]{:S(2)}) async-start(s8[6291456]{0:T(1024)(128)(4,1)} %bitcast.260), calls=%async_computation.4 | async-start | bytes 4194304
  160.2 41.7 %copy-start.25 = (f32[512,256]{0,1:T(8,128)}, f32[512,256]{0,1:T(8,128)S(1)}, u32[]{:S(2)}) copy-start(f32[512,256]{0,1:T(8,128)S(1)} %get-tuple-element.110) | copy-start | bytes 1572868
  243.0 44.9 %copy-start.12 = (f32[256,2048]{1,0:T(8,128)}, f32[256,2048]{1,0:T(8,128)S(1)}, u32[]{:S(2)}) copy-start(f32[256,2048]{1,0:T(8,128)S(1)} %get-tuple-element.114) | copy-start | bytes 6291460
  340.9 50.9 %copy-start.77 = (f32[512]{0:T(512)S(1)}, f32[512]{0:T(512)}, u32[]{:S(2)}) copy-start(f32[512]{0:T(512)} %copy-done.75) | copy-start | bytes 6148
  395.1 46.5 %copy-start.85 = (f32[512]{0:T(512)S(1)}, f32[512]{0:T(512)}, u32[]{:S(2)}) copy-start(f32[512]{0:T(512)} %copy-done.83) | copy-start | bytes 6148
  395.1 46.5 %copy-start.88 = (f32[512]{0:T(512)S(1)}, f32[512]{0:T(512)}, u32[]{:S(2)}) copy-start(f32[512]{0:T(512)} %copy-done.86) | copy-start | bytes 6148
  395.1 46.5 %copy-start.91 = (f32[512]{0:T(512)S(1)}, f32[512]{0:T(512)}, u32[]{:S(2)}) copy-start(f32[512]{0:T(512)} %copy-done.89) | copy-start | bytes 6148
  475.4 19.0 %collective-permute-start.3 = (bf16[256,512]{1,0:T(8,128)(2,1)}, bf16[256,512]{1,0:T(8,128)(2,1)}, u32[]{:S(2)}, u32[]{:S(2)}) collective-permute-start(bf16[256,512]{1,0:T(8,128)(2,1)} %get-tuple-element.67), channel_id=1, source_target_pairs={{0,1},{1,2},{2,3},{3,4},{4,5},{5,6},{6,7},{8,9},{9,10},{10,11},{11... | collective-permute-start | bytes 786440 | tf_op jit(solution)/shard_map/ppermute | solution.py:245
  478.3 16.0 %collective-permute-start.2 = (bf16[256,512]{1,0:T(8,128)(2,1)}, bf16[256,512]{1,0:T(8,128)(2,1)}, u32[]{:S(2)}, u32[]{:S(2)}) collective-permute-start(bf16[256,512]{1,0:T(8,128)(2,1)} %get-tuple-element.66), channel_id=1, source_target_pairs={{1,0},{2,1},{3,2},{4,3},{5,4},{6,5},{7,6},{9,8},{10,9},{11,10},{12... | collective-permute-start | bytes 786440 | tf_op jit(solution)/shard_map/ppermute | solution.py:244
  577.0 43.4 %copy-start.115 = (f32[1,512]{1,0:T(1,128)S(1)}, f32[1,512]{1,0:T(1,128)}, u32[]{:S(2)}) copy-start(f32[1,512]{1,0:T(1,128)} %get-tuple-element.77) | copy-start | bytes 6148
  580.4 150.2 %copy-start.52 = (f32[192,512]{1,0:T(8,128)S(1)}, f32[192,512]{1,0:T(8,128)}, u32[]{:S(2)}) copy-start(f32[192,512]{1,0:T(8,128)} %param.17) | copy-start | bytes 1179652
  580.5 150.2 %copy-start.66 = (f32[192,512]{1,0:T(8,128)S(1)}, f32[192,512]{1,0:T(8,128)}, u32[]{:S(2)}) copy-start(f32[192,512]{1,0:T(8,128)} %param.19) | copy-start | bytes 1179652
  580.5 150.2 %copy-start.67 = (f32[192,512]{1,0:T(8,128)S(1)}, f32[192,512]{1,0:T(8,128)}, u32[]{:S(2)}) copy-start(f32[192,512]{1,0:T(8,128)} %param.18) | copy-start | bytes 1179652
  (123 other events, 1006.8 us)
Sparse Core Ops, SparseCore 0:
  11.6 72.3 all-gather.17
  575.4 155.1 reduce-scatter.1

commit v2 on v1

v2 whole, which is shorter than its diff:
```python
import functools

import jax
import jax.numpy as jnp
import numpy as np
from jax import lax
from jax.experimental import pallas as pl
from jax.experimental.pallas import tpu as pltpu
from jax.sharding import PartitionSpec as P

C = 512
FF = 2048
KL = 31
KS = 5
STEP = 10

norm_eps = 1e-05
beta_one = 0.9
beta_two = 0.999
adam_eps = 1e-08
decay_rate = 0.05
matrix_rate = 0.05
norm_rate = 0.5

TH = 16
TW = 16
NY = 47
NX = 31
NF = 768
REACH = (KL - 1) // 2
AXES = ("batch", "rows")
f32 = jnp.float32
bf16 = jnp.bfloat16


@functools.lru_cache(None)
def tables():
    freqs = [(ky, 0) for ky in range((NY + 1) // 2)]
    freqs += [(ky, kx) for kx in range(1, (NX + 1) // 2) for ky in range(NY)]
    ky = np.array([f[0] for f in freqs], np.int64)[:, None]
    kx = np.array([f[1] for f in freqs], np.int64)[:, None]
    pad = NF - len(freqs)

    def angle(rows, cols):
        ty = (ky * rows.reshape(1, -1)) % NY
        tx = (kx * cols.reshape(1, -1)) % NX
        return 2 * np.pi * (ty / NY + tx / NX)

    def grid(rows, cols):
        r, c = np.meshgrid(rows, cols, indexing="ij")
        return r.reshape(-1), c.reshape(-1)

    def stack(re, im):
        z = np.zeros((pad, re.shape[1]))
        return np.concatenate([re, z, im, z], axis=0)

    r, c = grid(np.arange(-TH, 2 * TH), np.arange(TW))
    used = ((r + REACH >= 0) & (r + REACH < NY - 1)).astype(np.float64)[None]
    t = angle(r + REACH, c)
    a = stack(np.cos(t) * used, -np.sin(t) * used)
    i, j = grid(np.arange(KL), np.arange(KL))
    t = angle(i, j - REACH)
    b = stack(np.cos(t), -np.sin(t))
    lead = REACH - (KS - 1) // 2
    small = ((i >= lead) & (i < lead + KS) & (j >= lead) & (j < lead + KS)).nonzero()[0]
    bs = np.pad(b[:, small], ((0, 0), (0, 32 - KS * KS)))
    b = np.pad(b, ((0, 0), (0, 2 * C - KL * KL)))
    y, x = grid(np.arange(TH), np.arange(TW))
    t = angle(y, x)
    w = np.full((len(freqs), 1), 2.0)
    w[0] = 1.0
    w /= NY * NX
    ct = stack(w * np.cos(t), -w * np.sin(t))
    return tuple(m.astype(np.float32).astype(bf16) for m in (a, a.T, b, b.T, bs, bs.T, ct.T, ct))


def dot(a, b, dims=(1, 0)):
    return lax.dot_general(a, b, (((dims[0],), (dims[1],)), ((), ())), preferred_element_type=f32)


def exchange_kernel(nb, nr, x_ref, o_ref, send_sem, recv_sem):
    nd = nb * nr
    me = lax.axis_index("batch") * nr + lax.axis_index("rows")

    def peer(k):
        other = lax.rem(me + k, nd)
        return (other // nr, lax.rem(other, nr))

    barrier = pltpu.get_barrier_semaphore()

    @pl.loop(1, nd)
    def _(k):
        pl.semaphore_signal(barrier, inc=1, device_id=peer(k), device_id_type=pl.DeviceIdType.MESH)

    o_ref[me] = x_ref[...]
    pl.semaphore_wait(barrier, nd - 1)

    @pl.loop(1, nd)
    def _(k):
        pltpu.make_async_remote_copy(
            o_ref.at[me], o_ref.at[me], send_sem, recv_sem, device_id=peer(k), device_id_type=pl.DeviceIdType.MESH
        ).start()

    others = o_ref.at[pl.ds(0, nd - 1)]
    pltpu.make_async_copy(others, others, recv_sem).wait()
    pltpu.make_async_copy(others, others, send_sem).wait()


def exchange(rows):
    x = jnp.stack(rows)
    nb, nr = lax.axis_size("batch"), lax.axis_size("rows")
    return pl.pallas_call(
        functools.partial(exchange_kernel, nb, nr),
        out_shape=jax.ShapeDtypeStruct((nb * nr,) + x.shape, f32),
        in_specs=[pl.BlockSpec(memory_space=pltpu.VMEM)],
        out_specs=pl.BlockSpec(memory_space=pltpu.VMEM),
        scratch_shapes=[pltpu.SemaphoreType.DMA, pltpu.SemaphoreType.DMA],
        compiler_params=pltpu.CompilerParams(
            collective_id=x.shape[0] + 8 * (x.shape[1] != C), has_side_effects=True, vmem_limit_bytes=32 * 2**20
        ),
    )(x)


MESH = pl.DeviceIdType.MESH
WIDTHS = (4, 3, 8, 8, 5, 3, 2)


def chunks(n, fn, init=()):
    return lax.fori_loop(0, n // 32, lambda i, c: fn(pl.ds(pl.multiple_of(i * 32, 32), 32), c), init)


def fold(v):
    return jnp.sum(v.reshape(v.shape[0] // 8, 8, v.shape[1]), axis=0)


def close(v):
    return jnp.sum(v, axis=0, keepdims=True)


def gelu_both(v):
    a = np.float32(np.sqrt(2 / np.pi))
    sq = v * v
    t = jnp.tanh(a * (v + 0.044715 * (sq * v)))
    half = 0.5 * (1 + t)
    return v * half, half + 0.5 * v * (1 - t * t) * (a * (1 + 3 * 0.044715 * sq))


def core_kernel(
    nb, nr, x_ref, cot_ref, sx_ref, tab_hbm, a_hbm, at_hbm, b_hbm, bt_hbm, bs_ref, bst_ref, c_hbm, ct_hbm,
    out_ref, gin_ref, grad_hbm,
    tab, ta, tat, tb, tbt, tc, tct, pre_low, wide, dz, spec_u, spec_l, spec_s, prod_l, prod_s, prod_k,
    d_l, d_s, s_val, t_low, p_val, mid, c_low, gy_low, hid, gact, a_low, gh_low, g_f, acc, stage0, stage1, halo_out, halo_in,
    *rest,
):
    first = rest[: len(WIDTHS)]
    second = rest[len(WIDTHS) : 2 * len(WIDTHS)]
    send_sem, recv_sem, halo_send, halo_recv, load_sem, store_sem = rest[2 * len(WIDTHS) :]
    n = x_ref.shape[0]
    every = float(n * nb * nr)
    b = lax.axis_index("batch")
    r = lax.axis_index("rows")

    barrier = pltpu.get_barrier_semaphore()
    for k in range(1, nr):
        pl.semaphore_signal(barrier, inc=1, device_id=(b, lax.rem(r + k, nr)), device_id_type=MESH)
    for k in range(1, nb):
        pl.semaphore_signal(barrier, inc=1, device_id=(lax.rem(b + k, nb), r), device_id_type=MESH)

    pieces = [pl.ds(0, 2 * C), pl.ds(2 * C + 2 * FF, 2 * C), pl.ds(2 * C, 2 * FF)]
    moves = [(tab_hbm.at[p], tab.at[p]) for p in pieces]
    order = [moves[0], moves[1], (b_hbm, tb), (a_hbm, ta), (c_hbm, tc), moves[2], (ct_hbm, tct), (at_hbm, tat), (bt_hbm, tbt)]
    loads = [pltpu.make_async_copy(s, d, load_sem.at[i]) for i, (s, d) in enumerate(order)]
    for c in loads:
        c.start()
    ld_w, ld_k, ld_b, ld_a, ld_c, ld_f, ld_ct, ld_at, ld_bt = loads

    def share(e, v, merge, work=lambda: None):
        count = n
        for stage, (buf, mine, axis, size) in enumerate(((first[e], r, "rows", nr), (second[e], b, "batch", nb))):
            buf[mine] = v
            for k in range(1, size):
                other = lax.rem(mine + k, size)
                where = (b, other) if axis == "rows" else (other, r)
                pltpu.make_async_remote_copy(
                    buf.at[mine], buf.at[mine], send_sem.at[e, stage], recv_sem.at[e, stage],
                    device_id=where, device_id_type=MESH,
                ).start()
            if stage == 0:
                work()
            got = buf.at[pl.ds(0, size - 1)]
            pltpu.make_async_copy(got, got, recv_sem.at[e, stage]).wait()
            v = merge(buf, size, float(count))
            count = count * size
        return v

    def merge_sum(buf, size, count):
        return jnp.sum(buf[...], axis=0)

    def merge_stats(h):
        def merge(buf, size, count):
            v = buf[...]
            means = v[:, :h]
            m = jnp.sum(means, axis=0) * (1.0 / size)
            d = means - m
            parts = [m, jnp.sum(v[:, h : 2 * h], axis=0) + count * jnp.sum(d * d, axis=0)]
            if v.shape[1] > 2 * h:
                parts.append(jnp.sum(v[:, 2 * h :], axis=0))
            return jnp.concatenate(parts, axis=0)

        return merge

    zero = jnp.zeros((8, C), f32)

    m_x, q_x = sx_ref[0:1, :], sx_ref[1:2, :]
    inv_x = lax.rsqrt(q_x + norm_eps)
    ld_w.wait()
    ld_k.wait()
    small = tab[pl.ds(2 * C + 2 * FF + 976, 48), :].astype(f32)
    row = lambda i: small[32 + i : 33 + i, :]
    mid_gain = lambda j: small[42 + j : 43 + j, :]
    mid_bias = lambda j: small[25 + j : 26 + j, :]

    def pre(s, sx):
        d = x_ref[s, :] - m_x
        pre_low[s, :] = (d * (inv_x * row(0)) + row(1)).astype(bf16)
        return sx + fold(d)

    sum_x = close(chunks(n, pre, zero))
    dz[...] = dot(pre_low[...], tab[pl.ds(0, C), :])

    def act(s, c):
        u, d = gelu_both(dz[s, :])
        dz[s, :] = d
        wide[pl.ds(pl.multiple_of(n + s.start, 32), 32), :] = u.astype(bf16)
        return c

    chunks(n, act)

    pl.semaphore_wait(barrier, nr - 1 + nb - 1)
    mine = wide.at[pl.ds(n, n)]
    up = pltpu.make_async_remote_copy(
        mine, wide.at[pl.ds(2 * n, n)], halo_send.at[0], halo_recv.at[0], device_id=(b, lax.rem(r + nr - 1, nr)), device_id_type=MESH
    )
    down = pltpu.make_async_remote_copy(
        mine, wide.at[pl.ds(0, n)], halo_send.at[1], halo_recv.at[1], device_id=(b, lax.rem(r + 1, nr)), device_id_type=MESH
    )
    has_above, has_below = r > 0, r < nr - 1

    @pl.when(has_above)
    def _():
        up.start()

    @pl.when(has_below)
    def _():
        down.start()

    ld_b.wait()
    kernel_rows = pl.ds(2 * C + 2 * FF, 2 * C)
    small_rows = pl.ds(2 * C + 2 * FF + 976, 32)

    @pl.loop(0, 2 * NF // 256)
    def _(t):
        s = pl.ds(pl.multiple_of(t * 256, 256), 256)
        spec_l[s, :] = dot(tb[s, :], tab[kernel_rows, :])
        spec_s[s, :] = dot(bs_ref[s, :], tab[small_rows, :])

    @pl.when(has_below)
    def _():
        up.wait_recv()
        down.wait_send()

    @pl.when(has_above)
    def _():
        down.wait_recv()
        up.wait_send()

    @pl.when(jnp.logical_not(has_above))
    def _():
        wide[pl.ds(0, n), :] = jnp.zeros((n, C), bf16)

    @pl.when(jnp.logical_not(has_below))
    def _():
        wide[pl.ds(2 * n, n), :] = jnp.zeros((n, C), bf16)

    ld_a.wait()

    @pl.loop(0, 2 * NF // 256)
    def _(t):
        s = pl.ds(pl.multiple_of(t * 256, 256), 256)
        spec_u[s, :] = dot(ta[s, :], wide[...])

    def halves(i):
        return pl.ds(pl.multiple_of(i * 32, 32), 32), pl.ds(pl.multiple_of(NF + i * 32, 32), 32)

    @pl.loop(0, NF // 32)
    def _(i):
        re, im = halves(i)
        ur, ui = spec_u[re, :], spec_u[im, :]
        for k, p in ((spec_l, prod_l), (spec_s, prod_s)):
            kr, ki = k[re, :], k[im, :]
            p[re, :] = (ur * kr + ui * ki).astype(bf16)
            p[im, :] = (ui * kr - ur * ki).astype(bf16)

    ld_c.wait()
    d_l[...] = dot(tc[...], prod_l[...])
    d_s[...] = dot(tc[...], prod_s[...])

    def local(ref):
        m = close(chunks(n, lambda s, c: c + fold(ref[s, :]), zero)) * (1.0 / n)

        def sq(s, c):
            d = ref[s, :] - m
            return c + fold(d * d)

        return m, close(chunks(n, sq, zero))

    m_l, v_l = local(d_l)
    m_s, v_s = local(d_s)

    def early():
        def low(s, c):
            gy_low[s, :] = cot_ref[s, :].astype(bf16)
            return c

        chunks(n, low)

    tot = share(0, jnp.concatenate([m_l, m_s, v_l, v_s], axis=0), merge_stats(2), early)
    m_l, m_s = tot[0:1], tot[1:2]
    inv_l, inv_s = lax.rsqrt(tot[2:3] / every + norm_eps), lax.rsqrt(tot[3:4] / every + norm_eps)

    def pair(s, c):
        hl = (d_l[s, :] - m_l) * inv_l
        hs = (d_s[s, :] - m_s) * inv_s
        d_l[s, :] = hl
        d_s[s, :] = hs
        t, d = gelu_both(hl * row(2) + row(3) + hs * row(4) + row(5))
        s_val[s, :] = d
        t_low[s, :] = t.astype(bf16)
        return c

    chunks(n, pair)
    p_val[...] = dot(t_low[...], tab[pl.ds(C, C), :])
    m_p = close(chunks(n, lambda s, c: c + fold(p_val[s, :]), zero)) * (1.0 / n)

    def proj(s, c):
        d = p_val[s, :] - m_p
        return c[0] + fold(d * d), c[1] + fold(d * (x_ref[s, :] - m_x))

    v_p, cross = chunks(n, proj, (zero, zero))
    tot = share(1, jnp.concatenate([m_p, close(v_p), close(cross) + m_p * sum_x], axis=0), merge_stats(1))
    m_p, q_p, cov = tot[0:1], tot[1:2] / every, tot[2:3] / every
    inv_p = lax.rsqrt(q_p + norm_eps)
    slope = row(6) * inv_p
    m_f = m_x + row(7)
    q_f = jnp.maximum(q_x + 2 * slope * cov + slope * slope * q_p, 0.0)
    inv_f = lax.rsqrt(q_f + norm_eps)
    hats = inv_f * inv_p * (cov + slope * q_p)

    def ffn(s, c):
        ph = (p_val[s, :] - m_p) * inv_p
        p_val[s, :] = ph
        m = x_ref[s, :] + (ph * row(6) + row(7))
        mid[s, :] = m
        c_low[s, :] = ((m - m_f) * (inv_f * row(8)) + row(9)).astype(bf16)
        g = cot_ref[s, :]
        return c[0] + fold(g), c[1] + fold(g * ph)

    sum_c, sum_ch = chunks(n, ffn, (zero, zero))
    sum_c, sum_ch = close(sum_c), close(sum_ch)
    ld_f.wait()
    up_rows = lambda j: pl.ds(pl.multiple_of(2 * C + j * C, C), C)
    down_rows = lambda j: pl.ds(pl.multiple_of(2 * C + FF + j * C, C), C)
    blocks = FF // C
    for j in range(blocks):
        hid[j] = dot(c_low[...], tab[up_rows(j), :])
    st = [local(hid.at[j]) for j in range(blocks)]

    def back_first():
        for j in range(blocks):
            gact[j] = dot(gy_low[...], tab[down_rows(j), :], (1, 1))

    tot = share(2, jnp.concatenate([s[0] for s in st] + [s[1] for s in st], axis=0), merge_stats(blocks), back_first)
    m_h = tot[:blocks]
    inv_h = lax.rsqrt(tot[blocks:] / every + norm_eps)
    sums = []
    for j in range(blocks):
        mj, ij, gj, bj = m_h[j : j + 1], inv_h[j : j + 1], mid_gain(j), mid_bias(j)

        def hidden(s, c, j=j, mj=mj, ij=ij, gj=gj, bj=bj):
            hat = (hid[j, s, :] - mj) * ij
            hid[j, s, :] = hat
            a, d = gelu_both(hat * gj + bj)
            a_low[j, s, :] = a.astype(bf16)
            g = gact[j, s, :] * d
            gact[j, s, :] = g
            return c[0] + fold(g), c[1] + fold(g * hat)

        sums.append(tuple(close(v) for v in chunks(n, hidden, (zero, zero))))
    mid_rows = jnp.concatenate([s[0] for s in sums] + [s[1] for s in sums], axis=0)

    def half_cols(h):
        return pl.ds(pl.multiple_of(h * 256, 256), 256)

    def outputs():
        out_ref[...] = mid[...]
        for j in range(blocks):
            out_ref[...] += dot(a_low[j], tab[down_rows(j), :])
            for h in range(C // 256):
                stage0[pl.ds(j * C + h * 256, 256), :] = dot(a_low[j, :, half_cols(h)], gy_low[...], (0, 0))

    tot = share(3, mid_rows, merge_sum, outputs) * (1.0 / every)
    st_down = pltpu.make_async_copy(stage0, grad_hbm.at[pl.ds(2 * C + FF, FF)], store_sem.at[0])
    st_down.start()
    for j in range(blocks):
        tb_, tg_, sc = tot[j : j + 1], tot[blocks + j : blocks + j + 1], mid_gain(j) * inv_h[j : j + 1]

        def grad_h(s, c, j=j, tb_=tb_, tg_=tg_, sc=sc):
            gh_low[j, s, :] = (sc * (gact[j, s, :] - tb_ - hid[j, s, :] * tg_)).astype(bf16)
            return c

        chunks(n, grad_h)
    g_f[...] = dot(gh_low[0], tab[up_rows(0), :], (1, 1))
    for j in range(1, blocks):
        g_f[...] += dot(gh_low[j], tab[up_rows(j), :], (1, 1))

    def ffn_sums(s, c):
        g = g_f[s, :]
        hat = (mid[s, :] - m_f) * inv_f
        return c[0] + fold(g), c[1] + fold(g * hat), c[2] + fold(g * p_val[s, :])

    b_ffn, g_ffn, g_fp = (close(v) for v in chunks(n, ffn_sums, (zero, zero, zero)))

    def grad_up():
        for j in range(blocks):
            for h in range(C // 256):
                stage1[pl.ds(j * C + h * 256, 256), :] = dot(c_low[:, half_cols(h)], gh_low[j], (0, 0))

    tot = share(4, jnp.concatenate([b_ffn, g_ffn, g_fp, sum_c, sum_ch], axis=0), merge_sum, grad_up) * (1.0 / every)
    st_up = pltpu.make_async_copy(stage1, grad_hbm.at[pl.ds(2 * C, FF)], store_sem.at[1])
    st_up.start()
    scale_f = row(8) * inv_f
    mean_hat = tot[4:5] + scale_f * (tot[2:3] - tot[1:2] * hats)

    def grad_mid(s, c):
        hat = (mid[s, :] - m_f) * inv_f
        g = cot_ref[s, :] + scale_f * (g_f[s, :] - tot[0:1] - hat * tot[1:2])
        g_f[s, :] = g
        ph = p_val[s, :]
        pre_p = slope * (g - tot[3:4] - ph * mean_hat)
        gh_low[0, s, :] = pre_p.astype(bf16)
        return c[0] + fold(g), c[1] + fold(g * ph)

    b_proj, g_proj = (close(v) for v in chunks(n, grad_mid, (zero, zero)))
    p_val[...] = dot(gh_low[0], tab[pl.ds(C, C), :], (1, 1))

    def grad_s(s, c):
        g = p_val[s, :] * s_val[s, :]
        p_val[s, :] = g
        return c[0] + fold(g), c[1] + fold(g * d_l[s, :]), c[2] + fold(g * d_s[s, :])

    b_pair, g_lg, g_sg = (close(v) for v in chunks(n, grad_s, (zero, zero, zero)))
    st_down.wait()

    def grad_out():
        for h in range(C // 256):
            stage0[pl.ds(C + h * 256, 256), :] = dot(t_low[:, half_cols(h)], gh_low[0], (0, 0))

    tot = share(5, jnp.concatenate([b_pair, g_lg, g_sg], axis=0), merge_sum, grad_out) * (1.0 / every)
    sc_l, sc_s = row(2) * inv_l, row(4) * inv_s

    def grad_pair(s, c):
        g = p_val[s, :] - tot[0:1]
        t_low[s, :] = (sc_l * (g - d_l[s, :] * tot[1:2])).astype(bf16)
        gh_low[1, s, :] = (sc_s * (g - d_s[s, :] * tot[2:3])).astype(bf16)
        return c

    chunks(n, grad_pair)
    ld_ct.wait()

    @pl.loop(0, NF // 256)
    def _(t):
        re, im = pl.ds(pl.multiple_of(t * 256, 256), 256), pl.ds(pl.multiple_of(NF + t * 256, 256), 256)
        acc[0] = dot(tct[re, :], t_low[...])
        acc[1] = dot(tct[im, :], t_low[...])
        acc[2] = dot(tct[re, :], gh_low[1])
        acc[3] = dot(tct[im, :], gh_low[1])

        @pl.loop(0, 8)
        def _(i):
            s = pl.ds(pl.multiple_of(i * 32, 32), 32)
            re = pl.ds(pl.multiple_of(t * 256 + i * 32, 32), 32)
            im = pl.ds(pl.multiple_of(NF + t * 256 + i * 32, 32), 32)
            lr, li, sr, si = acc[0, s, :], acc[1, s, :], acc[2, s, :], acc[3, s, :]
            kr, ki = spec_l[re, :], spec_l[im, :]
            hr, hi = spec_s[re, :], spec_s[im, :]
            prod_k[re, :] = (lr * kr - li * ki + sr * hr - si * hi).astype(bf16)
            prod_k[im, :] = (lr * ki + li * kr + sr * hi + si * hr).astype(bf16)
            ur, ui = spec_u[re, :], spec_u[im, :]
            prod_l[re, :] = (lr * ur + li * ui).astype(bf16)
            prod_l[im, :] = (lr * ui - li * ur).astype(bf16)
            prod_s[re, :] = (sr * ur + si * ui).astype(bf16)
            prod_s[im, :] = (sr * ui - si * ur).astype(bf16)

    ld_at.wait()
    halo_out[0] = dot(tat[pl.ds(0, n), :], prod_k[...]).astype(bf16)
    halo_out[1] = dot(tat[pl.ds(2 * n, n), :], prod_k[...]).astype(bf16)
    up2 = pltpu.make_async_remote_copy(
        halo_out.at[0], halo_in.at[1], halo_send.at[2], halo_recv.at[2], device_id=(b, lax.rem(r + nr - 1, nr)), device_id_type=MESH
    )
    down2 = pltpu.make_async_remote_copy(
        halo_out.at[1], halo_in.at[0], halo_send.at[3], halo_recv.at[3], device_id=(b, lax.rem(r + 1, nr)), device_id_type=MESH
    )

    @pl.when(has_above)
    def _():
        up2.start()

    @pl.when(has_below)
    def _():
        down2.start()

    p_val[...] = dot(tat[pl.ds(n, n), :], prod_k[...])
    ld_bt.wait()

    @pl.loop(0, 4)
    def _(t):
        s = pl.ds(pl.multiple_of(t * 256, 256), 256)
        stage0[pl.ds(pl.multiple_of(2 * C + t * 256, 256), 256), :] = dot(tbt[s, :], prod_l[...])

    stage0[pl.ds(2 * C + 976, 32), :] = dot(bst_ref[...], prod_s[...])

    @pl.when(has_below)
    def _():
        up2.wait_recv()
        down2.wait_send()

    @pl.when(has_above)
    def _():
        down2.wait_recv()
        up2.wait_send()

    @pl.when(jnp.logical_not(has_above))
    def _():
        halo_in[0] = jnp.zeros((n, C), bf16)

    @pl.when(jnp.logical_not(has_below))
    def _():
        halo_in[1] = jnp.zeros((n, C), bf16)

    def grad_z(s, c):
        g = p_val[s, :] + halo_in[0, s, :].astype(f32) + halo_in[1, s, :].astype(f32)
        t_low[s, :] = (g * dz[s, :]).astype(bf16)
        return c

    chunks(n, grad_z)
    p_val[...] = dot(t_low[...], tab[pl.ds(0, C), :], (1, 1))

    def pre_sums(s, c):
        g = p_val[s, :]
        return c[0] + fold(g), c[1] + fold(g * ((x_ref[s, :] - m_x) * inv_x))

    b_pre, g_pre = (close(v) for v in chunks(n, pre_sums, (zero, zero)))

    def grad_in():
        for h in range(C // 256):
            stage0[pl.ds(h * 256, 256), :] = dot(pre_low[:, half_cols(h)], t_low[...], (0, 0))

    tot = share(6, jnp.concatenate([b_pre, g_pre], axis=0), merge_sum, grad_in) * (1.0 / every)
    scale_x = row(0) * inv_x
    norms = [g_pre, b_pre, g_lg, b_pair, g_sg, b_pair, g_proj, b_proj, g_ffn, b_ffn]
    norms += [mid_rows[blocks + j : blocks + j + 1] for j in range(blocks)]
    base = 2 * C + 976
    stage0[pl.ds(base + 32, 16), :] = jnp.concatenate(norms + [jnp.zeros((2, C), f32)], axis=0)
    for j in range(blocks):
        stage0[pl.ds(base + 25 + j, 1), :] = mid_rows[j : j + 1]
    stores = [
        pltpu.make_async_copy(stage0.at[pl.ds(0, 2 * C)], grad_hbm.at[pl.ds(0, 2 * C)], store_sem.at[2]),
        pltpu.make_async_copy(stage0.at[pl.ds(2 * C, 2 * C)], grad_hbm.at[pl.ds(2 * C + 2 * FF, 2 * C)], store_sem.at[3]),
    ]
    for c in stores:
        c.start()

    def last(s, c):
        hat = (x_ref[s, :] - m_x) * inv_x
        gin_ref[s, :] = g_f[s, :] + scale_x * (p_val[s, :] - tot[0:1] - hat * tot[1:2])
        return c

    chunks(n, last)
    for e in range(len(WIDTHS)):
        for stage, (buf, size) in enumerate(((first[e], nr), (second[e], nb))):
            sent = buf.at[pl.ds(0, size - 1)]
            pltpu.make_async_copy(sent, sent, send_sem.at[e, stage]).wait()
    st_up.wait()
    for c in stores:
        c.wait()


def core(x, cot, sx, tab, nb, nr):
    (a, at, b, bt, bs, bst, c, ct) = tables()
    n = x.shape[0]
    vm = lambda shape, dtype=f32: pltpu.VMEM(shape, dtype)
    pix = vm((n, C))
    low = vm((n, C), bf16)
    wide_spec = vm((2 * NF, C))
    low_spec = vm((2 * NF, C), bf16)
    vmem = pl.BlockSpec(memory_space=pltpu.VMEM)
    anywhere = pl.BlockSpec(memory_space=pl.ANY)
    scratch = [vm(tab.shape, bf16)] + [vm(m.shape, bf16) for m in (a, at, b, bt, c, ct)]
    scratch += [low, vm((3 * n, C), bf16), pix, wide_spec, wide_spec, wide_spec, low_spec, low_spec, low_spec]
    scratch += [pix, pix, pix, low, pix, pix, low, low]
    scratch += [vm((FF // C, n, C)), vm((FF // C, n, C)), vm((FF // C, n, C), bf16), vm((FF // C, n, C), bf16), pix, vm((4, 256, C))]
    scratch += [vm((FF, C)), vm((FF, C)), vm((2, n, C), bf16), vm((2, n, C), bf16)]
    scratch += [vm((nr, w, C)) for w in WIDTHS] + [vm((nb, w, C)) for w in WIDTHS]
    dma = pltpu.SemaphoreType.DMA
    scratch += [dma((len(WIDTHS), 2)), dma((len(WIDTHS), 2)), dma((4,)), dma((4,)), dma((9,)), dma((4,))]
    return pl.pallas_call(
        functools.partial(core_kernel, nb, nr),
        out_shape=[
            jax.ShapeDtypeStruct((n, C), f32),
            jax.ShapeDtypeStruct((n, C), f32),
            jax.ShapeDtypeStruct(tab.shape, f32),
        ],
        in_specs=[vmem] * 3 + [anywhere] * 5 + [vmem] * 2 + [anywhere] * 2,
        out_specs=[vmem, vmem, anywhere],
        scratch_shapes=scratch,
        compiler_params=pltpu.CompilerParams(collective_id=1, has_side_effects=True, vmem_limit_bytes=62 * 2**20),
    )(x, cot, sx, tab, a, at, b, bt, bs, bst, c, ct)


def table_place(t):
    start = 2 * C + 2 * FF
    k_end = start + KL * KL
    s_end = k_end + KS * KS
    m_gain = s_end + 10
    m_bias = m_gain + FF // C
    m_end = m_bias + FF // C
    up = t - 2 * C
    up = 2 * C + up % (FF // C) * C + up // (FF // C)
    base = start + 976
    unused = t - m_end
    unused = jnp.where(unused < 15, k_end + unused, jnp.where(unused < 18, base + 29 + unused - 15, base + 46 + unused - 18))
    p = jnp.where((t >= 2 * C) & (t < 2 * C + FF), up, t)
    p = jnp.where(t >= k_end, t - k_end + base, p)
    p = jnp.where(t >= s_end, t - s_end + base + 32, p)
    p = jnp.where(t >= m_bias, t - m_bias + base + 25, p)
    return jnp.where(t >= m_end, unused, p)


def body(image_in, cotangent, slot_rows, master, first_moment, second_moment):
    n = image_in.shape[0] * image_in.shape[1] * image_in.shape[2]
    nb, nr = lax.axis_size("batch"), lax.axis_size("rows")
    norm_start = 2 * C + 2 * FF + KL * KL + KS * KS
    places = table_place(slot_rows)
    own_copy = master.astype(bf16)
    gathered = lax.all_gather(own_copy, AXES, axis=0, tiled=True)
    ordered = jnp.zeros_like(gathered).at[places].set(gathered)
    x = image_in.reshape(n, C)
    cot = cotangent.reshape(n, C)
    m = jnp.mean(x, axis=0)
    d = x - m
    all_one = exchange((m, jnp.sum(d * d, axis=0)))
    m_x = jnp.mean(all_one[:, 0], axis=0)
    d = all_one[:, 0] - m_x
    q_x = (jnp.sum(all_one[:, 1], axis=0) + n * jnp.sum(d * d, axis=0)) / (n * nb * nr)
    result, grad_x, grads = core(x, cot, jnp.stack([m_x, q_x]), ordered, nb, nr)
    slot_grads = grads[places]
    reduced = lax.psum_scatter(slot_grads, AXES, scatter_dimension=0, tiled=True)
    own_count = master.shape[0]
    place = lax.axis_index("batch") * nr + lax.axis_index("rows")
    own_rows = lax.dynamic_slice_in_dim(slot_rows, place * own_count, own_count)
    rates = jnp.where(own_rows >= norm_start, norm_rate, matrix_rate)[:, None]
    new_first = beta_one * first_moment + (1.0 - beta_one) * reduced
    new_second = beta_two * second_moment + (1.0 - beta_two) * reduced * reduced
    first_hat = new_first / (1.0 - beta_one**STEP)
    second_hat = new_second / (1.0 - beta_two**STEP)
    new_master = master - rates * (
        first_hat / (jnp.sqrt(second_hat) + adam_eps) + decay_rate * master
    )
    return (
        result.reshape(image_in.shape),
        grad_x.reshape(image_in.shape),
        reduced,
        new_first,
        new_second,
        new_master,
        new_master.astype(bf16),
    )


def solution(mesh):
    image = P("batch", "rows", None, None)
    owner = P(AXES, None)
    return jax.shard_map(
        body,
        mesh=mesh,
        in_specs=(image, image, P(), owner, owner, owner),
        out_specs=(image, image, owner, owner, owner, owner, owner),
        check_vma=False,
    )
```

time: 749 us -> 395 us (0.53); the launches traced: 740 us -> 394 us
  blocking collectives: 328 us -> 0 us
  Pallas kernels: 0 us -> 94.2 us
  waiting for transfers between devices: 134 us -> 213 us
  matrix products: 76.7 us -> 0 us
  local copies, waits for them, and re-layouts: 132 us -> 63.7 us
  other arithmetic: 44.3 us -> 8.8 us
  starting transfers between devices: 9.62 us -> 0.08 us
    all_gather x8 -> x0, blocking collectives: 328 us -> none  [exchange(): return lax.all_gather(jnp.stack(rows), AXES, axis=0)]
    pallas_call x0 -> x2, Pallas kernels: none -> 94.2 us  [the longest x1 82.8 us: core(): pl.pallas_call(functools.partial(core_kernel, nb, nr), out_shape=[jax.Sha...]
    dot_general x43 -> x0, matrix products: 76.7 us -> none  [dot(): lax.dot_general(a, b, (((dims[0],), (dims[1],)), ((), ())), preferred_ele...]
    reduce_scatter x1, waiting for transfers between devices: 108 us -> 154 us  [body(): lax.psum_scatter(slot_grads, AXES, scatter_dimension=0, tiled=True)]
    concatenate x1 -> x0, local copies, waits for them, and re-layouts: 34.8 us -> none  [body(): jnp.concatenate([g_in, g_out, g_up.reshape(FF, C), g_down, g_k_l, g_k_s,...]
    all_gather x1, waiting for transfers between devices: 25.7 us -> 59.7 us  [body(): gathered = lax.all_gather(own_copy, AXES, axis=0, tiled=True)]
    pad x1 -> x0, local copies, waits for them, and re-layouts: 10.7 us -> none  [body(): grads = jnp.pad(grads, ((0, gathered.shape[0] - grads.shape[0]), (0, 0)))]
    reduce_sum x20 -> x4, other arithmetic: 13 us -> 2.4 us  [the longest x1 1.12 us: body(): all_one = exchange((m, jnp.sum(d * d, axis=0)))]
  transfers between devices with their start and end apart: 6 -> 2, of which waited for: 2 -> 2; matrix products, arithmetic and copies ran while one was open for 7% -> 1% of each run, Pallas kernels for 0% -> 3%
where the time goes in v2:
time: 395 us; the launch traced here: 394 us
  waiting for transfers between devices  213 us (54%)
  Pallas kernels  94.2 us (24%)
  local copies, waits for them, and re-layouts  63.7 us (16%)
  between operations  14.1 us (4%)
  other arithmetic  8.8 us (2%)
    reduce_scatter x1, waiting for transfers between devices, body(): lax.psum_scatter(slot_grads, AXES, scatter_dimension=0, tiled=True)  154 us
    pallas_call x1, Pallas kernels, core(): pl.pallas_call(functools.partial(core_kernel, nb, nr), out_shape=[jax.Sha...  82.8 us
    all_gather x1, waiting for transfers between devices, body(): gathered = lax.all_gather(own_copy, AXES, axis=0, tiled=True)  59.7 us
    gather x1, local copies, waits for them, and re-layouts, body(): slot_grads = grads[places]  31.1 us
    scatter x1, local copies, waits for them, and re-layouts, body(): ordered = jnp.zeros_like(gathered).at[places].set(gathered)  31 us
    pallas_call x1, Pallas kernels, exchange(): pl.pallas_call(functools.partial(exchange_kernel, nb, nr), out_shape=jax....  11.4 us
  transfers between devices with their start and end apart: 2, of which 2 were waited for; matrix products, arithmetic and copies ran while one was open for 1% of the time, Pallas kernels for 3%

profile of v2, /device:TPU:0, one launch (start us, length us, event | category | flops | bytes accessed | tf_op | source)
XLA Modules:
  0.0 394.3 jit_solution(11322352453878452621)
XLA Ops:
  7.2 0.0 all-gather.2.cloned.1.call-start
  7.2 1.7 convert_element_type.6
  8.9 0.0 all-gather.2.cloned.1.call-update
  8.9 0.0 reduce-scatter.2.cloned.1.call-start
  9.0 1.1 reduce_sum.45
  10.1 1.1 multiply_reduce_fusion
  11.2 11.4 %shard_map.189 = f32[32,2,512]{2,1,0:T(2,128)S(1)} custom-call(f32[2,512]{1,0:T(2,128)S(1)} %pad_maximum_fusion.x_ref), custom_call_target="tpu_custom_call" | custom-call | tf_op jit(solution)/shard_map/pallas_call | solution.py:112
  22.6 0.1 slice_reduce_fusion.1
  22.8 0.6 pad_maximum_fusion.1.sx_ref
  23.4 0.8 broadcast_clamp_fusion
  24.2 59.7 %all-gather.2.cloned.1.call-done = bf16[6144,512]{1,0:T(8,128)(2,1)} async-done(((bf16[192,512]{1,0:T(8,128)(2,1)}), bf16[6144,512]{1,0:T(8,128)(2,1)}) %all-gather.2.cloned.1.call-update) | async-done | bytes 6291472 | tf_op jit(solution)/shard_map/all_gather | solution.py:655
  83.9 31.0 %scatter_custom_fusion.tab_hbm = bf16[6144,512]{1,0:T(8,128)(2,1)} fusion(s32[6144]{0:T(1024)S(1)} %get-tuple-element.20, bf16[6144,512]{1,0:T(8,128)(2,1)} %all-gather.2.cloned.1.call-done, bf16[]{:T(256)} %constant.107.clone.1), kind=kCustom, calls=%fused_computation.2 | custom fusion | bytes 6291968 | tf_op jit(solution)/shard_map/scatter | solution.py:656
  114.9 82.8 %shard_map.190 = (f32[256,512]{1,0:T(8,128)}, f32[256,512]{1,0:T(8,128)}, f32[6144,512]{1,0:T(8,128)}) custom-call(f32[256,512]{1,0:T(8,128)} %bitcast.14, f32[256,512]{1,0:T(8,128)} %bitcast.15, f32[2,512]{1,0:T(2,128)} %pad_maximum_fusion.1.sx_ref, bf16[6144,512]{1,0:T(8,128)(2,1)} %scatter_custom_fusion.tab_hbm, bf16[1536,768]{1,0:T(8,128)(2,1)} %constant.142.clone.a_hbm, ...), custom_call_target="tpu_custom_call" | custom-call | tf_op jit(solution)/shard_map/pallas_call | solution.py:616
  197.7 31.1 %gather_fusion = f32[6144,512]{1,0:T(8,128)} fusion(f32[6144,512]{1,0:T(8,128)} %get-tuple-element.12, s32[6144]{0:T(1024)S(1)} %get-tuple-element.19), kind=kCustom, calls=%fused_computation | custom fusion | bytes 25190400 | tf_op jit(solution)/shard_map/gather | solution.py:666
  228.8 0.0 copy-start.1
  228.8 0.0 reduce-scatter.2.cloned.1.call-update
  228.9 0.9 compare_select_fusion.1
  229.8 153.8 %reduce-scatter.2.cloned.1.call-done = f32[192,512]{1,0:T(8,128)} async-done(((f32[6144,512]{1,0:T(8,128)}), f32[192,512]{1,0:T(8,128)}) %reduce-scatter.2.cloned.1.call-update) | async-done | bytes 393232 | tf_op jit(solution)/shard_map/reduce_scatter | solution.py:667
  383.5 0.0 copy-done
  383.5 0.0 copy-done.3
  383.5 0.0 copy-done.4
  383.5 2.4 fusion.18
  385.9 0.8 copy.25
  386.7 0.8 copy.26
  (11 shorter events, 0.1 us)
Async XLA Ops:
  7.2 76.7 %all-gather.2.cloned.1.call-start = ((), (), s32[]{:S(2)}) async-start(), calls=%async_computation.1 | async-start | bytes 6488064 | tf_op jit(solution)/shard_map/all_gather | solution.py:655
  8.9 374.6 %reduce-scatter.2.cloned.1.call-start = ((), (), s32[]{:S(2)}) async-start(), calls=%async_computation.2 | async-start | bytes 12976128 | tf_op jit(solution)/shard_map/reduce_scatter | solution.py:667
  228.8 154.7 %copy-start = (f32[192,512]{1,0:T(8,128)S(1)}, f32[192,512]{1,0:T(8,128)}, u32[]{:S(2)}) copy-start(f32[192,512]{1,0:T(8,128)} %param.17) | copy-start | bytes 1179652
  228.8 154.7 %copy-start.3 = (f32[192,512]{1,0:T(8,128)S(1)}, f32[192,512]{1,0:T(8,128)}, u32[]{:S(2)}) copy-start(f32[192,512]{1,0:T(8,128)} %param.19) | copy-start | bytes 1179652
  228.8 154.7 %copy-start.4 = (f32[192,512]{1,0:T(8,128)S(1)}, f32[192,512]{1,0:T(8,128)}, u32[]{:S(2)}) copy-start(f32[192,512]{1,0:T(8,128)} %param.18) | copy-start | bytes 1179652
  228.8 157.1 %copy-start.2 = (f32[256,512]{1,0:T(8,128)S(1)}, f32[256,512]{1,0:T(8,128)}, u32[]{:S(2)}) copy-start(f32[256,512]{1,0:T(8,128)} %get-tuple-element.10) | copy-start | bytes 1572868
  228.8 157.9 %copy-start.1 = (f32[256,512]{1,0:T(8,128)S(1)}, f32[256,512]{1,0:T(8,128)}, u32[]{:S(2)}) copy-start(f32[256,512]{1,0:T(8,128)} %get-tuple-element.11) | copy-start | bytes 1572868
Sparse Core Ops, SparseCore 0:
  11.6 72.2 all-gather.1
  229.0 154.5 reduce-scatter.1

commit v3 on v2

--- a/solution.py
+++ b/solution.py
@@ -116,7 +116,7 @@
         out_specs=pl.BlockSpec(memory_space=pltpu.VMEM),
         scratch_shapes=[pltpu.SemaphoreType.DMA, pltpu.SemaphoreType.DMA],
         compiler_params=pltpu.CompilerParams(
-            collective_id=x.shape[0] + 8 * (x.shape[1] != C), has_side_effects=True, vmem_limit_bytes=32 * 2**20
+            collective_id=0, has_side_effects=True, vmem_limit_bytes=32 * 2**20
         ),
     )(x)
 
@@ -135,6 +135,11 @@
 
 def close(v):
     return jnp.sum(v, axis=0, keepdims=True)
+
+
+def put(ref, start, v):
+    for j in range(4):
+        ref[pl.ds(start * 4 + j, v.shape[0], stride=4), :] = v[:, j * 128 : (j + 1) * 128]
 
 
 def gelu_both(v):
@@ -406,10 +411,10 @@
         for j in range(blocks):
             out_ref[...] += dot(a_low[j], tab[down_rows(j), :])
             for h in range(C // 256):
-                stage0[pl.ds(j * C + h * 256, 256), :] = dot(a_low[j, :, half_cols(h)], gy_low[...], (0, 0))
+                put(stage0, j * C + h * 256, dot(a_low[j, :, half_cols(h)], gy_low[...], (0, 0)))
 
     tot = share(3, mid_rows, merge_sum, outputs) * (1.0 / every)
-    st_down = pltpu.make_async_copy(stage0, grad_hbm.at[pl.ds(2 * C + FF, FF)], store_sem.at[0])
+    st_down = pltpu.make_async_copy(stage0, grad_hbm.at[pl.ds(4 * (2 * C + FF), 4 * FF)], store_sem.at[0])
     st_down.start()
     for j in range(blocks):
         tb_, tg_, sc = tot[j : j + 1], tot[blocks + j : blocks + j + 1], mid_gain(j) * inv_h[j : j + 1]
@@ -433,10 +438,10 @@
     def grad_up():
         for j in range(blocks):
             for h in range(C // 256):
-                stage1[pl.ds(j * C + h * 256, 256), :] = dot(c_low[:, half_cols(h)], gh_low[j], (0, 0))
+                put(stage1, j * C + h * 256, dot(c_low[:, half_cols(h)], gh_low[j], (0, 0)))
 
     tot = share(4, jnp.concatenate([b_ffn, g_ffn, g_fp, sum_c, sum_ch], axis=0), merge_sum, grad_up) * (1.0 / every)
-    st_up = pltpu.make_async_copy(stage1, grad_hbm.at[pl.ds(2 * C, FF)], store_sem.at[1])
+    st_up = pltpu.make_async_copy(stage1, grad_hbm.at[pl.ds(4 * 2 * C, 4 * FF)], store_sem.at[1])
     st_up.start()
     scale_f = row(8) * inv_f
     mean_hat = tot[4:5] + scale_f * (tot[2:3] - tot[1:2] * hats)
@@ -463,7 +468,7 @@
 
     def grad_out():
         for h in range(C // 256):
-            stage0[pl.ds(C + h * 256, 256), :] = dot(t_low[:, half_cols(h)], gh_low[0], (0, 0))
+            put(stage0, C + h * 256, dot(t_low[:, half_cols(h)], gh_low[0], (0, 0)))
 
     tot = share(5, jnp.concatenate([b_pair, g_lg, g_sg], axis=0), merge_sum, grad_out) * (1.0 / every)
     sc_l, sc_s = row(2) * inv_l, row(4) * inv_s
@@ -525,9 +530,9 @@
     @pl.loop(0, 4)
     def _(t):
         s = pl.ds(pl.multiple_of(t * 256, 256), 256)
-        stage0[pl.ds(pl.multiple_of(2 * C + t * 256, 256), 256), :] = dot(tbt[s, :], prod_l[...])
-
-    stage0[pl.ds(2 * C + 976, 32), :] = dot(bst_ref[...], prod_s[...])
+        put(stage0, 2 * C + t * 256, dot(tbt[s, :], prod_l[...]))
+
+    put(stage0, 2 * C + 976, dot(bst_ref[...], prod_s[...]))
 
     @pl.when(has_below)
     def _():
@@ -563,19 +568,20 @@
 
     def grad_in():
         for h in range(C // 256):
-            stage0[pl.ds(h * 256, 256), :] = dot(pre_low[:, half_cols(h)], t_low[...], (0, 0))
+            put(stage0, h * 256, dot(pre_low[:, half_cols(h)], t_low[...], (0, 0)))
 
     tot = share(6, jnp.concatenate([b_pre, g_pre], axis=0), merge_sum, grad_in) * (1.0 / every)
     scale_x = row(0) * inv_x
     norms = [g_pre, b_pre, g_lg, b_pair, g_sg, b_pair, g_proj, b_proj, g_ffn, b_ffn]
     norms += [mid_rows[blocks + j : blocks + j + 1] for j in range(blocks)]
     base = 2 * C + 976
-    stage0[pl.ds(base + 32, 16), :] = jnp.concatenate(norms + [jnp.zeros((2, C), f32)], axis=0)
+    put(stage0, base + 32, jnp.concatenate(norms + [jnp.zeros((2, C), f32)], axis=0))
     for j in range(blocks):
-        stage0[pl.ds(base + 25 + j, 1), :] = mid_rows[j : j + 1]
+        for k in range(4):
+            stage0[pl.ds((base + 25 + j) * 4 + k, 1), :] = mid_rows[j : j + 1, k * 128 : (k + 1) * 128]
     stores = [
-        pltpu.make_async_copy(stage0.at[pl.ds(0, 2 * C)], grad_hbm.at[pl.ds(0, 2 * C)], store_sem.at[2]),
-        pltpu.make_async_copy(stage0.at[pl.ds(2 * C, 2 * C)], grad_hbm.at[pl.ds(2 * C + 2 * FF, 2 * C)], store_sem.at[3]),
+        pltpu.make_async_copy(stage0.at[pl.ds(0, 8 * C)], grad_hbm.at[pl.ds(0, 8 * C)], store_sem.at[2]),
+        pltpu.make_async_copy(stage0.at[pl.ds(8 * C, 8 * C)], grad_hbm.at[pl.ds(4 * (2 * C + 2 * FF), 8 * C)], store_sem.at[3]),
     ]
     for c in stores:
         c.start()
@@ -609,7 +615,7 @@
     scratch += [low, vm((3 * n, C), bf16), pix, wide_spec, wide_spec, wide_spec, low_spec, low_spec, low_spec]
     scratch += [pix, pix, pix, low, pix, pix, low, low]
     scratch += [vm((FF // C, n, C)), vm((FF // C, n, C)), vm((FF // C, n, C), bf16), vm((FF // C, n, C), bf16), pix, vm((4, 256, C))]
-    scratch += [vm((FF, C)), vm((FF, C)), vm((2, n, C), bf16), vm((2, n, C), bf16)]
+    scratch += [vm((4 * FF, 128)), vm((4 * FF, 128)), vm((2, n, C), bf16), vm((2, n, C), bf16)]
     scratch += [vm((nr, w, C)) for w in WIDTHS] + [vm((nb, w, C)) for w in WIDTHS]
     dma = pltpu.SemaphoreType.DMA
     scratch += [dma((len(WIDTHS), 2)), dma((len(WIDTHS), 2)), dma((4,)), dma((4,)), dma((9,)), dma((4,))]
@@ -618,13 +624,198 @@
         out_shape=[
             jax.ShapeDtypeStruct((n, C), f32),
             jax.ShapeDtypeStruct((n, C), f32),
-            jax.ShapeDtypeStruct(tab.shape, f32),
+            jax.ShapeDtypeStruct((4 * tab.shape[0], 128), f32),
         ],
         in_specs=[vmem] * 3 + [anywhere] * 5 + [vmem] * 2 + [anywhere] * 2,
         out_specs=[vmem, vmem, anywhere],
         scratch_shapes=scratch,
         compiler_params=pltpu.CompilerParams(collective_id=1, has_side_effects=True, vmem_limit_bytes=62 * 2**20),
     )(x, cot, sx, tab, a, at, b, bt, bs, bst, c, ct)
+
+
+def flip(b, m):
+    k = 0
+    while m >> k:
+        if (m >> k) & 1:
+            b = b + (1 - 2 * lax.rem(b // 2**k, 2)) * 2**k
+        k += 1
+    return b
+
+
+def reduce_plan(nb):
+    bits = nb.bit_length() - 1
+    plan = []
+    for p in range(bits):
+        order = [(p + t) % bits for t in range(bits)]
+        steps, kept = [], list(range(nb))
+        for o in order:
+            sent = [m for m in kept if (m >> o) & 1]
+            kept = [m for m in kept if not (m >> o) & 1]
+            steps.append((o, sent, kept))
+        plan.append(steps)
+    return plan
+
+
+def reduce_kernel(
+    nb, nr, idx_ref, grad_hbm, out_ref,
+    grad, tmp, sib_out, sib_in, pair, hops, z_out, z_in,
+    load_sem, sib_send, sib_recv, hop_send, hop_recv, z_send, z_recv,
+):
+    nz = nr // 2
+    own = idx_ref.shape[0] // (nb * nr)
+    lines = 4 * own
+    unit = 32 if own % 32 == 0 else 8
+    plan = reduce_plan(nb)
+    parts = len(plan)
+    size = lines // parts
+    b = lax.axis_index("batch")
+    r = lax.axis_index("rows")
+    z, c = r // 2, lax.rem(r, 2)
+    sibling = (b, r + 1 - 2 * c)
+    load = pltpu.make_async_copy(grad_hbm, grad, load_sem)
+    load.start()
+
+    barrier = pltpu.get_barrier_semaphore()
+    pl.semaphore_signal(barrier, inc=1, device_id=sibling, device_id_type=MESH)
+    for k in range(parts):
+        pl.semaphore_signal(barrier, inc=1, device_id=(flip(b, 2**k), r), device_id_type=MESH)
+    for k in range(1, nz):
+        pl.semaphore_signal(barrier, inc=1, device_id=(b, 2 * lax.rem(z + k, nz) + c), device_id_type=MESH)
+
+    def column(i):
+        return lax.rem(z + 1 + i, nz)
+
+    def collect(m, zz, cc):
+        start = (flip(b, m) * nr + 2 * zz + cc) * own
+
+        @pl.loop(0, own // unit)
+        def _(g):
+            for u in range(unit):
+                tmp[pl.ds(pl.multiple_of((g * unit + u) * 4, 4), 4), :] = grad[idx_ref[start + g * unit + u]]
+
+    load.wait()
+    pl.semaphore_wait(barrier, 1 + parts + nz - 1)
+
+    def to_sibling(i, m):
+        return pltpu.make_async_remote_copy(
+            sib_out.at[i, m], sib_in.at[i, m], sib_send.at[i, m], sib_recv.at[i, m], device_id=sibling, device_id_type=MESH
+        )
+
+    @pl.loop(0, nz)
+    def _(i):
+        for m in range(nb):
+            collect(m, column(i), 1 - c)
+            sib_out[i, m] = tmp[...].astype(bf16)
+            to_sibling(i, m).start()
+
+    def rows_of(p):
+        return pl.ds(p * size, size)
+
+    def slots(p, t):
+        at = sum(len(plan[p][k][2]) for k in range(t))
+        return at, len(plan[p][t][2])
+
+    def hop(i, p, t, m):
+        o, sent, kept = plan[p][t]
+        at, _ = slots(p, t)
+        return pltpu.make_async_remote_copy(
+            pair.at[i, m, rows_of(p)], hops.at[i, p, at + kept.index(m ^ (1 << o))], hop_send.at[i, p, t], hop_recv.at[i, p, t],
+            device_id=(flip(b, 1 << o), r), device_id_type=MESH,
+        )
+
+    def hop_wait(i, p, t, sem):
+        at, count = slots(p, t)
+        whole = hops.at[i, p, pl.ds(at, count)]
+        pltpu.make_async_copy(whole, whole, sem.at[i, p, t]).wait()
+
+    @pl.loop(0, nz)
+    def _(i):
+        for m in reversed(range(nb)):
+            collect(m, column(i), c)
+            to_sibling(i, m).wait_recv()
+            pair[i, m] = (tmp[...] + sib_in[i, m].astype(f32)).astype(bf16)
+            for p in range(parts):
+                if m in plan[p][0][1]:
+                    hop(i, p, 0, m).start()
+
+    for t in range(parts - 1):
+
+        @pl.loop(0, nz)
+        def _(i):
+            for p in range(parts):
+                hop_wait(i, p, t, hop_recv)
+                at, _ = slots(p, t)
+                for k, m in enumerate(plan[p][t][2]):
+                    pair[i, m, rows_of(p)] = (
+                        pair[i, m, rows_of(p)].astype(f32) + hops[i, p, at + k].astype(f32)
+                    ).astype(bf16)
+                    if m in plan[p][t + 1][1]:
+                        hop(i, p, t + 1, m).start()
+
+    def to_owner(i):
+        return pltpu.make_async_remote_copy(
+            z_out.at[i], z_in.at[i], z_send.at[i], z_recv.at[i], device_id=(b, 2 * column(i) + c), device_id_type=MESH
+        )
+
+    @pl.loop(0, nz)
+    def _(i):
+        for p in range(parts):
+            hop_wait(i, p, parts - 1, hop_recv)
+            at, _ = slots(p, parts - 1)
+            tmp[rows_of(p), :] = pair[i, 0, rows_of(p)].astype(f32) + hops[i, p, at].astype(f32)
+
+        @pl.when(i < nz - 1)
+        def _():
+            z_out[i] = tmp[...].astype(bf16)
+            to_owner(i).start()
+
+    for i in range(nz - 1):
+        to_owner(i).wait_recv()
+        tmp[...] += z_in[i].astype(f32)
+    for j in range(4):
+        out_ref[:, j * 128 : (j + 1) * 128] = tmp[pl.ds(j, own, stride=4), :]
+
+    @pl.loop(0, nz)
+    def _(i):
+        for m in range(nb):
+            to_sibling(i, m).wait_send()
+        for p in range(parts):
+            for t in range(parts):
+                hop_wait(i, p, t, hop_send)
+
+    for i in range(nz - 1):
+        to_owner(i).wait_send()
+
+
+def reduce_slots(grads, places, own, nb, nr):
+    nz, parts = nr // 2, nb.bit_length() - 1
+    lines = 4 * own
+    vm = lambda shape, dtype=bf16: pltpu.VMEM(shape, dtype)
+    dma = pltpu.SemaphoreType.DMA
+    return pl.pallas_call(
+        functools.partial(reduce_kernel, nb, nr),
+        out_shape=jax.ShapeDtypeStruct((own, C), f32),
+        in_specs=[pl.BlockSpec(memory_space=pltpu.SMEM), pl.BlockSpec(memory_space=pl.ANY)],
+        out_specs=pl.BlockSpec(memory_space=pltpu.VMEM),
+        scratch_shapes=[
+            vm((grads.shape[0] // 4, 4, 128), f32),
+            vm((lines, 128), f32),
+            vm((nz, nb, lines, 128)),
+            vm((nz, nb, lines, 128)),
+            vm((nz, nb, lines, 128)),
+            vm((nz, parts, nb - 1, lines // parts, 128)),
+            vm((nz, lines, 128)),
+            vm((nz, lines, 128)),
+            dma,
+            dma((nz, nb)),
+            dma((nz, nb)),
+            dma((nz, parts, parts)),
+            dma((nz, parts, parts)),
+            dma((nz,)),
+            dma((nz,)),
+        ],
+        compiler_params=pltpu.CompilerParams(collective_id=2, has_side_effects=True, vmem_limit_bytes=48 * 2**20),
+    )(places, grads.reshape(-1, 4, 128))
 
 
 def table_place(t):
@@ -663,9 +854,8 @@
     d = all_one[:, 0] - m_x
     q_x = (jnp.sum(all_one[:, 1], axis=0) + n * jnp.sum(d * d, axis=0)) / (n * nb * nr)
     result, grad_x, grads = core(x, cot, jnp.stack([m_x, q_x]), ordered, nb, nr)
-    slot_grads = grads[places]
-    reduced = lax.psum_scatter(slot_grads, AXES, scatter_dimension=0, tiled=True)
     own_count = master.shape[0]
+    reduced = reduce_slots(grads, places, own_count, nb, nr)
     place = lax.axis_index("batch") * nr + lax.axis_index("rows")
     own_rows = lax.dynamic_slice_in_dim(slot_rows, place * own_count, own_count)
     rates = jnp.where(own_rows >= norm_start, norm_rate, matrix_rate)[:, None]

time: 395 us -> 256 us (0.65)
  waiting for transfers between devices: 213 us -> 58.9 us
  Pallas kernels: 94.2 us -> 140 us
  local copies, waits for them, and re-layouts: 63.7 us -> 33.4 us
    reduce_scatter x1 -> x0, waiting for transfers between devices: 154 us -> none  [body(): lax.psum_scatter(slot_grads, AXES, scatter_dimension=0, tiled=True)]
    pallas_call x0 -> x1, Pallas kernels: none -> 46.1 us  [reduce_slots(): pl.pallas_call(functools.partial(reduce_kernel, nb, nr), out_shape=jax.Sh...]
    gather x1 -> x0, local copies, waits for them, and re-layouts: 31.1 us -> none  [body(): slot_grads = grads[places]]
  transfers between devices with their start and end apart: 2 -> 1, of which waited for: 2 -> 1; matrix products, arithmetic and copies ran while one was open for 1% -> 2% of each run, Pallas kernels for 3% -> 4%
where the time goes in v3:
time: 256 us; the launch traced here: 254 us
  Pallas kernels  140 us (55%)
  waiting for transfers between devices  58.9 us (23%)
  local copies, waits for them, and re-layouts  33.4 us (13%)
  between operations  14.1 us (6%)
  other arithmetic  7.66 us (3%)
    pallas_call x1, Pallas kernels, core(): pl.pallas_call(functools.partial(core_kernel, nb, nr), out_shape=[jax.Sha...  82.7 us
    all_gather x1, waiting for transfers between devices, body(): gathered = lax.all_gather(own_copy, AXES, axis=0, tiled=True)  58.9 us
    pallas_call x1, Pallas kernels, reduce_slots(): pl.pallas_call(functools.partial(reduce_kernel, nb, nr), out_shape=jax.Sh...  46.1 us
    scatter x1, local copies, waits for them, and re-layouts, body(): ordered = jnp.zeros_like(gathered).at[places].set(gathered)  31 us
    pallas_call x1, Pallas kernels, exchange(): pl.pallas_call(functools.partial(exchange_kernel, nb, nr), out_shape=jax....  11.4 us
  transfers between devices with their start and end apart: 1, of which 1 were waited for; matrix products, arithmetic and copies ran while one was open for 2% of the time, Pallas kernels for 4%

profile of v3, /device:TPU:0, one launch (start us, length us, event | category | flops | bytes accessed | tf_op | source)
XLA Modules:
  0.0 254.4 jit_solution(13014666284953733478)
XLA Ops:
  7.2 0.0 all-gather.2.cloned.1.call-start
  7.2 1.7 convert_element_type.6
  8.9 0.0 all-gather.2.cloned.1.call-update
  8.9 1.1 reduce_sum.45
  10.0 1.1 multiply_reduce_fusion
  11.2 11.4 %shard_map.189 = f32[32,2,512]{2,1,0:T(2,128)S(1)} custom-call(f32[2,512]{1,0:T(2,128)S(1)} %pad_maximum_fusion.x_ref), custom_call_target="tpu_custom_call" | custom-call | tf_op jit(solution)/shard_map/pallas_call | solution.py:112
  22.6 0.8 compare_select_fusion.1
  23.3 0.1 slice_reduce_fusion.1
  23.5 0.6 pad_maximum_fusion.1.sx_ref
  24.1 0.8 compare_select_fusion
  24.9 58.9 %all-gather.2.cloned.1.call-done = bf16[6144,512]{1,0:T(8,128)(2,1)} async-done(((bf16[192,512]{1,0:T(8,128)(2,1)}), bf16[6144,512]{1,0:T(8,128)(2,1)}) %all-gather.2.cloned.1.call-update) | async-done | bytes 6291472 | tf_op jit(solution)/shard_map/all_gather | solution.py:846
  83.9 31.0 %scatter_custom_fusion.tab_hbm = bf16[6144,512]{1,0:T(8,128)(2,1)} fusion(s32[6144]{0:T(1024)S(1)} %get-tuple-element.19, bf16[6144,512]{1,0:T(8,128)(2,1)} %all-gather.2.cloned.1.call-done, bf16[]{:T(256)} %constant.107.clone.1), kind=kCustom, calls=%fused_computation.1 | custom fusion | bytes 6291968 | tf_op jit(solution)/shard_map/scatter | solution.py:847
  114.9 82.7 %shard_map.190 = (f32[256,512]{1,0:T(8,128)}, f32[256,512]{1,0:T(8,128)}, f32[24576,128]{1,0:T(8,128)}) custom-call(f32[256,512]{1,0:T(8,128)} %bitcast.16, f32[256,512]{1,0:T(8,128)} %bitcast.17, f32[2,512]{1,0:T(2,128)} %pad_maximum_fusion.1.sx_ref, bf16[6144,512]{1,0:T(8,128)(2,1)} %scatter_custom_fusion.tab_hbm, ...), custom_call_target="tpu_custom_call" | custom-call | tf_op jit(solution)/shard_map/pallas_call | solution.py:622
  197.6 0.0 copy-start
  197.7 0.0 copy-start.3
  197.7 0.0 copy-start.4
  197.7 0.0 copy-start.2
  197.7 0.0 copy-start.1
  197.7 46.1 %shard_map.191 = f32[192,512]{1,0:T(8,128)S(1)} custom-call(s32[6144]{0:T(1024)S(1)} %get-tuple-element.20.idx_ref, f32[6144,4,128]{2,1,0:T(4,128)} %bitcast.15), custom_call_target="tpu_custom_call" | custom-call | tf_op jit(solution)/shard_map/pallas_call | solution.py:795
  243.8 0.0 copy-done
  243.9 1.4 fusion.18
  245.2 0.8 copy.26
  246.0 0.8 copy.27
  246.8 0.7 copy.28
  (9 shorter events, 0.1 us)
Async XLA Ops:
  7.2 76.7 %all-gather.2.cloned.1.call-start = ((), (), s32[]{:S(2)}) async-start(), calls=%async_computation | async-start | bytes 6488064 | tf_op jit(solution)/shard_map/all_gather | solution.py:846
  197.6 46.2 %copy-start = (f32[192,512]{1,0:T(8,128)S(1)}, f32[192,512]{1,0:T(8,128)}, u32[]{:S(2)}) copy-start(f32[192,512]{1,0:T(8,128)} %param.17) | copy-start | bytes 1179652
  197.7 46.2 %copy-start.3 = (f32[192,512]{1,0:T(8,128)S(1)}, f32[192,512]{1,0:T(8,128)}, u32[]{:S(2)}) copy-start(f32[192,512]{1,0:T(8,128)} %param.19) | copy-start | bytes 1179652
  197.7 46.2 %copy-start.4 = (f32[192,512]{1,0:T(8,128)S(1)}, f32[192,512]{1,0:T(8,128)}, u32[]{:S(2)}) copy-start(f32[192,512]{1,0:T(8,128)} %param.18) | copy-start | bytes 1179652
  197.7 47.5 %copy-start.2 = (f32[256,512]{1,0:T(8,128)S(1)}, f32[256,512]{1,0:T(8,128)}, u32[]{:S(2)}) copy-start(f32[256,512]{1,0:T(8,128)} %get-tuple-element.10) | copy-start | bytes 1572868
  197.7 48.3 %copy-start.1 = (f32[256,512]{1,0:T(8,128)S(1)}, f32[256,512]{1,0:T(8,128)}, u32[]{:S(2)}) copy-start(f32[256,512]{1,0:T(8,128)} %get-tuple-element.11) | copy-start | bytes 1572868
Sparse Core Ops, SparseCore 0:
  11.6 72.2 all-gather.1

commit v4 on v3

--- a/solution.py
+++ b/solution.py
@@ -76,49 +76,6 @@
 
 def dot(a, b, dims=(1, 0)):
     return lax.dot_general(a, b, (((dims[0],), (dims[1],)), ((), ())), preferred_element_type=f32)
-
-
-def exchange_kernel(nb, nr, x_ref, o_ref, send_sem, recv_sem):
-    nd = nb * nr
-    me = lax.axis_index("batch") * nr + lax.axis_index("rows")
-
-    def peer(k):
-        other = lax.rem(me + k, nd)
-        return (other // nr, lax.rem(other, nr))
-
-    barrier = pltpu.get_barrier_semaphore()
-
-    @pl.loop(1, nd)
-    def _(k):
-        pl.semaphore_signal(barrier, inc=1, device_id=peer(k), device_id_type=pl.DeviceIdType.MESH)
-
-    o_ref[me] = x_ref[...]
-    pl.semaphore_wait(barrier, nd - 1)
-
-    @pl.loop(1, nd)
-    def _(k):
-        pltpu.make_async_remote_copy(
-            o_ref.at[me], o_ref.at[me], send_sem, recv_sem, device_id=peer(k), device_id_type=pl.DeviceIdType.MESH
-        ).start()
-
-    others = o_ref.at[pl.ds(0, nd - 1)]
-    pltpu.make_async_copy(others, others, recv_sem).wait()
-    pltpu.make_async_copy(others, others, send_sem).wait()
-
-
-def exchange(rows):
-    x = jnp.stack(rows)
-    nb, nr = lax.axis_size("batch"), lax.axis_size("rows")
-    return pl.pallas_call(
-        functools.partial(exchange_kernel, nb, nr),
-        out_shape=jax.ShapeDtypeStruct((nb * nr,) + x.shape, f32),
-        in_specs=[pl.BlockSpec(memory_space=pltpu.VMEM)],
-        out_specs=pl.BlockSpec(memory_space=pltpu.VMEM),
-        scratch_shapes=[pltpu.SemaphoreType.DMA, pltpu.SemaphoreType.DMA],
-        compiler_params=pltpu.CompilerParams(
-            collective_id=0, has_side_effects=True, vmem_limit_bytes=32 * 2**20
-        ),
-    )(x)
 
 
 MESH = pl.DeviceIdType.MESH
@@ -818,6 +775,267 @@
     )(places, grads.reshape(-1, 4, 128))
 
 
+def gather_kernel(
+    nb, nr, x_ref, master_ref, all_ref, sx_ref,
+    lin, stat_one, stat_two,
+    stat_send, stat_recv, z_send, z_recv, b_send, b_recv, half_send, half_recv, sib_send, sib_recv,
+):
+    nz = nr // 2
+    own = master_ref.shape[0]
+    lines = 4 * own
+    n = x_ref.shape[0]
+    b = lax.axis_index("batch")
+    r = lax.axis_index("rows")
+    z, c = r // 2, lax.rem(r, 2)
+    sibling = (b, r + 1 - 2 * c)
+    square = nb == 4
+
+    barrier = pltpu.get_barrier_semaphore()
+    for k in range(1, nr):
+        pl.semaphore_signal(barrier, inc=1, device_id=(b, lax.rem(r + k, nr)), device_id_type=MESH)
+    for m in range(1, nb):
+        pl.semaphore_signal(barrier, inc=1, device_id=(flip(b, m), r), device_id_type=MESH)
+    for j in range(4):
+        lin[pl.ds(j, own, stride=4), :] = master_ref[:, j * 128 : (j + 1) * 128]
+
+    def place(m, zz, core):
+        return flip(b, m) * nr + 2 * zz + core
+
+    all_ref[place(0, z, c)] = lin[...].astype(bf16)
+    pl.semaphore_wait(barrier, nr - 1 + nb - 1)
+
+    def along_z(zz, up):
+        at = place(0, zz, c)
+        return pltpu.make_async_remote_copy(
+            all_ref.at[at], all_ref.at[at], z_send.at[zz], z_recv.at[zz],
+            device_id=(b, r + 2 if up else r - 2), device_id_type=MESH,
+        )
+
+    def to_peer(m, zz):
+        at = place(0, zz, c)
+        return pltpu.make_async_remote_copy(
+            all_ref.at[at], all_ref.at[at], b_send.at[m, zz], b_recv.at[m, zz], device_id=(flip(b, m), r), device_id_type=MESH
+        )
+
+    def from_peer(m, zz):
+        at = all_ref.at[place(m, zz, c)]
+        return pltpu.make_async_copy(at, at, b_recv.at[m, zz])
+
+    def half(m, zz, h, to):
+        at = all_ref.at[place(m, zz, c), pl.ds(h * (lines // 2), lines // 2)]
+        return pltpu.make_async_remote_copy(
+            at, at, half_send.at[h, zz], half_recv.at[h, zz], device_id=(flip(b, to), r), device_id_type=MESH
+        )
+
+    def to_sibling(m, zz, core):
+        at = place(m, zz, core)
+        return pltpu.make_async_remote_copy(
+            all_ref.at[at], all_ref.at[at], sib_send.at[m, zz], sib_recv.at[m, zz], device_id=sibling, device_id_type=MESH
+        )
+
+    def sends(zz):
+        for m in range(1, nb):
+            if not (square and m == 3):
+                to_peer(m, zz).start()
+        to_sibling(0, zz, c).start()
+
+    def own_column(k):
+        if k == 0:
+
+            @pl.when(z < nz - 1)
+            def _():
+                along_z(z, True).start()
+
+            @pl.when(z > 0)
+            def _():
+                along_z(z, False).start()
+
+            sends(z)
+            return
+
+        @pl.when(z >= k)
+        def _():
+            along_z(z - k, True).wait_recv()
+
+            @pl.when(z < nz - 1)
+            def _():
+                along_z(z - k, True).start()
+
+            sends(z - k)
+
+        @pl.when(z + k < nz)
+        def _():
+            along_z(z + k, False).wait_recv()
+
+            @pl.when(z > 0)
+            def _():
+                along_z(z + k, False).start()
+
+            sends(z + k)
+
+    def each(k, fn):
+        if k == 0:
+            fn(z)
+            return
+
+        @pl.when(z >= k)
+        def _():
+            fn(z - k)
+
+        @pl.when(z + k < nz)
+        def _():
+            fn(z + k)
+
+    def pass_on(zz):
+        for m in range(1, nb):
+            if square and m == 3:
+                continue
+            from_peer(m, zz).wait()
+            if square:
+                half(m, zz, 2 - m, 3 - m).start()
+            to_sibling(m, zz, c).start()
+
+    def corner(zz):
+        if square:
+            for h in range(2):
+                half(3, zz, h, 0).wait_recv()
+            to_sibling(3, zz, c).start()
+
+    zero = jnp.zeros((8, C), f32)
+
+    def share(stage, v, buf, mine, size, where):
+        buf[mine] = v
+        for k in range(1, size):
+            pltpu.make_async_remote_copy(
+                buf.at[mine], buf.at[mine], stat_send.at[stage], stat_recv.at[stage], device_id=where(k), device_id_type=MESH
+            ).start()
+
+    def shared(stage, buf, size, count):
+        got = buf.at[pl.ds(0, size - 1)]
+        pltpu.make_async_copy(got, got, stat_recv.at[stage]).wait()
+        v = buf[...]
+        m = jnp.sum(v[:, :1], axis=0) * (1.0 / size)
+        d = v[:, :1] - m
+        return jnp.concatenate([m, jnp.sum(v[:, 1:], axis=0) + count * jnp.sum(d * d, axis=0)], axis=0)
+
+    own_column(0)
+    m_x = close(chunks(n, lambda s, a: a + fold(x_ref[s, :]), zero)) * (1.0 / n)
+
+    def sq(s, a):
+        d = x_ref[s, :] - m_x
+        return a + fold(d * d)
+
+    v_x = close(chunks(n, sq, zero))
+    share(0, jnp.concatenate([m_x, v_x], axis=0), stat_one, r, nr, lambda k: (b, lax.rem(r + k, nr)))
+    for k in range(1, nz):
+        own_column(k)
+        each(k - 1, pass_on)
+        if k > 1:
+            each(k - 2, corner)
+        if k == 1:
+            v = shared(0, stat_one, nr, float(n))
+            share(1, v, stat_two, b, nb, lambda m: (flip(b, m), r))
+    each(nz - 1, pass_on)
+    if nz > 1:
+        each(nz - 2, corner)
+    each(nz - 1, corner)
+    v = shared(1, stat_two, nb, float(n * nr))
+    sx_ref[0:1, :] = v[0:1]
+    sx_ref[1:2, :] = v[1:2] * (1.0 / (n * nb * nr))
+    for m in range(nb):
+
+        @pl.loop(0, nz)
+        def _(zz):
+            to_sibling(m, zz, 1 - c).wait_recv()
+            to_sibling(m, zz, c).wait_send()
+            if m and not (square and m == 3):
+                to_peer(m, zz).wait_send()
+            if square and m in (1, 2):
+                half(m, zz, 2 - m, 3 - m).wait_send()
+
+    for k in range(nz):
+
+        @pl.when((z >= k) & (z < nz - 1))
+        def _():
+            along_z(z - k, True).wait_send()
+
+        @pl.when((z + k < nz) & (z > 0))
+        def _():
+            along_z(z + k, False).wait_send()
+
+    for stage, (buf, size) in enumerate(((stat_one, nr), (stat_two, nb))):
+        sent = buf.at[pl.ds(0, size - 1)]
+        pltpu.make_async_copy(sent, sent, stat_send.at[stage]).wait()
+
+
+def gather_rows(x, master, nb, nr):
+    own, n, nz = master.shape[0], x.shape[0], nr // 2
+    vm = lambda shape, dtype=f32: pltpu.VMEM(shape, dtype)
+    dma = pltpu.SemaphoreType.DMA
+    vmem = pl.BlockSpec(memory_space=pltpu.VMEM)
+    return pl.pallas_call(
+        functools.partial(gather_kernel, nb, nr),
+        out_shape=[jax.ShapeDtypeStruct((nb * nr, 4 * own, 128), bf16), jax.ShapeDtypeStruct((2, C), f32)],
+        in_specs=[vmem, vmem],
+        out_specs=[vmem, vmem],
+        scratch_shapes=[vm((4 * own, 128)), vm((nr, 2, C)), vm((nb, 2, C))]
+        + [dma((2,))] * 2
+        + [dma((nz,))] * 2
+        + [dma((nb, nz))] * 2
+        + [dma((2, nz))] * 2
+        + [dma((nb, nz))] * 2,
+        compiler_params=pltpu.CompilerParams(collective_id=0, has_side_effects=True, vmem_limit_bytes=24 * 2**20),
+    )(x, master)
+
+
+def order_kernel(idx_ref, rows_ref, out_hbm, flat, lin, out, store_sem):
+    total = idx_ref.shape[0]
+    unit = 32
+
+    @pl.loop(0, total // 64)
+    def _(g):
+        s = pl.ds(pl.multiple_of(g * 256, 256), 256)
+        flat[s, :] = rows_ref[s, :].astype(f32)
+
+    @pl.loop(0, total // unit)
+    def _(g):
+        for u in range(unit):
+            s = g * unit + u
+            lin[pl.ds(pl.multiple_of(idx_ref[s], 4), 4), :] = flat[pl.ds(pl.multiple_of(s * 4, 4), 4), :]
+
+    parts = store_sem.shape[0]
+    part = total // parts
+    stores = [pltpu.make_async_copy(out.at[pl.ds(p * part, part)], out_hbm.at[pl.ds(p * part, part)], store_sem.at[p]) for p in range(parts)]
+    for p in range(parts):
+
+        @pl.loop(0, part // 64)
+        def _(g):
+            start = p * part + g * 64
+            for j in range(4):
+                out[pl.ds(pl.multiple_of(start, 64), 64), j * 128 : (j + 1) * 128] = lin[pl.ds(start * 4 + j, 64, stride=4), :].astype(bf16)
+
+        stores[p].start()
+    for c in stores:
+        c.wait()
+
+
+def order_rows(rows, places):
+    total = places.shape[0]
+    return pl.pallas_call(
+        order_kernel,
+        out_shape=jax.ShapeDtypeStruct((total, C), bf16),
+        in_specs=[pl.BlockSpec(memory_space=pltpu.SMEM), pl.BlockSpec(memory_space=pltpu.VMEM)],
+        out_specs=pl.BlockSpec(memory_space=pl.ANY),
+        scratch_shapes=[
+            pltpu.VMEM((4 * total, 128), f32),
+            pltpu.VMEM((4 * total, 128), f32),
+            pltpu.VMEM((total, C), bf16),
+            pltpu.SemaphoreType.DMA((8,)),
+        ],
+        compiler_params=pltpu.CompilerParams(vmem_limit_bytes=48 * 2**20),
+    )(places * 4, rows.reshape(-1, 128))
+
+
 def table_place(t):
     start = 2 * C + 2 * FF
     k_end = start + KL * KL
@@ -842,18 +1060,11 @@
     nb, nr = lax.axis_size("batch"), lax.axis_size("rows")
     norm_start = 2 * C + 2 * FF + KL * KL + KS * KS
     places = table_place(slot_rows)
-    own_copy = master.astype(bf16)
-    gathered = lax.all_gather(own_copy, AXES, axis=0, tiled=True)
-    ordered = jnp.zeros_like(gathered).at[places].set(gathered)
     x = image_in.reshape(n, C)
     cot = cotangent.reshape(n, C)
-    m = jnp.mean(x, axis=0)
-    d = x - m
-    all_one = exchange((m, jnp.sum(d * d, axis=0)))
-    m_x = jnp.mean(all_one[:, 0], axis=0)
-    d = all_one[:, 0] - m_x
-    q_x = (jnp.sum(all_one[:, 1], axis=0) + n * jnp.sum(d * d, axis=0)) / (n * nb * nr)
-    result, grad_x, grads = core(x, cot, jnp.stack([m_x, q_x]), ordered, nb, nr)
+    rows, sx = gather_rows(x, master, nb, nr)
+    ordered = order_rows(rows, places)
+    result, grad_x, grads = core(x, cot, sx, ordered, nb, nr)
     own_count = master.shape[0]
     reduced = reduce_slots(grads, places, own_count, nb, nr)
     place = lax.axis_index("batch") * nr + lax.axis_index("rows")

time: 256 us -> 191 us (0.75)
  waiting for transfers between devices: 58.9 us -> 0 us
  Pallas kernels: 140 us -> 178 us
  local copies, waits for them, and re-layouts: 33.4 us -> 7.63 us
  between operations: 14.1 us -> 0.74 us
  other arithmetic: 7.66 us -> 3.01 us
    all_gather x1 -> x0, waiting for transfers between devices: 58.9 us -> none  [body(): gathered = lax.all_gather(own_copy, AXES, axis=0, tiled=True)]
    pallas_call x1 -> x2, Pallas kernels: 11.4 us -> 49.9 us  [the longest x1 37.2 us: gather_rows(): pl.pallas_call(functools.partial(gather_kernel, nb, nr), out_shape=[jax.S...]
    scatter x1 -> x0, local copies, waits for them, and re-layouts: 31 us -> none  [body(): ordered = jnp.zeros_like(gathered).at[places].set(gathered)]
    unnamed x13 -> x21, local copies, waits for them, and re-layouts: 2.36 us -> 7.63 us
  transfers between devices with their start and end apart: 1 -> 0, of which waited for: 1 -> 0; matrix products, arithmetic and copies ran while one was open for 2% -> 0% of each run, Pallas kernels for 4% -> 0%
where the time goes in v4:
time: 191 us; the launch traced here: 189 us
  Pallas kernels  178 us (93%)
  local copies, waits for them, and re-layouts  7.63 us (4%)
  other arithmetic  3.01 us (2%)
    pallas_call x1, Pallas kernels, core(): pl.pallas_call(functools.partial(core_kernel, nb, nr), out_shape=[jax.Sha...  81.8 us
    pallas_call x1, Pallas kernels, reduce_slots(): pl.pallas_call(functools.partial(reduce_kernel, nb, nr), out_shape=jax.Sh...  46 us
    pallas_call x1, Pallas kernels, gather_rows(): pl.pallas_call(functools.partial(gather_kernel, nb, nr), out_shape=[jax.S...  37.2 us
    pallas_call x1, Pallas kernels, order_rows(): pl.pallas_call(order_kernel, out_shape=jax.ShapeDtypeStruct((total, C), b...  12.7 us
    unnamed x21, local copies, waits for them, and re-layouts  7.63 us

profile of v4, /device:TPU:0, one launch (start us, length us, event | category | flops | bytes accessed | tf_op | source)
XLA Modules:
  0.0 189.0 jit_solution(11517871387143213861)
XLA Ops:
  0.6 0.0 copy-start.1
  0.6 1.0 copy-done.1
  1.7 1.0 copy-done.2
  2.7 37.2 %shard_map.189 = (bf16[32,768,128]{2,1,0:T(8,128)(2,1)S(1)}, f32[2,512]{1,0:T(2,128)S(1)}) custom-call(f32[256,512]{1,0:T(8,128)S(1)} %bitcast.8, f32[192,512]{1,0:T(8,128)S(1)} %copy-done.2), custom_call_target="tpu_custom_call" | custom-call | tf_op jit(solution)/shard_map/pallas_call | solution.py:976
  39.8 0.0 copy-start
  39.9 2.6 %copy-done = bf16[32,768,128]{2,1,0:T(8,128)(2,1)} copy-done((bf16[32,768,128]{2,1,0:T(8,128)(2,1)}, bf16[32,768,128]{2,1,0:T(8,128)(2,1)S(1)}, u32[]{:S(2)}) %copy-start) | copy-done | bytes 6291480
  42.5 0.6 copy-done.4
  43.1 0.8 broadcast_multiply_fusion
  43.9 12.7 %shard_map.190.tab_hbm = bf16[6144,512]{1,0:T(8,128)(2,1)} custom-call(s32[6144]{0:T(1024)S(1)} %get-tuple-element.21.idx_ref, bf16[24576,128]{1,0:T(8,128)(2,1)} %bitcast.6), custom_call_target="tpu_custom_call" | custom-call | tf_op jit(solution)/shard_map/pallas_call | solution.py:1024
  56.6 81.8 %shard_map.191 = (f32[256,512]{1,0:T(8,128)}, f32[256,512]{1,0:T(8,128)}, f32[24576,128]{1,0:T(8,128)}) custom-call(f32[256,512]{1,0:T(8,128)} %bitcast.7, f32[256,512]{1,0:T(8,128)} %bitcast.10, f32[2,512]{1,0:T(2,128)} %copy-done.4, bf16[6144,512]{1,0:T(8,128)(2,1)} %shard_map.190.tab_hbm, bf16[1536,768]{1,0:T(8,128)(2,1)} %constant.127.clone.a_hbm, ...), custom_call_target="tpu_custom_call" | custom-call | tf_op jit(solution)/shard_map/pallas_call | solution.py:579
  138.4 0.0 copy-start.3
  138.4 0.0 copy-start.7
  138.4 0.0 copy-start.8
  138.4 46.0 %shard_map.192 = f32[192,512]{1,0:T(8,128)S(1)} custom-call(s32[6144]{0:T(1024)S(1)} %get-tuple-element.22.idx_ref, f32[6144,4,128]{2,1,0:T(4,128)} %bitcast.9), custom_call_target="tpu_custom_call" | custom-call | tf_op jit(solution)/shard_map/pallas_call | solution.py:752
  184.4 0.0 copy-start.6
  184.4 0.0 copy-start.5
  184.5 0.9 compare_select_fusion
  185.3 0.0 copy-done.3
  185.3 0.0 copy-done.7
  185.3 0.0 copy-done.8
  185.3 1.4 fusion.14
  186.7 0.8 copy.24
  187.5 0.8 copy.25
  188.3 0.7 copy.26
  (4 shorter events, 0.0 us)
Async XLA Ops:
  0.6 1.0 copy-start.1
  1.7 1.0 copy-start.2
  39.8 2.7 %copy-start = (bf16[32,768,128]{2,1,0:T(8,128)(2,1)}, bf16[32,768,128]{2,1,0:T(8,128)(2,1)S(1)}, u32[]{:S(2)}) copy-start(bf16[32,768,128]{2,1,0:T(8,128)(2,1)S(1)} %get-tuple-element.13) | copy-start | bytes 18874372
  42.5 0.6 copy-start.4
  138.4 47.0 %copy-start.3 = (f32[192,512]{1,0:T(8,128)S(1)}, f32[192,512]{1,0:T(8,128)}, u32[]{:S(2)}) copy-start(f32[192,512]{1,0:T(8,128)} %master_ref.1) | copy-start | bytes 1179652
  138.4 46.9 %copy-start.7 = (f32[192,512]{1,0:T(8,128)S(1)}, f32[192,512]{1,0:T(8,128)}, u32[]{:S(2)}) copy-start(f32[192,512]{1,0:T(8,128)} %param.19) | copy-start | bytes 1179652
  138.4 46.9 %copy-start.8 = (f32[192,512]{1,0:T(8,128)S(1)}, f32[192,512]{1,0:T(8,128)}, u32[]{:S(2)}) copy-start(f32[192,512]{1,0:T(8,128)} %param.18) | copy-start | bytes 1179652
  184.4 2.3 %copy-start.6 = (f32[256,512]{1,0:T(8,128)S(1)}, f32[256,512]{1,0:T(8,128)}, u32[]{:S(2)}) copy-start(f32[256,512]{1,0:T(8,128)} %get-tuple-element.14) | copy-start | bytes 1572868
  184.4 3.0 %copy-start.5 = (f32[256,512]{1,0:T(8,128)S(1)}, f32[256,512]{1,0:T(8,128)}, u32[]{:S(2)}) copy-start(f32[256,512]{1,0:T(8,128)} %get-tuple-element.15) | copy-start | bytes 1572868

commit v5 on v1

v5 whole, which is shorter than its diff:
```python
import functools
import types

import jax
import jax.numpy as jnp
import numpy as np
from jax import lax
from jax.experimental import pallas as pl
from jax.experimental.pallas import tpu as pltpu
from jax.sharding import PartitionSpec as P

C = 512
FF = 2048
KL = 31
KS = 5
STEP = 10

norm_eps = 1e-05
beta_one = 0.9
beta_two = 0.999
adam_eps = 1e-08
decay_rate = 0.05
matrix_rate = 0.05
norm_rate = 0.5

TH = 16
TW = 16
NY = 47
NX = 31
NF = 768
REACH = (KL - 1) // 2
AXES = ("batch", "rows")
f32 = jnp.float32
bf16 = jnp.bfloat16


@functools.lru_cache(None)
def tables():
    freqs = [(ky, 0) for ky in range((NY + 1) // 2)]
    freqs += [(ky, kx) for kx in range(1, (NX + 1) // 2) for ky in range(NY)]
    ky = np.array([f[0] for f in freqs], np.int64)[:, None]
    kx = np.array([f[1] for f in freqs], np.int64)[:, None]
    pad = NF - len(freqs)

    def angle(rows, cols):
        ty = (ky * rows.reshape(1, -1)) % NY
        tx = (kx * cols.reshape(1, -1)) % NX
        return 2 * np.pi * (ty / NY + tx / NX)

    def grid(rows, cols):
        r, c = np.meshgrid(rows, cols, indexing="ij")
        return r.reshape(-1), c.reshape(-1)

    def stack(re, im):
        z = np.zeros((pad, re.shape[1]))
        return np.concatenate([re, z, im, z], axis=0)

    r, c = grid(np.arange(-TH, 2 * TH), np.arange(TW))
    used = ((r + REACH >= 0) & (r + REACH < NY - 1)).astype(np.float64)[None]
    t = angle(r + REACH, c)
    a = stack(np.cos(t) * used, -np.sin(t) * used)
    i, j = grid(np.arange(KL), np.arange(KL))
    t = angle(i, j - REACH)
    b = stack(np.cos(t), -np.sin(t))
    lead = REACH - (KS - 1) // 2
    small = ((i >= lead) & (i < lead + KS) & (j >= lead) & (j < lead + KS)).nonzero()[0]
    bs = np.pad(b[:, small], ((0, 0), (0, 32 - KS * KS)))
    b = np.pad(b, ((0, 0), (0, 2 * C - KL * KL)))
    y, x = grid(np.arange(TH), np.arange(TW))
    t = angle(y, x)
    w = np.full((len(freqs), 1), 2.0)
    w[0] = 1.0
    w /= NY * NX
    ct = stack(w * np.cos(t), -w * np.sin(t))
    return tuple(m.astype(np.float32).astype(bf16) for m in (a, a.T, b, b.T, bs, bs.T, ct.T, ct))


def dot(a, b, dims=(1, 0)):
    return lax.dot_general(a, b, (((dims[0],), (dims[1],)), ((), ())), preferred_element_type=f32)


MESH = pl.DeviceIdType.MESH
WIDTHS = (2, 4, 3, 8, 8, 5, 3, 2)
BASE = 2 * C + 2 * FF + 976


def chunks(n, fn, init=()):
    return lax.fori_loop(0, n // 32, lambda i, c: fn(pl.ds(pl.multiple_of(i * 32, 32), 32), c), init)


def fold(v):
    return jnp.sum(v.reshape(v.shape[0] // 8, 8, v.shape[1]), axis=0)


def close(v):
    return jnp.sum(v, axis=0, keepdims=True)


def put(ref, start, v):
    for j in range(4):
        ref[pl.ds(start * 4 + j, v.shape[0], stride=4), :] = v[:, j * 128 : (j + 1) * 128]


def gelu_both(v):
    a = np.float32(np.sqrt(2 / np.pi))
    sq = v * v
    t = jnp.tanh(a * (v + 0.044715 * (sq * v)))
    half = 0.5 * (1 + t)
    return v * half, half + 0.5 * v * (1 - t * t) * (a * (1 + 3 * 0.044715 * sq))


def flip(b, m):
    k = 0
    while m >> k:
        if (m >> k) & 1:
            b = b + (1 - 2 * lax.rem(b // 2**k, 2)) * 2**k
        k += 1
    return b


def reduce_plan(nb):
    bits = nb.bit_length() - 1
    plan = []
    for p in range(bits):
        order = [(p + t) % bits for t in range(bits)]
        steps, kept = [], list(range(nb))
        for o in order:
            sent = [m for m in kept if (m >> o) & 1]
            kept = [m for m in kept if not (m >> o) & 1]
            steps.append((o, sent, kept))
        plan.append(steps)
    return plan


def merge_sum(v, count):
    return jnp.sum(v, axis=0)


def merge_stats(h):
    def merge(v, count):
        means = v[:, :h]
        m = jnp.sum(means, axis=0) * (1.0 / v.shape[0])
        d = means - m
        parts = [m, jnp.sum(v[:, h : 2 * h], axis=0) + count * jnp.sum(d * d, axis=0)]
        if v.shape[1] > 2 * h:
            parts.append(jnp.sum(v[:, 2 * h :], axis=0))
        return jnp.concatenate(parts, axis=0)

    return merge


def local(read, n):
    zero = jnp.zeros((8, C), f32)
    m = close(chunks(n, lambda s, c: c + fold(read(s)), zero)) * (1.0 / n)

    def sq(s, c):
        d = read(s) - m
        return c + fold(d * d)

    return m, close(chunks(n, sq, zero))


def half_cols(h):
    return pl.ds(pl.multiple_of(h * 256, 256), 256)


def up_rows(j):
    return pl.ds(pl.multiple_of(2 * C + j * C, C), C)


def down_rows(j):
    return pl.ds(pl.multiple_of(2 * C + FF + j * C, C), C)


def step_kernel(nb, nr, names, *refs):
    S = types.SimpleNamespace(**dict(zip(names, refs)))
    nz = nr // 2
    nd = nb * nr
    n = S.x.shape[0]
    own = S.master.shape[0]
    lines = 4 * own
    total = S.tab.shape[0]
    every = float(n * nd)
    b = lax.axis_index("batch")
    r = lax.axis_index("rows")
    z, c = r // 2, lax.rem(r, 2)
    sibling = (b, r + 1 - 2 * c)
    square = nb == 4
    blocks = FF // C
    zero = jnp.zeros((8, C), f32)
    rows_in = S.rows_in

    def load(i, src, dst):
        return pltpu.make_async_copy(src, dst, S.load_sem.at[i])

    ld_m, ld_x, ld_c = load(0, S.master_hbm, S.master), load(1, S.x_hbm, S.x), load(2, S.cot_hbm, S.cot)
    for copy in (ld_m, ld_x, ld_c):
        copy.start()
    barrier = pltpu.get_barrier_semaphore()
    for k in range(1, nr):
        pl.semaphore_signal(barrier, inc=1, device_id=(b, lax.rem(r + k, nr)), device_id_type=MESH)
    for m in range(1, nb):
        pl.semaphore_signal(barrier, inc=1, device_id=(flip(b, m), r), device_id_type=MESH)


    def share_stage(e, stage):
        if stage == 0:
            return getattr(S, f"one{e}"), r, nr, [(b, lax.rem(r + k, nr)) for k in range(1, nr)]
        return getattr(S, f"two{e}"), b, nb, [(flip(b, m), r) for m in range(1, nb)]

    def share_send(e, stage, v):
        buf, mine, size, peers = share_stage(e, stage)
        buf[mine] = v
        for peer in peers:
            pltpu.make_async_remote_copy(
                buf.at[mine], buf.at[mine], S.stat_send.at[e, stage], S.stat_recv.at[e, stage], device_id=peer, device_id_type=MESH
            ).start()

    def share_wait(e, stage, merge):
        buf, mine, size, peers = share_stage(e, stage)
        got = buf.at[pl.ds(0, size - 1)]
        pltpu.make_async_copy(got, got, S.stat_recv.at[e, stage]).wait()
        return merge(buf[...], float(n if stage == 0 else n * nr))

    def share(e, v, merge, work=None, more=None):
        share_send(e, 0, v)
        if work:
            work()
        v = share_wait(e, 0, merge)
        share_send(e, 1, v)
        if more:
            more()
        return share_wait(e, 1, merge)


    def place(m, zz, core):
        return flip(b, m) * nr + 2 * zz + core

    def along_z(zz, up):
        at = rows_in.at[place(0, zz, c)]
        return pltpu.make_async_remote_copy(
            at, at, S.z_send.at[zz], S.z_recv.at[zz], device_id=(b, r + 2 if up else r - 2), device_id_type=MESH
        )

    def to_peer(m, zz):
        at = rows_in.at[place(0, zz, c)]
        return pltpu.make_async_remote_copy(
            at, at, S.b_send.at[m, zz], S.b_recv.at[m, zz], device_id=(flip(b, m), r), device_id_type=MESH
        )

    def from_peer(m, zz):
        at = rows_in.at[place(m, zz, c)]
        return pltpu.make_async_copy(at, at, S.b_recv.at[m, zz])

    def half(m, zz, h, to):
        at = rows_in.at[place(m, zz, c), pl.ds(h * (lines // 2), lines // 2)]
        return pltpu.make_async_remote_copy(
            at, at, S.half_send.at[h, zz], S.half_recv.at[h, zz], device_id=(flip(b, to), r), device_id_type=MESH
        )

    def to_other_core(m, zz, core):
        at = rows_in.at[place(m, zz, core)]
        return pltpu.make_async_remote_copy(
            at, at, S.core_send.at[m, zz], S.core_recv.at[m, zz], device_id=sibling, device_id_type=MESH
        )

    def sends(zz):
        for m in range(1, nb):
            if not (square and m == 3):
                to_peer(m, zz).start()
        to_other_core(0, zz, c).start()

    def own_column(k):
        if k == 0:

            @pl.when(z < nz - 1)
            def _():
                along_z(z, True).start()

            @pl.when(z > 0)
            def _():
                along_z(z, False).start()

            sends(z)
            return

        @pl.when(z >= k)
        def _():
            along_z(z - k, True).wait_recv()

            @pl.when(z < nz - 1)
            def _():
                along_z(z - k, True).start()

            sends(z - k)

        @pl.when(z + k < nz)
        def _():
            along_z(z + k, False).wait_recv()

            @pl.when(z > 0)
            def _():
                along_z(z + k, False).start()

            sends(z + k)

    def each(k, fn):
        if k == 0:
            fn(z)
            return

        @pl.when(z >= k)
        def _():
            fn(z - k)

        @pl.when(z + k < nz)
        def _():
            fn(z + k)

    def pass_on(zz):
        for m in range(1, nb):
            if square and m == 3:
                continue
            from_peer(m, zz).wait()
            if square:
                half(m, zz, 2 - m, 3 - m).start()
            to_other_core(m, zz, c).start()

    def corner(zz):
        if square:
            for h in range(2):
                half(3, zz, h, 0).wait_recv()
            to_other_core(3, zz, c).start()

    def find(part, parts):
        tiles = total // 1024
        unit = 16
        spots = [
            lax.broadcasted_iota(jnp.int32, (8, 128), 0) * 128 + lax.broadcasted_iota(jnp.int32, (8, 128), 1) + 1024 * k
            for k in range(tiles)
        ]

        def some(g, acc):
            for u in range(unit):
                s = part * (total // parts) + g * unit + u
                p = S.idx[s]
                acc = [jnp.where(spot == p, s, a) for spot, a in zip(spots, acc)]
            return acc

        acc = [S.inv[k * 8 : k * 8 + 8, :] if part else jnp.zeros((8, 128), jnp.int32) for k in range(tiles)]
        acc = lax.fori_loop(0, total // parts // unit, some, acc)
        for k in range(tiles):
            S.inv[k * 8 : k * 8 + 8, :] = acc[k]

    def order(start, stop):
        flat = S.flat.reshape(total, 4, 128)
        unit = 32

        @pl.loop(start, stop)
        def _(t):
            @pl.loop(0, 128 // unit)
            def _(g):
                for u in range(unit):
                    S.chunk[pl.ds(pl.multiple_of((g * unit + u) * 4, 4), 4), :] = flat[S.inv_at[t, g * unit + u]]

            rows = pl.ds(pl.multiple_of(t * 128, 128), 128)
            for j in range(4):
                S.tab[rows, j * 128 : (j + 1) * 128] = S.chunk[pl.ds(j, 128, stride=4), :].astype(bf16)

    def front(ta, tb, tc):
        ld_a, ld_b, ld_t = load(3, S.a_hbm, ta), load(4, S.b_hbm, tb), load(5, S.c_hbm, tc)
        for copy in (ld_b, ld_a, ld_t):
            copy.start()
        ld_m.wait()
        for j in range(4):
            S.tmp[pl.ds(j, own, stride=4), :] = S.master[:, j * 128 : (j + 1) * 128]
        rows_in[place(0, z, c)] = S.tmp[...].astype(bf16)
        pl.semaphore_wait(barrier, nr - 1 + nb - 1)
        own_column(0)
        ld_x.wait()
        share_send(0, 0, jnp.concatenate(local(lambda s: S.x[s, :], n), axis=0))
        steps = max(nz - 1, 1)
        for k in range(1, nz):
            find(k - 1, steps)
            own_column(k)
            each(k - 1, pass_on)
            if k > 1:
                each(k - 2, corner)
            if k == 1:
                share_send(0, 1, share_wait(0, 0, merge_stats(1)))
        if nz == 1:
            find(0, 1)
            share_send(0, 1, share_wait(0, 0, merge_stats(1)))
        to_scalar = pltpu.make_async_copy(S.inv, S.inv_at, S.load_sem.at[6])
        to_scalar.start()
        each(nz - 1, pass_on)
        if nz > 1:
            each(nz - 2, corner)
        each(nz - 1, corner)
        tot = share_wait(0, 1, merge_stats(1))
        m_x, q_x = tot[0:1], tot[1:2] * (1.0 / every)
        inv_x = lax.rsqrt(q_x + norm_eps)
        to_scalar.wait()
        for m in range(nb):

            @pl.loop(0, nz)
            def _(zz):
                to_other_core(m, zz, 1 - c).wait_recv()

        @pl.loop(0, nd)
        def _(d):
            S.flat[pl.ds(pl.multiple_of(d * lines, lines), lines), :] = rows_in[d].astype(f32)

        tiles = total // 128
        late = (2 * C + 2 * FF) // 128
        order(0, 2 * C // 128)
        order(late, tiles)

        for m in range(nb):

            @pl.loop(0, nz)
            def _(zz):
                to_other_core(m, zz, c).wait_send()
                if m and not (square and m == 3):
                    to_peer(m, zz).wait_send()
                if square and m in (1, 2):
                    half(m, zz, 2 - m, 3 - m).wait_send()

        for k in range(nz):

            @pl.when((z >= k) & (z < nz - 1))
            def _():
                along_z(z - k, True).wait_send()

            @pl.when((z + k < nz) & (z > 0))
            def _():
                along_z(z + k, False).wait_send()

        small = S.tab[pl.ds(BASE, 48), :].astype(f32)
        S.small[...] = small
        row = lambda i: small[32 + i : 33 + i, :]

        def pre(s, sx):
            d = S.x[s, :] - m_x
            S.pre_low[s, :] = (d * (inv_x * row(0)) + row(1)).astype(bf16)
            return sx + fold(d)

        sum_x = close(chunks(n, pre, zero))
        S.dz[...] = dot(S.pre_low[...], S.tab[pl.ds(0, C), :])

        def act(s, a):
            u, d = gelu_both(S.dz[s, :])
            S.dz[s, :] = d
            S.wide[pl.ds(pl.multiple_of(n + s.start, 32), 32), :] = u.astype(bf16)
            return a

        chunks(n, act)
        mine = S.wide.at[pl.ds(n, n)]
        halo_up = halo(0, mine, S.wide.at[pl.ds(2 * n, n)], True)
        halo_down = halo(1, mine, S.wide.at[pl.ds(0, n)], False)
        halo_start(halo_up, halo_down)

        ld_b.wait()

        @pl.loop(0, 2 * NF // 256)
        def _(t):
            s = pl.ds(pl.multiple_of(t * 256, 256), 256)
            S.spec_l[s, :] = dot(tb[s, :], S.tab[pl.ds(2 * C + 2 * FF, 2 * C), :])
            S.spec_s[s, :] = dot(S.bs[s, :], S.tab[pl.ds(BASE, 32), :])

        halo_wait(halo_up, halo_down, S.wide.at[pl.ds(0, n)], S.wide.at[pl.ds(2 * n, n)])
        ld_a.wait()

        @pl.loop(0, 2 * NF // 256)
        def _(t):
            s = pl.ds(pl.multiple_of(t * 256, 256), 256)
            S.spec_u[s, :] = dot(ta[s, :], S.wide[...])

        @pl.loop(0, NF // 32)
        def _(i):
            re, im = pl.ds(pl.multiple_of(i * 32, 32), 32), pl.ds(pl.multiple_of(NF + i * 32, 32), 32)
            ur, ui = S.spec_u[re, :], S.spec_u[im, :]
            for k, p in ((S.spec_l, S.prod_l), (S.spec_s, S.prod_s)):
                kr, ki = k[re, :], k[im, :]
                p[re, :] = (ur * kr + ui * ki).astype(bf16)
                p[im, :] = (ui * kr - ur * ki).astype(bf16)

        ld_t.wait()
        S.d_l[...] = dot(tc[...], S.prod_l[...])
        S.d_s[...] = dot(tc[...], S.prod_s[...])
        return m_x, q_x, sum_x


    has_above, has_below = r > 0, r < nr - 1

    def halo(i, src, dst, up):
        peer = lax.rem(r + nr - 1, nr) if up else lax.rem(r + 1, nr)
        return pltpu.make_async_remote_copy(
            src, dst, S.halo_send.at[i], S.halo_recv.at[i], device_id=(b, peer), device_id_type=MESH
        )

    def halo_start(up, down):
        @pl.when(has_above)
        def _():
            up.start()

        @pl.when(has_below)
        def _():
            down.start()

    def halo_wait(up, down, above, below):
        @pl.when(has_below)
        def _():
            up.wait_recv()
            down.wait_send()

        @pl.when(has_above)
        def _():
            down.wait_recv()
            up.wait_send()

        @pl.when(jnp.logical_not(has_above))
        def _():
            above[...] = jnp.zeros((n, C), bf16)

        @pl.when(jnp.logical_not(has_below))
        def _():
            below[...] = jnp.zeros((n, C), bf16)

    m_x, q_x, sum_x = pl.run_scoped(
        front, pltpu.VMEM(S.a_hbm.shape, bf16), pltpu.VMEM(S.b_hbm.shape, bf16), pltpu.VMEM(S.c_hbm.shape, bf16)
    )
    inv_x = lax.rsqrt(q_x + norm_eps)
    small = S.small[...]
    row = lambda i: small[32 + i : 33 + i, :]
    mid_gain = lambda j: small[42 + j : 43 + j, :]
    mid_bias = lambda j: small[25 + j : 26 + j, :]
    m_l, v_l = local(lambda s: S.d_l[s, :], n)
    m_s, v_s = local(lambda s: S.d_s[s, :], n)
    ld_c.wait()

    def early():
        order(2 * C // 128, (2 * C + FF) // 128)

        def low(s, a):
            S.gy_low[s, :] = S.cot[s, :].astype(bf16)
            return a

        chunks(n, low)

    tot = share(
        1, jnp.concatenate([m_l, m_s, v_l, v_s], axis=0), merge_stats(2), early,
        lambda: order((2 * C + FF) // 128, (2 * C + 2 * FF) // 128),
    )
    m_l, m_s = tot[0:1], tot[1:2]
    inv_l, inv_s = lax.rsqrt(tot[2:3] / every + norm_eps), lax.rsqrt(tot[3:4] / every + norm_eps)

    def pair(s, a):
        hl = (S.d_l[s, :] - m_l) * inv_l
        hs = (S.d_s[s, :] - m_s) * inv_s
        S.d_l[s, :] = hl
        S.d_s[s, :] = hs
        t, d = gelu_both(hl * row(2) + row(3) + hs * row(4) + row(5))
        S.s_val[s, :] = d
        S.t_low[s, :] = t.astype(bf16)
        return a

    chunks(n, pair)
    S.p_val[...] = dot(S.t_low[...], S.tab[pl.ds(C, C), :])
    m_p = close(chunks(n, lambda s, a: a + fold(S.p_val[s, :]), zero)) * (1.0 / n)

    def proj(s, a):
        d = S.p_val[s, :] - m_p
        return a[0] + fold(d * d), a[1] + fold(d * (S.x[s, :] - m_x))

    v_p, cross = chunks(n, proj, (zero, zero))
    tot = share(2, jnp.concatenate([m_p, close(v_p), close(cross) + m_p * sum_x], axis=0), merge_stats(1))
    m_p, q_p, cov = tot[0:1], tot[1:2] / every, tot[2:3] / every
    inv_p = lax.rsqrt(q_p + norm_eps)
    slope = row(6) * inv_p
    m_f = m_x + row(7)
    q_f = jnp.maximum(q_x + 2 * slope * cov + slope * slope * q_p, 0.0)
    inv_f = lax.rsqrt(q_f + norm_eps)
    hats = inv_f * inv_p * (cov + slope * q_p)

    def ffn(s, a):
        ph = (S.p_val[s, :] - m_p) * inv_p
        S.p_val[s, :] = ph
        m = S.x[s, :] + (ph * row(6) + row(7))
        S.mid[s, :] = m
        S.c_low[s, :] = ((m - m_f) * (inv_f * row(8)) + row(9)).astype(bf16)
        g = S.cot[s, :]
        return a[0] + fold(g), a[1] + fold(g * ph)

    sum_c, sum_ch = chunks(n, ffn, (zero, zero))
    sum_c, sum_ch = close(sum_c), close(sum_ch)

    def middle(hid, gact, a_low, gh_low):
        for j in range(blocks):
            hid[j] = dot(S.c_low[...], S.tab[up_rows(j), :])
        st = [local(lambda s, j=j: hid[j, s, :], n) for j in range(blocks)]

        def back_first():
            for j in range(blocks):
                gact[j] = dot(S.gy_low[...], S.tab[down_rows(j), :], (1, 1))

        tot = share(3, jnp.concatenate([s[0] for s in st] + [s[1] for s in st], axis=0), merge_stats(blocks), back_first)
        m_h = tot[:blocks]
        inv_h = lax.rsqrt(tot[blocks:] / every + norm_eps)
        sums = []
        for j in range(blocks):
            mj, ij, gj, bj = m_h[j : j + 1], inv_h[j : j + 1], mid_gain(j), mid_bias(j)

            def hidden(s, a, j=j, mj=mj, ij=ij, gj=gj, bj=bj):
                hat = (hid[j, s, :] - mj) * ij
                hid[j, s, :] = hat
                v, d = gelu_both(hat * gj + bj)
                a_low[j, s, :] = v.astype(bf16)
                g = gact[j, s, :] * d
                gact[j, s, :] = g
                return a[0] + fold(g), a[1] + fold(g * hat)

            sums.append(tuple(close(v) for v in chunks(n, hidden, (zero, zero))))
        mid_rows = jnp.concatenate([s[0] for s in sums] + [s[1] for s in sums], axis=0)

        def down_grads():
            for j in range(blocks):
                for h in range(C // 256):
                    put(S.flat, 2 * C + FF + j * C + h * 256, dot(a_low[j, :, half_cols(h)], S.gy_low[...], (0, 0)))

        def outputs():
            S.out[...] = S.mid[...]
            for j in range(blocks):
                S.out[...] += dot(a_low[j], S.tab[down_rows(j), :])

        tot = share(4, mid_rows, merge_sum, down_grads, outputs) * (1.0 / every)
        out_copy.start()
        for j in range(blocks):
            tb_, tg_, sc = tot[j : j + 1], tot[blocks + j : blocks + j + 1], mid_gain(j) * inv_h[j : j + 1]

            def grad_h(s, a, j=j, tb_=tb_, tg_=tg_, sc=sc):
                gh_low[j, s, :] = (sc * (gact[j, s, :] - tb_ - hid[j, s, :] * tg_)).astype(bf16)
                return a

            chunks(n, grad_h)
        S.g_f[...] = dot(gh_low[0], S.tab[up_rows(0), :], (1, 1))
        for j in range(1, blocks):
            S.g_f[...] += dot(gh_low[j], S.tab[up_rows(j), :], (1, 1))

        def ffn_sums(s, a):
            g = S.g_f[s, :]
            hat = (S.mid[s, :] - m_f) * inv_f
            return a[0] + fold(g), a[1] + fold(g * hat), a[2] + fold(g * S.p_val[s, :])

        b_ffn, g_ffn, g_fp = (close(v) for v in chunks(n, ffn_sums, (zero, zero, zero)))

        def grad_up():
            for j in range(blocks):
                for h in range(C // 256):
                    put(S.flat, 2 * C + j * C + h * 256, dot(S.c_low[:, half_cols(h)], gh_low[j], (0, 0)))

        tot = share(5, jnp.concatenate([b_ffn, g_ffn, g_fp, sum_c, sum_ch], axis=0), merge_sum, grad_up) * (1.0 / every)
        return mid_rows, b_ffn, g_ffn, tot

    out_copy = pltpu.make_async_copy(S.out, S.out_hbm, S.load_sem.at[7])
    hidden_shape = (blocks, n, C)
    mid_rows, b_ffn, g_ffn, tot = pl.run_scoped(
        middle, pltpu.VMEM(hidden_shape, f32), pltpu.VMEM(hidden_shape, f32), pltpu.VMEM(hidden_shape, bf16), pltpu.VMEM(hidden_shape, bf16)
    )

    def back(tat, tbt, tct, acc):
        ld_ct, ld_at, ld_bt = load(3, S.ct_hbm, tct), load(4, S.at_hbm, tat), load(5, S.bt_hbm, tbt)
        for copy in (ld_ct, ld_at, ld_bt):
            copy.start()
        scale_f = row(8) * inv_f
        mean_hat = tot[4:5] + scale_f * (tot[2:3] - tot[1:2] * hats)

        def grad_mid(s, a):
            hat = (S.mid[s, :] - m_f) * inv_f
            g = S.cot[s, :] + scale_f * (S.g_f[s, :] - tot[0:1] - hat * tot[1:2])
            S.g_f[s, :] = g
            ph = S.p_val[s, :]
            S.gp_low[s, :] = (slope * (g - tot[3:4] - ph * mean_hat)).astype(bf16)
            return a[0] + fold(g), a[1] + fold(g * ph)

        b_proj, g_proj = (close(v) for v in chunks(n, grad_mid, (zero, zero)))
        S.p_val[...] = dot(S.gp_low[...], S.tab[pl.ds(C, C), :], (1, 1))

        def grad_s(s, a):
            g = S.p_val[s, :] * S.s_val[s, :]
            S.p_val[s, :] = g
            return a[0] + fold(g), a[1] + fold(g * S.d_l[s, :]), a[2] + fold(g * S.d_s[s, :])

        b_pair, g_lg, g_sg = (close(v) for v in chunks(n, grad_s, (zero, zero, zero)))

        def grad_out():
            for h in range(C // 256):
                put(S.flat, C + h * 256, dot(S.t_low[:, half_cols(h)], S.gp_low[...], (0, 0)))

        sums = share(6, jnp.concatenate([b_pair, g_lg, g_sg], axis=0), merge_sum, grad_out) * (1.0 / every)
        sc_l, sc_s = row(2) * inv_l, row(4) * inv_s
        gl_low, gs_low = S.t_low, S.gp_low

        def grad_pair(s, a):
            g = S.p_val[s, :] - sums[0:1]
            gl_low[s, :] = (sc_l * (g - S.d_l[s, :] * sums[1:2])).astype(bf16)
            gs_low[s, :] = (sc_s * (g - S.d_s[s, :] * sums[2:3])).astype(bf16)
            return a

        chunks(n, grad_pair)
        ld_ct.wait()

        @pl.loop(0, NF // 256)
        def _(t):
            re, im = pl.ds(pl.multiple_of(t * 256, 256), 256), pl.ds(pl.multiple_of(NF + t * 256, 256), 256)
            acc[0] = dot(tct[re, :], gl_low[...])
            acc[1] = dot(tct[im, :], gl_low[...])
            acc[2] = dot(tct[re, :], gs_low[...])
            acc[3] = dot(tct[im, :], gs_low[...])

            @pl.loop(0, 8)
            def _(i):
                s = pl.ds(pl.multiple_of(i * 32, 32), 32)
                re = pl.ds(pl.multiple_of(t * 256 + i * 32, 32), 32)
                im = pl.ds(pl.multiple_of(NF + t * 256 + i * 32, 32), 32)
                lr, li, sr, si = acc[0, s, :], acc[1, s, :], acc[2, s, :], acc[3, s, :]
                kr, ki = S.spec_l[re, :], S.spec_l[im, :]
                hr, hi = S.spec_s[re, :], S.spec_s[im, :]
                S.prod_k[re, :] = (lr * kr - li * ki + sr * hr - si * hi).astype(bf16)
                S.prod_k[im, :] = (lr * ki + li * kr + sr * hi + si * hr).astype(bf16)
                ur, ui = S.spec_u[re, :], S.spec_u[im, :]
                S.prod_l[re, :] = (lr * ur + li * ui).astype(bf16)
                S.prod_l[im, :] = (lr * ui - li * ur).astype(bf16)
                S.prod_s[re, :] = (sr * ur + si * ui).astype(bf16)
                S.prod_s[im, :] = (sr * ui - si * ur).astype(bf16)

        ld_at.wait()
        S.halo_out[0] = dot(tat[pl.ds(0, n), :], S.prod_k[...]).astype(bf16)
        S.halo_out[1] = dot(tat[pl.ds(2 * n, n), :], S.prod_k[...]).astype(bf16)
        halo_up = halo(2, S.halo_out.at[0], S.halo_in.at[1], True)
        halo_down = halo(3, S.halo_out.at[1], S.halo_in.at[0], False)
        halo_start(halo_up, halo_down)
        S.p_val[...] = dot(tat[pl.ds(n, n), :], S.prod_k[...])
        ld_bt.wait()

        @pl.loop(0, 4)
        def _(t):
            s = pl.ds(pl.multiple_of(t * 256, 256), 256)
            put(S.flat, 2 * C + 2 * FF + t * 256, dot(tbt[s, :], S.prod_l[...]))

        put(S.flat, BASE, dot(S.bst[...], S.prod_s[...]))
        halo_wait(halo_up, halo_down, S.halo_in.at[0], S.halo_in.at[1])
        gz_low = S.t_low

        def grad_z(s, a):
            g = S.p_val[s, :] + S.halo_in[0, s, :].astype(f32) + S.halo_in[1, s, :].astype(f32)
            gz_low[s, :] = (g * S.dz[s, :]).astype(bf16)
            return a

        chunks(n, grad_z)
        S.p_val[...] = dot(gz_low[...], S.tab[pl.ds(0, C), :], (1, 1))

        def pre_sums(s, a):
            g = S.p_val[s, :]
            return a[0] + fold(g), a[1] + fold(g * ((S.x[s, :] - m_x) * inv_x))

        b_pre, g_pre = (close(v) for v in chunks(n, pre_sums, (zero, zero)))
        share_send(7, 0, jnp.concatenate([b_pre, g_pre], axis=0))
        for h in range(C // 256):
            put(S.flat, h * 256, dot(S.pre_low[:, half_cols(h)], gz_low[...], (0, 0)))
        norms = [g_pre, b_pre, g_lg, b_pair, g_sg, b_pair, g_proj, b_proj, g_ffn, b_ffn]
        norms += [mid_rows[blocks + j : blocks + j + 1] for j in range(blocks)]
        put(S.flat, BASE + 32, jnp.concatenate(norms + [jnp.zeros((2, C), f32)], axis=0))
        for j in range(blocks):
            for k in range(4):
                S.flat[pl.ds((BASE + 25 + j) * 4 + k, 1), :] = mid_rows[j : j + 1, k * 128 : (k + 1) * 128]

    pl.run_scoped(
        back, pltpu.VMEM(S.at_hbm.shape, bf16), pltpu.VMEM(S.bt_hbm.shape, bf16), pltpu.VMEM(S.ct_hbm.shape, bf16), pltpu.VMEM((4, 256, C), f32)
    )


    plan = reduce_plan(nb)
    parts = len(plan)
    size = lines // parts
    unit = 32 if own % 32 == 0 else 8
    tmp = S.tmp
    hop_base = nz * nb
    z_base = hop_base + nz * (nb - 1)

    def tail(sib_out, pair, z_out):
        grad = S.flat.reshape(total, 4, 128)

        def column(i):
            return lax.rem(z + 1 + i, nz)

        def collect(m, zz, cc):
            start = (flip(b, m) * nr + 2 * zz + cc) * own

            @pl.loop(0, own // unit)
            def _(g):
                for u in range(unit):
                    tmp[pl.ds(pl.multiple_of((g * unit + u) * 4, 4), 4), :] = grad[S.idx[start + g * unit + u]]

        def to_sibling(i, m):
            return pltpu.make_async_remote_copy(
                sib_out.at[i, m], rows_in.at[i * nb + m], S.sib_send.at[i, m], S.sib_recv.at[i, m],
                device_id=sibling, device_id_type=MESH,
            )

        def rows_of(p):
            return pl.ds(p * size, size)

        def slots(p, t):
            at = sum(len(plan[p][k][2]) for k in range(t))
            return at, len(plan[p][t][2])

        def hop_at(i, p, at, count):
            return rows_in.at[pl.ds(hop_base + i * (nb - 1) + at, count), rows_of(p)]

        def hop(i, p, t, m):
            o, sent, kept = plan[p][t]
            at, _ = slots(p, t)
            landing = rows_in.at[hop_base + i * (nb - 1) + at + kept.index(m ^ (1 << o)), rows_of(p)]
            return pltpu.make_async_remote_copy(
                pair.at[i, m, rows_of(p)], landing, S.hop_send.at[i, p, t], S.hop_recv.at[i, p, t],
                device_id=(flip(b, 1 << o), r), device_id_type=MESH,
            )

        def hop_wait(i, p, t, sem):
            whole = hop_at(i, p, *slots(p, t))
            pltpu.make_async_copy(whole, whole, sem.at[i, p, t]).wait()

        def for_sibling(i):
            for m in range(nb):
                collect(m, column(i), 1 - c)
                sib_out[i, m] = tmp[...].astype(bf16)
                to_sibling(i, m).start()

        for_sibling(0)

        @pl.loop(0, nz)
        def _(i):
            @pl.when(i < nz - 1)
            def _():
                for_sibling(i + 1)

            for m in reversed(range(nb)):
                collect(m, column(i), c)
                to_sibling(i, m).wait_recv()
                pair[i, m] = (tmp[...] + rows_in[i * nb + m].astype(f32)).astype(bf16)
                for p in range(parts):
                    if m in plan[p][0][1]:
                        hop(i, p, 0, m).start()

        share_send(7, 1, share_wait(7, 0, merge_sum))

        for t in range(parts - 1):

            @pl.loop(0, nz)
            def _(i):
                for p in range(parts):
                    hop_wait(i, p, t, S.hop_recv)
                    at, _ = slots(p, t)
                    for k, m in enumerate(plan[p][t][2]):
                        pair[i, m, rows_of(p)] = (
                            pair[i, m, rows_of(p)].astype(f32)
                            + rows_in[hop_base + i * (nb - 1) + at + k, rows_of(p)].astype(f32)
                        ).astype(bf16)
                        if m in plan[p][t + 1][1]:
                            hop(i, p, t + 1, m).start()

        sums = share_wait(7, 1, merge_sum) * (1.0 / every)
        scale_x = row(0) * inv_x

        def last(s, a):
            hat = (S.x[s, :] - m_x) * inv_x
            S.g_f[s, :] = S.g_f[s, :] + scale_x * (S.p_val[s, :] - sums[0:1] - hat * sums[1:2])
            return a

        chunks(n, last)
        gin_copy = pltpu.make_async_copy(S.g_f, S.gin_hbm, S.load_sem.at[6])
        gin_copy.start()
        for i in range(own):
            p = S.idx[(b * nr + r) * own + i]
            fast = (p >= 2 * C + 2 * FF + KL * KL) & ((p < BASE) | (p >= BASE + KS * KS))
            S.rate[pl.ds(i, 1), :] = jnp.full((1, 128), jnp.where(fast, np.float32(norm_rate), np.float32(matrix_rate)), f32)

        def to_owner(i):
            return pltpu.make_async_remote_copy(
                z_out.at[i], rows_in.at[z_base + i], S.own_send.at[i], S.own_recv.at[i],
                device_id=(b, 2 * column(i) + c), device_id_type=MESH,
            )

        @pl.loop(0, nz)
        def _(i):
            for p in range(parts):
                hop_wait(i, p, parts - 1, S.hop_recv)
                at, _ = slots(p, parts - 1)
                tmp[rows_of(p), :] = pair[i, 0, rows_of(p)].astype(f32) + rows_in[hop_base + i * (nb - 1) + at, rows_of(p)].astype(f32)

            @pl.when(i < nz - 1)
            def _():
                z_out[i] = tmp[...].astype(bf16)
                to_owner(i).start()

        for i in range(nz - 1):
            to_owner(i).wait_recv()
            tmp[...] += rows_in[z_base + i].astype(f32)
        for j in range(4):
            S.red[:, j * 128 : (j + 1) * 128] = tmp[pl.ds(j, own, stride=4), :]

        @pl.loop(0, nz)
        def _(i):
            for m in range(nb):
                to_sibling(i, m).wait_send()
            for p in range(parts):
                for t in range(parts):
                    hop_wait(i, p, t, S.hop_send)

        for i in range(nz - 1):
            to_owner(i).wait_send()
        gin_copy.wait()

    low_block = lambda *lead: pltpu.VMEM(lead + (lines, 128), bf16)
    pl.run_scoped(tail, low_block(nz, nb), low_block(nz, nb), low_block(nz))
    for e in range(len(WIDTHS)):
        for stage in range(2):
            buf, mine, count, peers = share_stage(e, stage)
            sent = buf.at[pl.ds(0, count - 1)]
            pltpu.make_async_copy(sent, sent, S.stat_send.at[e, stage]).wait()
    out_copy.wait()


def step(x, cot, master, places, nb, nr):
    (a, at, b, bt, bs, bst, c, ct) = tables()
    n, own, nz, parts = x.shape[0], master.shape[0], nr // 2, nb.bit_length() - 1
    total = places.shape[0]
    vm = lambda *shape: pltpu.VMEM(shape, f32)
    low = lambda *shape: pltpu.VMEM(shape, bf16)
    dma = lambda *shape: pltpu.SemaphoreType.DMA(shape)
    vmem, anywhere = pl.BlockSpec(memory_space=pltpu.VMEM), pl.BlockSpec(memory_space=pl.ANY)
    ins = dict(
        idx=(places, pl.BlockSpec(memory_space=pltpu.SMEM)), x_hbm=(x, anywhere), cot_hbm=(cot, anywhere), master_hbm=(master, anywhere),
        a_hbm=(a, anywhere), at_hbm=(at, anywhere), b_hbm=(b, anywhere), bt_hbm=(bt, anywhere), bs=(bs, vmem), bst=(bst, vmem),
        c_hbm=(c, anywhere), ct_hbm=(ct, anywhere),
    )
    image = jax.ShapeDtypeStruct((n, C), f32)
    outs = dict(
        out_hbm=(image, anywhere), gin_hbm=(image, anywhere), red=(jax.ShapeDtypeStruct((own, C), f32), vmem),
        rate=(jax.ShapeDtypeStruct((own, 128), f32), vmem),
    )
    scratch = dict(
        rows_in=low(nb * nr, 4 * own, 128), flat=vm(4 * total, 128), tab=low(total, C), x=vm(n, C), cot=vm(n, C), master=vm(own, C),
        tmp=vm(4 * own, 128), chunk=vm(512, 128), inv=pltpu.VMEM((total // 128, 128), jnp.int32),
        inv_at=pltpu.SMEM((total // 128, 128), jnp.int32), small=vm(48, C),
        pre_low=low(n, C), wide=low(3 * n, C), dz=vm(n, C), spec_u=vm(2 * NF, C), spec_l=vm(2 * NF, C), spec_s=vm(2 * NF, C),
        prod_l=low(2 * NF, C), prod_s=low(2 * NF, C), prod_k=low(2 * NF, C), d_l=vm(n, C), d_s=vm(n, C), s_val=vm(n, C),
        t_low=low(n, C), p_val=vm(n, C), mid=vm(n, C), c_low=low(n, C), gy_low=low(n, C), gp_low=low(n, C), g_f=vm(n, C), out=vm(n, C),
        halo_out=low(2, n, C), halo_in=low(2, n, C),
    )
    for e, w in enumerate(WIDTHS):
        scratch[f"one{e}"] = vm(nr, w, C)
        scratch[f"two{e}"] = vm(nb, w, C)
    scratch.update(
        load_sem=dma(8), stat_send=dma(len(WIDTHS), 2), stat_recv=dma(len(WIDTHS), 2), halo_send=dma(4), halo_recv=dma(4),
        z_send=dma(nz), z_recv=dma(nz), b_send=dma(nb, nz), b_recv=dma(nb, nz), half_send=dma(2, nz), half_recv=dma(2, nz),
        core_send=dma(nb, nz), core_recv=dma(nb, nz), sib_send=dma(nz, nb), sib_recv=dma(nz, nb),
        hop_send=dma(nz, parts, parts), hop_recv=dma(nz, parts, parts), own_send=dma(nz), own_recv=dma(nz),
    )
    return pl.pallas_call(
        functools.partial(step_kernel, nb, nr, [*ins, *outs, *scratch]),
        out_shape=[v[0] for v in outs.values()],
        in_specs=[v[1] for v in ins.values()],
        out_specs=[v[1] for v in outs.values()],
        scratch_shapes=list(scratch.values()),
        compiler_params=pltpu.CompilerParams(collective_id=0, has_side_effects=True, vmem_limit_bytes=62 * 2**20),
    )(*[v[0] for v in ins.values()])


def finish_kernel(
    red_ref, rate_ref, first_hbm, second_hbm, master_hbm, out_hbm, gin_hbm,
    result_hbm, grad_hbm, slots_ref, new_first_ref, new_second_ref, new_master_ref, new_copy_ref,
    first_ref, second_ref, master_ref, out_ref, gin_ref, sem,
):
    ends = ((first_hbm, first_ref), (second_hbm, second_ref), (master_hbm, master_ref), (out_hbm, out_ref), (gin_hbm, gin_ref))
    loads = [pltpu.make_async_copy(src, dst, sem.at[2 + i]) for i, (src, dst) in enumerate(ends)]
    for copy in loads:
        copy.start()
    through = [pltpu.make_async_copy(out_ref, result_hbm, sem.at[0]), pltpu.make_async_copy(gin_ref, grad_hbm, sem.at[1])]
    for copy in loads:
        copy.wait()
    for copy in through:
        copy.start()
    own = red_ref.shape[0]
    size = 32 if own % 32 == 0 else 8
    for s in range(0, own, size):
        s = pl.ds(s, size)
        for j in range(C // 128):
            at = (s, pl.ds(j * 128, 128))
            g = red_ref[at]
            first = beta_one * first_ref[at] + (1.0 - beta_one) * g
            second = beta_two * second_ref[at] + (1.0 - beta_two) * g * g
            slots_ref[at] = g
            new_first_ref[at] = first
            new_second_ref[at] = second
            first_hat = first / (1.0 - beta_one**STEP)
            second_hat = second / (1.0 - beta_two**STEP)
            master = master_ref[at]
            new = master - rate_ref[s, :] * (first_hat / (jnp.sqrt(second_hat) + adam_eps) + decay_rate * master)
            new_master_ref[at] = new
            new_copy_ref[at] = new.astype(bf16)
    for copy in through:
        copy.wait()


def finish(reduced, first, second, master, rates, out, gin):
    vmem, anywhere = pl.BlockSpec(memory_space=pltpu.VMEM), pl.BlockSpec(memory_space=pl.ANY)
    slot = jax.ShapeDtypeStruct(reduced.shape, f32)
    image = jax.ShapeDtypeStruct(out.shape, f32)
    return pl.pallas_call(
        finish_kernel,
        out_shape=[image, image, slot, slot, slot, slot, jax.ShapeDtypeStruct(reduced.shape, bf16)],
        in_specs=[vmem] * 2 + [anywhere] * 5,
        out_specs=[anywhere] * 2 + [vmem] * 5,
        scratch_shapes=[pltpu.VMEM(reduced.shape, f32)] * 3 + [pltpu.VMEM(out.shape, f32)] * 2 + [pltpu.SemaphoreType.DMA((7,))],
        compiler_params=pltpu.CompilerParams(vmem_limit_bytes=62 * 2**20),
    )(reduced, rates, first, second, master, out, gin)


def table_place(t):
    start = 2 * C + 2 * FF
    k_end = start + KL * KL
    s_end = k_end + KS * KS
    m_gain = s_end + 10
    m_bias = m_gain + FF // C
    m_end = m_bias + FF // C
    up = t - 2 * C
    up = 2 * C + up % (FF // C) * C + up // (FF // C)
    base = start + 976
    unused = t - m_end
    unused = jnp.where(unused < 15, k_end + unused, jnp.where(unused < 18, base + 29 + unused - 15, base + 46 + unused - 18))
    p = jnp.where((t >= 2 * C) & (t < 2 * C + FF), up, t)
    p = jnp.where(t >= k_end, t - k_end + base, p)
    p = jnp.where(t >= s_end, t - s_end + base + 32, p)
    p = jnp.where(t >= m_bias, t - m_bias + base + 25, p)
    return jnp.where(t >= m_end, unused, p)


def body(image_in, cotangent, slot_rows, master, first_moment, second_moment):
    n = image_in.shape[0] * image_in.shape[1] * image_in.shape[2]
    nb, nr = lax.axis_size("batch"), lax.axis_size("rows")
    out, grad_in, reduced, rates = step(
        image_in.reshape(n, C), cotangent.reshape(n, C), master, table_place(slot_rows), nb, nr
    )
    result, grad_x, *slots = finish(reduced, first_moment, second_moment, master, rates, out, grad_in)
    return (result.reshape(image_in.shape), grad_x.reshape(image_in.shape), *slots)


def solution(mesh):
    image = P("batch", "rows", None, None)
    owner = P(AXES, None)
    return jax.shard_map(
        body,
        mesh=mesh,
        in_specs=(image, image, P(), owner, owner, owner),
        out_specs=(image, image, owner, owner, owner, owner, owner),
        check_vma=False,
    )
```

time: 749 us -> 169 us (0.23)
  blocking collectives: 328 us -> 0 us
  Pallas kernels: 0 us -> 165 us
  waiting for transfers between devices: 134 us -> 0 us
  local copies, waits for them, and re-layouts: 132 us -> 0 us
  matrix products: 76.7 us -> 0 us
  other arithmetic: 44.3 us -> 1.39 us
  between operations: 16.2 us -> 0.8 us
  starting transfers between devices: 9.62 us -> 0 us
    all_gather x8 -> x0, blocking collectives: 328 us -> none  [exchange(): return lax.all_gather(jnp.stack(rows), AXES, axis=0)]
    pallas_call x0 -> x2, Pallas kernels: none -> 165 us  [the longest x1 160 us: step(): pl.pallas_call(functools.partial(step_kernel, nb, nr, [*ins, *outs, *scra...]
    reduce_scatter x1 -> x0, waiting for transfers between devices: 108 us -> none  [body(): lax.psum_scatter(slot_grads, AXES, scatter_dimension=0, tiled=True)]
    dot_general x43 -> x0, matrix products: 76.7 us -> none  [dot(): lax.dot_general(a, b, (((dims[0],), (dims[1],)), ((), ())), preferred_ele...]
    concatenate x1 -> x0, local copies, waits for them, and re-layouts: 34.8 us -> none  [body(): jnp.concatenate([g_in, g_out, g_up.reshape(FF, C), g_down, g_k_l, g_k_s,...]
    gather x1 -> x0, local copies, waits for them, and re-layouts: 31.2 us -> none  [body(): slot_grads = grads[slot_rows]]
    scatter x1 -> x0, local copies, waits for them, and re-layouts: 31.1 us -> none  [body(): ordered = jnp.zeros_like(gathered).at[slot_rows].set(gathered)]
    all_gather x1 -> x0, waiting for transfers between devices: 25.7 us -> none  [body(): gathered = lax.all_gather(own_copy, AXES, axis=0, tiled=True)]
  transfers between devices with their start and end apart: 6 -> 0, of which waited for: 2 -> 0; matrix products, arithmetic and copies ran while one was open for 7% -> 0% of each run, Pallas kernels for 0% -> 0%
where the time goes in v5:
time: 169 us; the launch traced here: 167 us
  Pallas kernels  165 us (98%)
    pallas_call x1, Pallas kernels, step(): pl.pallas_call(functools.partial(step_kernel, nb, nr, [*ins, *outs, *scra...  160 us
    pallas_call x1, Pallas kernels, finish(): pl.pallas_call(finish_kernel, out_shape=[image, image, slot, slot, slot,...  4.79 us

profile of v5, /device:TPU:0, one launch (start us, length us, event | category | flops | bytes accessed | tf_op | source)
XLA Modules:
  0.0 167.3 jit_solution(17577915429336437555)
XLA Ops:
  0.6 1.4 fusion.1.refs_0_
  2.0 160.3 %shard_map.189 = (f32[256,512]{1,0:T(8,128)}, f32[256,512]{1,0:T(8,128)}, f32[192,512]{1,0:T(8,128)}, f32[192,128]{1,0:T(8,128)}) custom-call(s32[6144]{0:T(1024)} %fusion.1.refs_0_, f32[256,512]{1,0:T(8,128)} %bitcast.4, f32[256,512]{1,0:T(8,128)} %bitcast.5, f32[192,512]{1,0:T(8,128)} %master_hbm.1, bf16[1536,768]{1,0:T(8,128)(2,1)} %constant.89.clone.refs_4_, ...), custom_call_target="tpu_custom_call" | custom-call | tf_op jit(solution)/shard_map/pallas_call | solution.py:971
  162.3 4.8 %shard_map.190 = (f32[256,512]{1,0:T(8,128)}, f32[256,512]{1,0:T(8,128)}, f32[192,512]{1,0:T(8,128)}, f32[192,512]{1,0:T(8,128)}, f32[192,512]{1,0:T(8,128)}, /*...) custom-call(f32[192,512]{1,0:T(8,128)} %get-tuple-element.18.red_ref, f32[192,128]{1,0:T(8,128)} %get-tuple-element.19.rate_ref, ...), custom_call_target="tpu_custom_call" | custom-call | tf_op jit(solution)/shard_map/pallas_call | solution.py:1021

commit v6 on v5

--- a/solution.py
+++ b/solution.py
@@ -264,11 +264,16 @@
             at, at, S.core_send.at[m, zz], S.core_recv.at[m, zz], device_id=sibling, device_id_type=MESH
         )
 
+    def cast(m, zz, core):
+        d = place(m, zz, core)
+        S.flat[pl.ds(pl.multiple_of(d * lines, lines), lines), :] = rows_in[d].astype(f32)
+
     def sends(zz):
         for m in range(1, nb):
             if not (square and m == 3):
                 to_peer(m, zz).start()
         to_other_core(0, zz, c).start()
+        cast(0, zz, c)
 
     def own_column(k):
         if k == 0:
@@ -325,12 +330,19 @@
             if square:
                 half(m, zz, 2 - m, 3 - m).start()
             to_other_core(m, zz, c).start()
+            cast(m, zz, c)
 
     def corner(zz):
         if square:
             for h in range(2):
                 half(3, zz, h, 0).wait_recv()
             to_other_core(3, zz, c).start()
+            cast(3, zz, c)
+
+    def other_core(zz):
+        for m in range(nb):
+            to_other_core(m, zz, 1 - c).wait_recv()
+            cast(m, zz, 1 - c)
 
     def find(part, parts):
         tiles = total // 1024
@@ -354,14 +366,11 @@
 
     def order(start, stop):
         flat = S.flat.reshape(total, 4, 128)
-        unit = 32
 
         @pl.loop(start, stop)
         def _(t):
-            @pl.loop(0, 128 // unit)
-            def _(g):
-                for u in range(unit):
-                    S.chunk[pl.ds(pl.multiple_of((g * unit + u) * 4, 4), 4), :] = flat[S.inv_at[t, g * unit + u]]
+            for u in range(128):
+                S.chunk[4 * u : 4 * u + 4, :] = flat[S.inv_at[t, u]]
 
             rows = pl.ds(pl.multiple_of(t * 128, 128), 128)
             for j in range(4):
@@ -386,6 +395,8 @@
             each(k - 1, pass_on)
             if k > 1:
                 each(k - 2, corner)
+            if k > 2:
+                each(k - 3, other_core)
             if k == 1:
                 share_send(0, 1, share_wait(0, 0, merge_stats(1)))
         if nz == 1:
@@ -397,20 +408,12 @@
         if nz > 1:
             each(nz - 2, corner)
         each(nz - 1, corner)
+        for k in range(max(nz - 3, 0), nz):
+            each(k, other_core)
         tot = share_wait(0, 1, merge_stats(1))
         m_x, q_x = tot[0:1], tot[1:2] * (1.0 / every)
         inv_x = lax.rsqrt(q_x + norm_eps)
         to_scalar.wait()
-        for m in range(nb):
-
-            @pl.loop(0, nz)
-            def _(zz):
-                to_other_core(m, zz, 1 - c).wait_recv()
-
-        @pl.loop(0, nd)
-        def _(d):
-            S.flat[pl.ds(pl.multiple_of(d * lines, lines), lines), :] = rows_in[d].astype(f32)
-
         tiles = total // 128
         late = (2 * C + 2 * FF) // 128
         order(0, 2 * C // 128)
@@ -783,7 +786,7 @@
     plan = reduce_plan(nb)
     parts = len(plan)
     size = lines // parts
-    unit = 32 if own % 32 == 0 else 8
+    unit = 96 if own % 96 == 0 else 8
     tmp = S.tmp
     hop_base = nz * nb
     z_base = hop_base + nz * (nb - 1)
@@ -837,10 +840,13 @@
                 sib_out[i, m] = tmp[...].astype(bf16)
                 to_sibling(i, m).start()
 
-        for_sibling(0)
-
-        @pl.loop(0, nz)
-        def _(i):
+        def to_owner(i):
+            return pltpu.make_async_remote_copy(
+                z_out.at[i], rows_in.at[z_base + i], S.own_send.at[i], S.own_recv.at[i],
+                device_id=(b, 2 * column(i) + c), device_id_type=MESH,
+            )
+
+        def first_step(i):
             @pl.when(i < nz - 1)
             def _():
                 for_sibling(i + 1)
@@ -853,47 +859,19 @@
                     if m in plan[p][0][1]:
                         hop(i, p, 0, m).start()
 
-        share_send(7, 1, share_wait(7, 0, merge_sum))
-
-        for t in range(parts - 1):
-
-            @pl.loop(0, nz)
-            def _(i):
-                for p in range(parts):
-                    hop_wait(i, p, t, S.hop_recv)
-                    at, _ = slots(p, t)
-                    for k, m in enumerate(plan[p][t][2]):
-                        pair[i, m, rows_of(p)] = (
-                            pair[i, m, rows_of(p)].astype(f32)
-                            + rows_in[hop_base + i * (nb - 1) + at + k, rows_of(p)].astype(f32)
-                        ).astype(bf16)
-                        if m in plan[p][t + 1][1]:
-                            hop(i, p, t + 1, m).start()
-
-        sums = share_wait(7, 1, merge_sum) * (1.0 / every)
-        scale_x = row(0) * inv_x
-
-        def last(s, a):
-            hat = (S.x[s, :] - m_x) * inv_x
-            S.g_f[s, :] = S.g_f[s, :] + scale_x * (S.p_val[s, :] - sums[0:1] - hat * sums[1:2])
-            return a
-
-        chunks(n, last)
-        gin_copy = pltpu.make_async_copy(S.g_f, S.gin_hbm, S.load_sem.at[6])
-        gin_copy.start()
-        for i in range(own):
-            p = S.idx[(b * nr + r) * own + i]
-            fast = (p >= 2 * C + 2 * FF + KL * KL) & ((p < BASE) | (p >= BASE + KS * KS))
-            S.rate[pl.ds(i, 1), :] = jnp.full((1, 128), jnp.where(fast, np.float32(norm_rate), np.float32(matrix_rate)), f32)
-
-        def to_owner(i):
-            return pltpu.make_async_remote_copy(
-                z_out.at[i], rows_in.at[z_base + i], S.own_send.at[i], S.own_recv.at[i],
-                device_id=(b, 2 * column(i) + c), device_id_type=MESH,
-            )
-
-        @pl.loop(0, nz)
-        def _(i):
+        def next_step(i, t):
+            for p in range(parts):
+                hop_wait(i, p, t, S.hop_recv)
+                at, _ = slots(p, t)
+                for k, m in enumerate(plan[p][t][2]):
+                    pair[i, m, rows_of(p)] = (
+                        pair[i, m, rows_of(p)].astype(f32)
+                        + rows_in[hop_base + i * (nb - 1) + at + k, rows_of(p)].astype(f32)
+                    ).astype(bf16)
+                    if m in plan[p][t + 1][1]:
+                        hop(i, p, t + 1, m).start()
+
+        def last_step(i):
             for p in range(parts):
                 hop_wait(i, p, parts - 1, S.hop_recv)
                 at, _ = slots(p, parts - 1)
@@ -903,6 +881,49 @@
             def _():
                 z_out[i] = tmp[...].astype(bf16)
                 to_owner(i).start()
+
+        def grad_image():
+            sums = share_wait(7, 1, merge_sum) * (1.0 / every)
+            scale_x = row(0) * inv_x
+
+            def last(s, a):
+                hat = (S.x[s, :] - m_x) * inv_x
+                S.g_f[s, :] = S.g_f[s, :] + scale_x * (S.p_val[s, :] - sums[0:1] - hat * sums[1:2])
+                return a
+
+            chunks(n, last)
+            gin_copy.start()
+            for i in range(own):
+                p = S.idx[(b * nr + r) * own + i]
+                fast = (p >= 2 * C + 2 * FF + KL * KL) & ((p < BASE) | (p >= BASE + KS * KS))
+                S.rate[pl.ds(i, 1), :] = jnp.full((1, 128), jnp.where(fast, np.float32(norm_rate), np.float32(matrix_rate)), f32)
+
+        gin_copy = pltpu.make_async_copy(S.g_f, S.gin_hbm, S.load_sem.at[6])
+        for_sibling(0)
+
+        @pl.loop(0, nz + parts)
+        def _(q):
+            @pl.when(q < nz)
+            def _():
+                first_step(q)
+
+            @pl.when(q == 0)
+            def _():
+                share_send(7, 1, share_wait(7, 0, merge_sum))
+
+            for t in range(parts - 1):
+
+                @pl.when((q >= t + 1) & (q < nz + t + 1))
+                def _():
+                    next_step(q - t - 1, t)
+
+            @pl.when(q == 1)
+            def _():
+                grad_image()
+
+            @pl.when(q >= parts)
+            def _():
+                last_step(q - parts)
 
         for i in range(nz - 1):
             to_owner(i).wait_recv()
@@ -978,54 +999,64 @@
     )(*[v[0] for v in ins.values()])
 
 
-def finish_kernel(
-    red_ref, rate_ref, first_hbm, second_hbm, master_hbm, out_hbm, gin_hbm,
-    result_hbm, grad_hbm, slots_ref, new_first_ref, new_second_ref, new_master_ref, new_copy_ref,
-    first_ref, second_ref, master_ref, out_ref, gin_ref, sem,
-):
-    ends = ((first_hbm, first_ref), (second_hbm, second_ref), (master_hbm, master_ref), (out_hbm, out_ref), (gin_hbm, gin_ref))
-    loads = [pltpu.make_async_copy(src, dst, sem.at[2 + i]) for i, (src, dst) in enumerate(ends)]
+def finish_kernel(*refs):
+    ins, outs, bufs, (load_sem, store_sem) = refs[:7], refs[7:14], refs[14:25], refs[25:]
+    red, rate, first_ref, second_ref, master_ref, out, gin = bufs[:7]
+    new_first, new_second, new_master, new_copy = bufs[7:11]
+    loads = [pltpu.make_async_copy(src, dst, load_sem.at[i]) for i, (src, dst) in enumerate(zip(ins, bufs[:7]))]
     for copy in loads:
         copy.start()
-    through = [pltpu.make_async_copy(out_ref, result_hbm, sem.at[0]), pltpu.make_async_copy(gin_ref, grad_hbm, sem.at[1])]
-    for copy in loads:
+    own = red.shape[0]
+    size = 64 if own % 64 == 0 else own
+    for copy in loads[:5]:
         copy.wait()
-    for copy in through:
-        copy.start()
-    own = red_ref.shape[0]
-    size = 32 if own % 32 == 0 else 8
-    for s in range(0, own, size):
-        s = pl.ds(s, size)
-        for j in range(C // 128):
-            at = (s, pl.ds(j * 128, 128))
-            g = red_ref[at]
-            first = beta_one * first_ref[at] + (1.0 - beta_one) * g
-            second = beta_two * second_ref[at] + (1.0 - beta_two) * g * g
-            slots_ref[at] = g
-            new_first_ref[at] = first
-            new_second_ref[at] = second
-            first_hat = first / (1.0 - beta_one**STEP)
-            second_hat = second / (1.0 - beta_two**STEP)
-            master = master_ref[at]
-            new = master - rate_ref[s, :] * (first_hat / (jnp.sqrt(second_hat) + adam_eps) + decay_rate * master)
-            new_master_ref[at] = new
-            new_copy_ref[at] = new.astype(bf16)
-    for copy in through:
+    stores = [pltpu.make_async_copy(red, outs[2], store_sem.at[2, 0])]
+    stores[0].start()
+    for part in range(own // size):
+        for k in range(0, size, 8):
+            s = slice(part * size + k, part * size + k + 8)
+            for j in range(C // 128):
+                at = (s, slice(j * 128, (j + 1) * 128))
+                g = red[at]
+                first = beta_one * first_ref[at] + (1.0 - beta_one) * g
+                second = beta_two * second_ref[at] + (1.0 - beta_two) * g * g
+                new_first[at] = first
+                new_second[at] = second
+                first_hat = first / (1.0 - beta_one**STEP)
+                second_hat = second / (1.0 - beta_two**STEP)
+                master = master_ref[at]
+                new_master[at] = master - rate[s, :] * (first_hat / (jnp.sqrt(second_hat) + adam_eps) + decay_rate * master)
+        s = pl.ds(part * size, size)
+        new_copy[s, :] = new_master[s, :].astype(bf16)
+        if part == 0:
+            for i in (5, 6):
+                loads[i].wait()
+                stores.append(pltpu.make_async_copy(bufs[i], outs[i - 5], store_sem.at[i - 5, 0]))
+                stores[-1].start()
+        for i, buf in enumerate((new_first, new_second, new_master, new_copy)):
+            stores.append(pltpu.make_async_copy(buf.at[s], outs[3 + i].at[s], store_sem.at[3 + i, part]))
+            stores[-1].start()
+    for copy in stores:
         copy.wait()
 
 
 def finish(reduced, first, second, master, rates, out, gin):
-    vmem, anywhere = pl.BlockSpec(memory_space=pltpu.VMEM), pl.BlockSpec(memory_space=pl.ANY)
+    anywhere = pl.BlockSpec(memory_space=pl.ANY)
     slot = jax.ShapeDtypeStruct(reduced.shape, f32)
     image = jax.ShapeDtypeStruct(out.shape, f32)
+    low = jax.ShapeDtypeStruct(reduced.shape, bf16)
+    ins = (reduced, rates, first, second, master, out, gin)
+    outs = [image, image, slot, slot, slot, slot, low]
     return pl.pallas_call(
         finish_kernel,
-        out_shape=[image, image, slot, slot, slot, slot, jax.ShapeDtypeStruct(reduced.shape, bf16)],
-        in_specs=[vmem] * 2 + [anywhere] * 5,
-        out_specs=[anywhere] * 2 + [vmem] * 5,
-        scratch_shapes=[pltpu.VMEM(reduced.shape, f32)] * 3 + [pltpu.VMEM(out.shape, f32)] * 2 + [pltpu.SemaphoreType.DMA((7,))],
+        out_shape=outs,
+        in_specs=[anywhere] * 7,
+        out_specs=[anywhere] * 7,
+        scratch_shapes=[pltpu.VMEM(v.shape, f32) for v in ins]
+        + [pltpu.VMEM(v.shape, v.dtype) for v in (slot, slot, slot, low)]
+        + [pltpu.SemaphoreType.DMA((7,)), pltpu.SemaphoreType.DMA((7, 4))],
         compiler_params=pltpu.CompilerParams(vmem_limit_bytes=62 * 2**20),
-    )(reduced, rates, first, second, master, out, gin)
+    )(*ins)
 
 
 def table_place(t):

time: 169 us -> 155 us (0.917)
  Pallas kernels: 165 us -> 153 us
    pallas_call x1, Pallas kernels: 160 us -> 149 us  [step(): pl.pallas_call(functools.partial(step_kernel, nb, nr, [*ins, *outs, *scra...]
where the time goes in v6:
time: 155 us
  Pallas kernels  153 us (99%)
    pallas_call x1, Pallas kernels, step(): pl.pallas_call(functools.partial(step_kernel, nb, nr, [*ins, *outs, *scra...  149 us
    pallas_call x1, Pallas kernels, finish(): pl.pallas_call(finish_kernel, out_shape=outs, in_specs=[anywhere] * 7, ou...  3.28 us

profile of v6, /device:TPU:0, one launch (start us, length us, event | category | flops | bytes accessed | tf_op | source)
XLA Modules:
  0.0 154.8 jit_solution(1153296650075105101)
XLA Ops:
  0.6 1.4 fusion.1.refs_0_
  2.0 149.3 %shard_map.189 = (f32[256,512]{1,0:T(8,128)}, f32[256,512]{1,0:T(8,128)}, f32[192,512]{1,0:T(8,128)}, f32[192,128]{1,0:T(8,128)}) custom-call(s32[6144]{0:T(1024)} %fusion.1.refs_0_, f32[256,512]{1,0:T(8,128)} %bitcast.4, f32[256,512]{1,0:T(8,128)} %bitcast.5, f32[192,512]{1,0:T(8,128)} %refs_4_.2, bf16[1536,768]{1,0:T(8,128)(2,1)} %constant.89.clone.refs_4_, ...), custom_call_target="tpu_custom_call" | custom-call | tf_op jit(solution)/shard_map/pallas_call | solution.py:992
  151.3 3.3 %shard_map.190 = (f32[256,512]{1,0:T(8,128)}, f32[256,512]{1,0:T(8,128)}, f32[192,512]{1,0:T(8,128)}, f32[192,512]{1,0:T(8,128)}, f32[192,512]{1,0:T(8,128)}, /*...) custom-call(f32[192,512]{1,0:T(8,128)} %get-tuple-element.18.refs_0_, f32[192,128]{1,0:T(8,128)} %get-tuple-element.19.refs_1_, ...), custom_call_target="tpu_custom_call" | custom-call | tf_op jit(solution)/shard_map/pallas_call | solution.py:1050

commit v7 on v6

--- a/solution.py
+++ b/solution.py
@@ -81,6 +81,7 @@
 
 MESH = pl.DeviceIdType.MESH
 WIDTHS = (2, 4, 3, 8, 8, 5, 3, 2)
+BY_CHIP = (1, 2, 5, 6)
 BASE = 2 * C + 2 * FF + 976
 
 
@@ -132,6 +133,10 @@
     return plan
 
 
+def by_chip(e, chips):
+    return e in BY_CHIP and chips <= 32
+
+
 def merge_sum(v, count):
     return jnp.sum(v, axis=0)
 
@@ -170,6 +175,25 @@
 
 def down_rows(j):
     return pl.ds(pl.multiple_of(2 * C + FF + j * C, C), C)
+
+
+def table_place(t):
+    start = 2 * C + 2 * FF
+    k_end = start + KL * KL
+    s_end = k_end + KS * KS
+    m_gain = s_end + 10
+    m_bias = m_gain + FF // C
+    m_end = m_bias + FF // C
+    up = t - 2 * C
+    up = 2 * C + (up & (FF // C - 1)) * C + (up >> ((FF // C).bit_length() - 1))
+    base = start + 976
+    unused = t - m_end
+    unused = jnp.where(unused < 15, k_end + unused, jnp.where(unused < 18, base + 29 + unused - 15, base + 46 + unused - 18))
+    p = jnp.where((t >= 2 * C) & (t < 2 * C + FF), up, t)
+    p = jnp.where(t >= k_end, t - k_end + base, p)
+    p = jnp.where(t >= s_end, t - s_end + base + 32, p)
+    p = jnp.where(t >= m_bias, t - m_bias + base + 25, p)
+    return jnp.where(t >= m_end, unused, p)
 
 
 def step_kernel(nb, nr, names, *refs):
@@ -194,7 +218,8 @@
         return pltpu.make_async_copy(src, dst, S.load_sem.at[i])
 
     ld_m, ld_x, ld_c = load(0, S.master_hbm, S.master), load(1, S.x_hbm, S.x), load(2, S.cot_hbm, S.cot)
-    for copy in (ld_m, ld_x, ld_c):
+    ld_s = load(8, S.slots_hbm, S.at_v)
+    for copy in (ld_s, ld_m, ld_x, ld_c):
         copy.start()
     barrier = pltpu.get_barrier_semaphore()
     for k in range(1, nr):
@@ -202,32 +227,56 @@
     for m in range(1, nb):
         pl.semaphore_signal(barrier, inc=1, device_id=(flip(b, m), r), device_id_type=MESH)
 
+    @pl.loop(0, (nb - 1) * (nz - 1))
+    def _(k):
+        at = (lax.rem(b + 1 + k // (nz - 1), nb), 2 * lax.rem(z + 1 + lax.rem(k, nz - 1), nz) + c)
+        pl.semaphore_signal(barrier, inc=1, device_id=at, device_id_type=MESH)
+
 
     def share_stage(e, stage):
-        if stage == 0:
-            return getattr(S, f"one{e}"), r, nr, [(b, lax.rem(r + k, nr)) for k in range(1, nr)]
-        return getattr(S, f"two{e}"), b, nb, [(flip(b, m), r) for m in range(1, nb)]
+        buf = getattr(S, ("one" if stage == 0 else "two") + str(e))
+        if by_chip(e, nb * nz):
+            return (buf, c, 2) if stage == 0 else (buf, b * nz + z, nb * nz)
+        return (buf, r, nr) if stage == 0 else (buf, b, nb)
+
+    def share_peer(e, stage, k):
+        if by_chip(e, nb * nz):
+            if stage == 0:
+                return sibling
+            other = lax.rem(b * nz + z + k, nb * nz)
+            return (other // nz, 2 * lax.rem(other, nz) + c)
+        return (b, lax.rem(r + k, nr)) if stage == 0 else (lax.rem(b + k, nb), r)
 
     def share_send(e, stage, v):
-        buf, mine, size, peers = share_stage(e, stage)
+        buf, mine, size = share_stage(e, stage)
         buf[mine] = v
-        for peer in peers:
+
+        def one(k):
             pltpu.make_async_remote_copy(
-                buf.at[mine], buf.at[mine], S.stat_send.at[e, stage], S.stat_recv.at[e, stage], device_id=peer, device_id_type=MESH
+                buf.at[mine], buf.at[mine], S.stat_send.at[e, stage], S.stat_recv.at[e, stage],
+                device_id=share_peer(e, stage, k), device_id_type=MESH,
             ).start()
 
+        if size > 8:
+            pl.loop(1, size)(one)
+        else:
+            for k in range(1, size):
+                one(k)
+
     def share_wait(e, stage, merge):
-        buf, mine, size, peers = share_stage(e, stage)
+        buf, mine, size = share_stage(e, stage)
         got = buf.at[pl.ds(0, size - 1)]
         pltpu.make_async_copy(got, got, S.stat_recv.at[e, stage]).wait()
-        return merge(buf[...], float(n if stage == 0 else n * nr))
+        return merge(buf[...], float(n if stage == 0 else n * getattr(S, f"one{e}").shape[0]))
 
     def share(e, v, merge, work=None, more=None):
         share_send(e, 0, v)
-        if work:
+        if work and not by_chip(e, nb * nz):
             work()
         v = share_wait(e, 0, merge)
         share_send(e, 1, v)
+        if work and by_chip(e, nb * nz):
+            work()
         if more:
             more()
         return share_wait(e, 1, merge)
@@ -354,8 +403,9 @@
 
         def some(g, acc):
             for u in range(unit):
-                s = part * (total // parts) + g * unit + u
-                p = S.idx[s]
+                start = part * (total // parts) + g * unit
+                s = start + u
+                p = S.idx[start // 128, lax.rem(start, 128) + u]
                 acc = [jnp.where(spot == p, s, a) for spot, a in zip(spots, acc)]
             return acc
 
@@ -380,12 +430,17 @@
         ld_a, ld_b, ld_t = load(3, S.a_hbm, ta), load(4, S.b_hbm, tb), load(5, S.c_hbm, tc)
         for copy in (ld_b, ld_a, ld_t):
             copy.start()
+        ld_s.wait()
+        S.at_v[...] = table_place(S.at_v[...])
+        to_scalar = pltpu.make_async_copy(S.at_v, S.idx, S.load_sem.at[8])
+        to_scalar.start()
         ld_m.wait()
         for j in range(4):
             S.tmp[pl.ds(j, own, stride=4), :] = S.master[:, j * 128 : (j + 1) * 128]
         rows_in[place(0, z, c)] = S.tmp[...].astype(bf16)
-        pl.semaphore_wait(barrier, nr - 1 + nb - 1)
+        pl.semaphore_wait(barrier, nr - 1 + nb - 1 + (nb - 1) * (nz - 1))
         own_column(0)
+        to_scalar.wait()
         ld_x.wait()
         share_send(0, 0, jnp.concatenate(local(lambda s: S.x[s, :], n), axis=0))
         steps = max(nz - 1, 1)
@@ -416,8 +471,8 @@
         to_scalar.wait()
         tiles = total // 128
         late = (2 * C + 2 * FF) // 128
-        order(0, 2 * C // 128)
-        order(late, tiles)
+        order(0, C // 128)
+        order(tiles - 2, tiles)
 
         for m in range(nb):
 
@@ -462,6 +517,8 @@
         halo_up = halo(0, mine, S.wide.at[pl.ds(2 * n, n)], True)
         halo_down = halo(1, mine, S.wide.at[pl.ds(0, n)], False)
         halo_start(halo_up, halo_down)
+        order(late, tiles - 2)
+        order(C // 128, 2 * C // 128)
 
         ld_b.wait()
 
@@ -738,11 +795,20 @@
                 S.prod_s[im, :] = (sr * ui - si * ur).astype(bf16)
 
         ld_at.wait()
-        S.halo_out[0] = dot(tat[pl.ds(0, n), :], S.prod_k[...]).astype(bf16)
-        S.halo_out[1] = dot(tat[pl.ds(2 * n, n), :], S.prod_k[...]).astype(bf16)
         halo_up = halo(2, S.halo_out.at[0], S.halo_in.at[1], True)
         halo_down = halo(3, S.halo_out.at[1], S.halo_in.at[0], False)
-        halo_start(halo_up, halo_down)
+        S.halo_out[0] = dot(tat[pl.ds(0, n), :], S.prod_k[...]).astype(bf16)
+
+        @pl.when(has_above)
+        def _():
+            halo_up.start()
+
+        S.halo_out[1] = dot(tat[pl.ds(2 * n, n), :], S.prod_k[...]).astype(bf16)
+
+        @pl.when(has_below)
+        def _():
+            halo_down.start()
+
         S.p_val[...] = dot(tat[pl.ds(n, n), :], S.prod_k[...])
         ld_bt.wait()
 
@@ -786,7 +852,7 @@
     plan = reduce_plan(nb)
     parts = len(plan)
     size = lines // parts
-    unit = 96 if own % 96 == 0 else 8
+    unit = 64 if own % 64 == 0 else 8
     tmp = S.tmp
     hop_base = nz * nb
     z_base = hop_base + nz * (nb - 1)
@@ -802,8 +868,9 @@
 
             @pl.loop(0, own // unit)
             def _(g):
+                at = start + g * unit
                 for u in range(unit):
-                    tmp[pl.ds(pl.multiple_of((g * unit + u) * 4, 4), 4), :] = grad[S.idx[start + g * unit + u]]
+                    tmp[pl.ds(pl.multiple_of((g * unit + u) * 4, 4), 4), :] = grad[S.idx[at // 128, lax.rem(at, 128) + u]]
 
         def to_sibling(i, m):
             return pltpu.make_async_remote_copy(
@@ -835,7 +902,7 @@
             pltpu.make_async_copy(whole, whole, sem.at[i, p, t]).wait()
 
         def for_sibling(i):
-            for m in range(nb):
+            for m in reversed(range(nb)):
                 collect(m, column(i), 1 - c)
                 sib_out[i, m] = tmp[...].astype(bf16)
                 to_sibling(i, m).start()
@@ -847,10 +914,6 @@
             )
 
         def first_step(i):
-            @pl.when(i < nz - 1)
-            def _():
-                for_sibling(i + 1)
-
             for m in reversed(range(nb)):
                 collect(m, column(i), c)
                 to_sibling(i, m).wait_recv()
@@ -858,6 +921,10 @@
                 for p in range(parts):
                     if m in plan[p][0][1]:
                         hop(i, p, 0, m).start()
+
+            @pl.when(i < nz - 1)
+            def _():
+                for_sibling(i + 1)
 
         def next_step(i, t):
             for p in range(parts):
@@ -894,7 +961,8 @@
             chunks(n, last)
             gin_copy.start()
             for i in range(own):
-                p = S.idx[(b * nr + r) * own + i]
+                at = (b * nr + r) * own + i // unit * unit
+                p = S.idx[at // 128, lax.rem(at, 128) + i % unit]
                 fast = (p >= 2 * C + 2 * FF + KL * KL) & ((p < BASE) | (p >= BASE + KS * KS))
                 S.rate[pl.ds(i, 1), :] = jnp.full((1, 128), jnp.where(fast, np.float32(norm_rate), np.float32(matrix_rate)), f32)
 
@@ -947,22 +1015,22 @@
     pl.run_scoped(tail, low_block(nz, nb), low_block(nz, nb), low_block(nz))
     for e in range(len(WIDTHS)):
         for stage in range(2):
-            buf, mine, count, peers = share_stage(e, stage)
+            buf, mine, count = share_stage(e, stage)
             sent = buf.at[pl.ds(0, count - 1)]
             pltpu.make_async_copy(sent, sent, S.stat_send.at[e, stage]).wait()
     out_copy.wait()
 
 
-def step(x, cot, master, places, nb, nr):
+def step(x, cot, master, slots, nb, nr):
     (a, at, b, bt, bs, bst, c, ct) = tables()
     n, own, nz, parts = x.shape[0], master.shape[0], nr // 2, nb.bit_length() - 1
-    total = places.shape[0]
+    total = slots.size
     vm = lambda *shape: pltpu.VMEM(shape, f32)
     low = lambda *shape: pltpu.VMEM(shape, bf16)
     dma = lambda *shape: pltpu.SemaphoreType.DMA(shape)
     vmem, anywhere = pl.BlockSpec(memory_space=pltpu.VMEM), pl.BlockSpec(memory_space=pl.ANY)
     ins = dict(
-        idx=(places, pl.BlockSpec(memory_space=pltpu.SMEM)), x_hbm=(x, anywhere), cot_hbm=(cot, anywhere), master_hbm=(master, anywhere),
+        slots_hbm=(slots, anywhere), x_hbm=(x, anywhere), cot_hbm=(cot, anywhere), master_hbm=(master, anywhere),
         a_hbm=(a, anywhere), at_hbm=(at, anywhere), b_hbm=(b, anywhere), bt_hbm=(bt, anywhere), bs=(bs, vmem), bst=(bst, vmem),
         c_hbm=(c, anywhere), ct_hbm=(ct, anywhere),
     )
@@ -973,7 +1041,8 @@
     )
     scratch = dict(
         rows_in=low(nb * nr, 4 * own, 128), flat=vm(4 * total, 128), tab=low(total, C), x=vm(n, C), cot=vm(n, C), master=vm(own, C),
-        tmp=vm(4 * own, 128), chunk=vm(512, 128), inv=pltpu.VMEM((total // 128, 128), jnp.int32),
+        tmp=vm(4 * own, 128), chunk=vm(512, 128), inv=pltpu.VMEM((total // 128, 128), jnp.int32), at_v=pltpu.VMEM((total // 128, 128), jnp.int32),
+        idx=pltpu.SMEM((total // 128, 128), jnp.int32),
         inv_at=pltpu.SMEM((total // 128, 128), jnp.int32), small=vm(48, C),
         pre_low=low(n, C), wide=low(3 * n, C), dz=vm(n, C), spec_u=vm(2 * NF, C), spec_l=vm(2 * NF, C), spec_s=vm(2 * NF, C),
         prod_l=low(2 * NF, C), prod_s=low(2 * NF, C), prod_k=low(2 * NF, C), d_l=vm(n, C), d_s=vm(n, C), s_val=vm(n, C),
@@ -981,10 +1050,11 @@
         halo_out=low(2, n, C), halo_in=low(2, n, C),
     )
     for e, w in enumerate(WIDTHS):
-        scratch[f"one{e}"] = vm(nr, w, C)
-        scratch[f"two{e}"] = vm(nb, w, C)
+        one, two = (2, nb * nz) if by_chip(e, nb * nz) else (nr, nb)
+        scratch[f"one{e}"] = vm(one, w, C)
+        scratch[f"two{e}"] = vm(two, w, C)
     scratch.update(
-        load_sem=dma(8), stat_send=dma(len(WIDTHS), 2), stat_recv=dma(len(WIDTHS), 2), halo_send=dma(4), halo_recv=dma(4),
+        load_sem=dma(9), stat_send=dma(len(WIDTHS), 2), stat_recv=dma(len(WIDTHS), 2), halo_send=dma(4), halo_recv=dma(4),
         z_send=dma(nz), z_recv=dma(nz), b_send=dma(nb, nz), b_recv=dma(nb, nz), half_send=dma(2, nz), half_recv=dma(2, nz),
         core_send=dma(nb, nz), core_recv=dma(nb, nz), sib_send=dma(nz, nb), sib_recv=dma(nz, nb),
         hop_send=dma(nz, parts, parts), hop_recv=dma(nz, parts, parts), own_send=dma(nz), own_recv=dma(nz),
@@ -1059,30 +1129,11 @@
     )(*ins)
 
 
-def table_place(t):
-    start = 2 * C + 2 * FF
-    k_end = start + KL * KL
-    s_end = k_end + KS * KS
-    m_gain = s_end + 10
-    m_bias = m_gain + FF // C
-    m_end = m_bias + FF // C
-    up = t - 2 * C
-    up = 2 * C + up % (FF // C) * C + up // (FF // C)
-    base = start + 976
-    unused = t - m_end
-    unused = jnp.where(unused < 15, k_end + unused, jnp.where(unused < 18, base + 29 + unused - 15, base + 46 + unused - 18))
-    p = jnp.where((t >= 2 * C) & (t < 2 * C + FF), up, t)
-    p = jnp.where(t >= k_end, t - k_end + base, p)
-    p = jnp.where(t >= s_end, t - s_end + base + 32, p)
-    p = jnp.where(t >= m_bias, t - m_bias + base + 25, p)
-    return jnp.where(t >= m_end, unused, p)
-
-
 def body(image_in, cotangent, slot_rows, master, first_moment, second_moment):
     n = image_in.shape[0] * image_in.shape[1] * image_in.shape[2]
     nb, nr = lax.axis_size("batch"), lax.axis_size("rows")
     out, grad_in, reduced, rates = step(
-        image_in.reshape(n, C), cotangent.reshape(n, C), master, table_place(slot_rows), nb, nr
+        image_in.reshape(n, C), cotangent.reshape(n, C), master, slot_rows.reshape(-1, 128), nb, nr
     )
     result, grad_x, *slots = finish(reduced, first_moment, second_moment, master, rates, out, grad_in)
     return (result.reshape(image_in.shape), grad_x.reshape(image_in.shape), *slots)

time: 155 us -> 152 us (0.981)
  Pallas kernels: 153 us -> 151 us
where the time goes in v7:
time: 152 us
  Pallas kernels  151 us (99%)
    pallas_call x1, Pallas kernels, step(): pl.pallas_call(functools.partial(step_kernel, nb, nr, [*ins, *outs, *scra...  148 us
    pallas_call x1, Pallas kernels, finish(): pl.pallas_call(finish_kernel, out_shape=outs, in_specs=[anywhere] * 7, ou...  3.28 us

profile of v7, /device:TPU:0, one launch (start us, length us, event | category | flops | bytes accessed | tf_op | source)
XLA Modules:
  0.0 152.3 jit_solution(2609792161860920845)
XLA Ops:
  0.6 148.2 %shard_map.189 = (f32[256,512]{1,0:T(8,128)}, f32[256,512]{1,0:T(8,128)}, f32[192,512]{1,0:T(8,128)}, f32[192,128]{1,0:T(8,128)}) custom-call(s32[48,128]{1,0:T(8,128)} %bitcast.7, f32[256,512]{1,0:T(8,128)} %bitcast.5, f32[256,512]{1,0:T(8,128)} %bitcast.6, f32[192,512]{1,0:T(8,128)} %refs_4_.2, bf16[1536,768]{1,0:T(8,128)(2,1)} %constant.16.clone.refs_4_, ...), custom_call_target="tpu_custom_call" | custom-call | tf_op jit(solution)/shard_map/pallas_call | solution.py:1062
  148.8 3.3 %shard_map.190 = (f32[256,512]{1,0:T(8,128)}, f32[256,512]{1,0:T(8,128)}, f32[192,512]{1,0:T(8,128)}, f32[192,512]{1,0:T(8,128)}, f32[192,512]{1,0:T(8,128)}, /*...) custom-call(f32[192,512]{1,0:T(8,128)} %get-tuple-element.18.refs_0_, f32[192,128]{1,0:T(8,128)} %get-tuple-element.19.refs_1_, ...), custom_call_target="tpu_custom_call" | custom-call | tf_op jit(solution)/shard_map/pallas_call | solution.py:1120

commit v8 on v7

--- a/solution.py
+++ b/solution.py
@@ -131,6 +131,10 @@
             steps.append((o, sent, kept))
         plan.append(steps)
     return plan
+
+
+def first_along_z(nb, lines):
+    return lines // 6 if nb == 4 and lines % 192 == 0 else 0
 
 
 def by_chip(e, chips):
@@ -851,7 +855,10 @@
 
     plan = reduce_plan(nb)
     parts = len(plan)
-    size = lines // parts
+    by_z = first_along_z(nb, lines)
+    main = lines - by_z
+    size = main // parts
+    z_size = by_z // parts
     unit = 64 if own % 64 == 0 else 8
     tmp = S.tmp
     hop_base = nz * nb
@@ -909,9 +916,59 @@
 
         def to_owner(i):
             return pltpu.make_async_remote_copy(
-                z_out.at[i], rows_in.at[z_base + i], S.own_send.at[i], S.own_recv.at[i],
+                z_out.at[i], rows_in.at[z_base + i, pl.ds(0, main)], S.own_send.at[i], S.own_recv.at[i],
                 device_id=(b, 2 * column(i) + c), device_id_type=MESH,
             )
+
+        def to_layer(i, m):
+            return pltpu.make_async_remote_copy(
+                pair.at[i, m, pl.ds(main, by_z)], S.layer_in.at[i, m], S.layer_send.at[i], S.layer_recv.at[i],
+                device_id=(b, 2 * column(i) + c), device_id_type=MESH,
+            )
+
+        def layer_wait(i, sem):
+            pltpu.make_async_copy(S.layer_in.at[i], S.layer_in.at[i], sem.at[i]).wait()
+
+        def z_rows(p):
+            return pl.ds(main + p * z_size, z_size)
+
+        def z_hop(p, t, m):
+            o, sent, kept = plan[p][t]
+            at, _ = slots(p, t)
+            return pltpu.make_async_remote_copy(
+                pair.at[nz - 1, m, z_rows(p)], S.z_hops.at[p, at + kept.index(m ^ (1 << o))], S.z_hop_send.at[p, t], S.z_hop_recv.at[p, t],
+                device_id=(flip(b, 1 << o), r), device_id_type=MESH,
+            )
+
+        def z_hop_wait(p, t, sem):
+            at, count = slots(p, t)
+            whole = S.z_hops.at[p, pl.ds(at, count)]
+            pltpu.make_async_copy(whole, whole, sem.at[p, t]).wait()
+
+        def z_start():
+            for i in range(nz - 1):
+                layer_wait(i, S.layer_recv)
+            for m in reversed(range(nb)):
+                v = pair[nz - 1, m, pl.ds(main, by_z)].astype(f32)
+                for i in range(nz - 1):
+                    v = v + S.layer_in[i, m].astype(f32)
+                pair[nz - 1, m, pl.ds(main, by_z)] = v.astype(bf16)
+                for p in range(parts):
+                    if m in plan[p][0][1]:
+                        z_hop(p, 0, m).start()
+
+        def z_next(t):
+            for p in range(parts):
+                z_hop_wait(p, t, S.z_hop_recv)
+                at, _ = slots(p, t)
+                for k, m in enumerate(plan[p][t][2]):
+                    v = pair[nz - 1, m, z_rows(p)].astype(f32) + S.z_hops[p, at + k].astype(f32)
+                    if t == parts - 1:
+                        tmp[z_rows(p), :] = v
+                        continue
+                    pair[nz - 1, m, z_rows(p)] = v.astype(bf16)
+                    if m in plan[p][t + 1][1]:
+                        z_hop(p, t + 1, m).start()
 
         def first_step(i):
             for m in reversed(range(nb)):
@@ -921,6 +978,11 @@
                 for p in range(parts):
                     if m in plan[p][0][1]:
                         hop(i, p, 0, m).start()
+                if by_z:
+
+                    @pl.when(i < nz - 1)
+                    def _():
+                        to_layer(i, m).start()
 
             @pl.when(i < nz - 1)
             def _():
@@ -946,7 +1008,7 @@
 
             @pl.when(i < nz - 1)
             def _():
-                z_out[i] = tmp[...].astype(bf16)
+                z_out[i] = tmp[pl.ds(0, main), :].astype(bf16)
                 to_owner(i).start()
 
         def grad_image():
@@ -979,6 +1041,12 @@
             def _():
                 share_send(7, 1, share_wait(7, 0, merge_sum))
 
+            if by_z:
+
+                @pl.when(q == nz - 1)
+                def _():
+                    z_start()
+
             for t in range(parts - 1):
 
                 @pl.when((q >= t + 1) & (q < nz + t + 1))
@@ -989,13 +1057,22 @@
             def _():
                 grad_image()
 
+            if by_z:
+
+                @pl.when(q == nz)
+                def _():
+                    for t in range(parts - 1):
+                        z_next(t)
+
             @pl.when(q >= parts)
             def _():
                 last_step(q - parts)
 
         for i in range(nz - 1):
             to_owner(i).wait_recv()
-            tmp[...] += rows_in[z_base + i].astype(f32)
+            tmp[pl.ds(0, main), :] += rows_in[z_base + i, pl.ds(0, main)].astype(f32)
+        if by_z:
+            z_next(parts - 1)
         for j in range(4):
             S.red[:, j * 128 : (j + 1) * 128] = tmp[pl.ds(j, own, stride=4), :]
 
@@ -1009,10 +1086,16 @@
 
         for i in range(nz - 1):
             to_owner(i).wait_send()
+            if by_z:
+                layer_wait(i, S.layer_send)
+        if by_z:
+            for p in range(parts):
+                for t in range(parts):
+                    z_hop_wait(p, t, S.z_hop_send)
         gin_copy.wait()
 
     low_block = lambda *lead: pltpu.VMEM(lead + (lines, 128), bf16)
-    pl.run_scoped(tail, low_block(nz, nb), low_block(nz, nb), low_block(nz))
+    pl.run_scoped(tail, low_block(nz, nb), low_block(nz, nb), pltpu.VMEM((nz, main, 128), bf16))
     for e in range(len(WIDTHS)):
         for stage in range(2):
             buf, mine, count = share_stage(e, stage)
@@ -1049,6 +1132,12 @@
         t_low=low(n, C), p_val=vm(n, C), mid=vm(n, C), c_low=low(n, C), gy_low=low(n, C), gp_low=low(n, C), g_f=vm(n, C), out=vm(n, C),
         halo_out=low(2, n, C), halo_in=low(2, n, C),
     )
+    by_z = first_along_z(nb, 4 * own)
+    if by_z:
+        scratch.update(
+            layer_in=low(nz - 1, nb, by_z, 128), z_hops=low(parts, nb - 1, by_z // parts, 128), layer_send=dma(nz), layer_recv=dma(nz),
+            z_hop_send=dma(parts, parts), z_hop_recv=dma(parts, parts),
+        )
     for e, w in enumerate(WIDTHS):
         one, two = (2, nb * nz) if by_chip(e, nb * nz) else (nr, nb)
         scratch[f"one{e}"] = vm(one, w, C)

time: 152 us -> 149 us (0.980)
  Pallas kernels: 151 us -> 148 us
    pallas_call x1, Pallas kernels: 148 us -> 145 us  [step(): pl.pallas_call(functools.partial(step_kernel, nb, nr, [*ins, *outs, *scra...]
where the time goes in v8:
time: 149 us
  Pallas kernels  148 us (99%)
    pallas_call x1, Pallas kernels, step(): pl.pallas_call(functools.partial(step_kernel, nb, nr, [*ins, *outs, *scra...  145 us
    pallas_call x1, Pallas kernels, finish(): pl.pallas_call(finish_kernel, out_shape=outs, in_specs=[anywhere] * 7, ou...  3.28 us

profile of v8, /device:TPU:0, one launch (start us, length us, event | category | flops | bytes accessed | tf_op | source)
XLA Modules:
  0.0 148.8 jit_solution(5572242530807542260)
XLA Ops:
  0.6 144.7 %shard_map.189 = (f32[256,512]{1,0:T(8,128)}, f32[256,512]{1,0:T(8,128)}, f32[192,512]{1,0:T(8,128)}, f32[192,128]{1,0:T(8,128)}) custom-call(s32[48,128]{1,0:T(8,128)} %bitcast.7, f32[256,512]{1,0:T(8,128)} %bitcast.5, f32[256,512]{1,0:T(8,128)} %bitcast.6, f32[192,512]{1,0:T(8,128)} %refs_4_.2, bf16[1536,768]{1,0:T(8,128)(2,1)} %constant.16.clone.refs_4_, ...), custom_call_target="tpu_custom_call" | custom-call | tf_op jit(solution)/shard_map/pallas_call | solution.py:1151
  145.3 3.3 %shard_map.190 = (f32[256,512]{1,0:T(8,128)}, f32[256,512]{1,0:T(8,128)}, f32[192,512]{1,0:T(8,128)}, f32[192,512]{1,0:T(8,128)}, f32[192,512]{1,0:T(8,128)}, /*...) custom-call(f32[192,512]{1,0:T(8,128)} %get-tuple-element.18.refs_0_, f32[192,128]{1,0:T(8,128)} %get-tuple-element.19.refs_1_, ...), custom_call_target="tpu_custom_call" | custom-call | tf_op jit(solution)/shard_map/pallas_call | solution.py:1209

commit v9 on v8

--- a/solution.py
+++ b/solution.py
@@ -289,113 +289,174 @@
     def place(m, zz, core):
         return flip(b, m) * nr + 2 * zz + core
 
+    spread = first_along_z(nb, lines)
+    rest = pl.ds(lines - spread, spread)
+
+    def lines_of(k):
+        return lines if k == 0 else lines - spread
+
+    def part(m, zz, core, k):
+        return rows_in.at[place(m, zz, core), pl.ds(0, lines_of(k))]
+
     def along_z(zz, up):
-        at = rows_in.at[place(0, zz, c)]
+        at = part(0, zz, c, 1)
         return pltpu.make_async_remote_copy(
             at, at, S.z_send.at[zz], S.z_recv.at[zz], device_id=(b, r + 2 if up else r - 2), device_id_type=MESH
         )
 
-    def to_peer(m, zz):
-        at = rows_in.at[place(0, zz, c)]
+    def to_peer(m, zz, k):
+        at = part(0, zz, c, k)
         return pltpu.make_async_remote_copy(
             at, at, S.b_send.at[m, zz], S.b_recv.at[m, zz], device_id=(flip(b, m), r), device_id_type=MESH
         )
 
-    def from_peer(m, zz):
-        at = rows_in.at[place(m, zz, c)]
+    def from_peer(m, zz, k):
+        at = part(m, zz, c, k)
         return pltpu.make_async_copy(at, at, S.b_recv.at[m, zz])
 
-    def half(m, zz, h, to):
-        at = rows_in.at[place(m, zz, c), pl.ds(h * (lines // 2), lines // 2)]
+    def half(m, zz, h, to, k):
+        size = lines_of(k) // 2
+        at = rows_in.at[place(m, zz, c), pl.ds(h * size, size)]
         return pltpu.make_async_remote_copy(
             at, at, S.half_send.at[h, zz], S.half_recv.at[h, zz], device_id=(flip(b, to), r), device_id_type=MESH
         )
 
-    def to_other_core(m, zz, core):
-        at = rows_in.at[place(m, zz, core)]
+    def to_other_core(m, zz, core, k):
+        at = part(m, zz, core, k)
         return pltpu.make_async_remote_copy(
             at, at, S.core_send.at[m, zz], S.core_recv.at[m, zz], device_id=sibling, device_id_type=MESH
         )
 
-    def cast(m, zz, core):
+    def cast(m, zz, core, k):
         d = place(m, zz, core)
-        S.flat[pl.ds(pl.multiple_of(d * lines, lines), lines), :] = rows_in[d].astype(f32)
-
-    def sends(zz):
-        for m in range(1, nb):
-            if not (square and m == 3):
-                to_peer(m, zz).start()
-        to_other_core(0, zz, c).start()
-        cast(0, zz, c)
-
-    def own_column(k):
+        S.flat[pl.ds(pl.multiple_of(d * lines, lines), lines_of(k)), :] = rows_in[d, pl.ds(0, lines_of(k))].astype(f32)
+
+    def rest_out(m, zz):
+        at = rows_in.at[place(m, z, c), rest]
+        return pltpu.make_async_remote_copy(
+            at, at, S.rest_send.at[m, zz], S.rest_recv.at[m, z], device_id=(b, 2 * zz + c), device_id_type=MESH
+        )
+
+    def rest_in(m, zz):
+        at = rows_in.at[place(m, zz, c), rest]
+        return pltpu.make_async_copy(at, at, S.rest_recv.at[m, zz])
+
+    def rest_to_core(m, zz, core):
+        at = rows_in.at[place(m, zz, core), rest]
+        return pltpu.make_async_remote_copy(
+            at, at, S.rest_core_send.at[m, zz], S.rest_core_recv.at[m, zz], device_id=sibling, device_id_type=MESH
+        )
+
+    def rest_cast(m, zz, core):
+        d = place(m, zz, core)
+        S.flat[pl.ds(pl.multiple_of(d * lines + lines - spread, 64), spread), :] = rows_in[d, rest].astype(f32)
+
+    direct = [m for m in range(1, nb) if not (square and m == 3)]
+
+    def each(k, fn):
         if k == 0:
+            fn(z, True, True)
+            return
+
+        @pl.when(z >= k)
+        def _():
+            fn(z - k, True, False)
+
+        @pl.when(z + k < nz)
+        def _():
+            fn(z + k, False, True)
+
+    def onward(zz, below, above, act):
+        if below:
 
             @pl.when(z < nz - 1)
             def _():
-                along_z(z, True).start()
+                act(along_z(zz, True))
+
+        if above:
 
             @pl.when(z > 0)
             def _():
-                along_z(z, False).start()
-
-            sends(z)
-            return
-
-        @pl.when(z >= k)
-        def _():
-            along_z(z - k, True).wait_recv()
-
-            @pl.when(z < nz - 1)
-            def _():
-                along_z(z - k, True).start()
-
-            sends(z - k)
-
-        @pl.when(z + k < nz)
-        def _():
-            along_z(z + k, False).wait_recv()
-
-            @pl.when(z > 0)
-            def _():
-                along_z(z + k, False).start()
-
-            sends(z + k)
-
-    def each(k, fn):
-        if k == 0:
-            fn(z)
-            return
-
-        @pl.when(z >= k)
-        def _():
-            fn(z - k)
-
-        @pl.when(z + k < nz)
-        def _():
-            fn(z + k)
-
-    def pass_on(zz):
-        for m in range(1, nb):
-            if square and m == 3:
-                continue
-            from_peer(m, zz).wait()
-            if square:
-                half(m, zz, 2 - m, 3 - m).start()
-            to_other_core(m, zz, c).start()
-            cast(m, zz, c)
-
-    def corner(zz):
+                act(along_z(zz, False))
+
+    def own_column(k):
+        def go(zz, below, above):
+            if k:
+                along_z(zz, below).wait_recv()
+            onward(zz, below, above, lambda copy: copy.start())
+            for m in direct:
+                to_peer(m, zz, k).start()
+            to_other_core(0, zz, c, k).start()
+            cast(0, zz, c, k)
+
+        each(k, go)
+
+    def pass_on(k):
+        def go(zz, below, above):
+            for m in direct:
+                from_peer(m, zz, k).wait()
+                if square:
+                    half(m, zz, 2 - m, 3 - m, k).start()
+                to_other_core(m, zz, c, k).start()
+                cast(m, zz, c, k)
+
+        each(k, go)
+
+    def corner(k):
+        def go(zz, below, above):
+            for h in range(2):
+                half(3, zz, h, 0, k).wait_recv()
+            if k == 0 and spread:
+                for d in range(1, nz):
+                    for m in range(nb):
+                        rest_out(m, lax.rem(z + d, nz)).start()
+            to_other_core(3, zz, c, k).start()
+            cast(3, zz, c, k)
+
         if square:
-            for h in range(2):
-                half(3, zz, h, 0).wait_recv()
-            to_other_core(3, zz, c).start()
-            cast(3, zz, c)
-
-    def other_core(zz):
-        for m in range(nb):
-            to_other_core(m, zz, 1 - c).wait_recv()
-            cast(m, zz, 1 - c)
+            each(k, go)
+
+    def other_core(k):
+        def go(zz, below, above):
+            for m in range(nb):
+                to_other_core(m, zz, 1 - c, k).wait_recv()
+                cast(m, zz, 1 - c, k)
+
+        each(k, go)
+
+    def rest_here(k):
+        def go(zz, below, above):
+            for m in range(nb):
+                rest_in(m, zz).wait()
+                rest_to_core(m, zz, c).start()
+                rest_cast(m, zz, c)
+
+        if spread:
+            each(k, go)
+
+    def rest_there(k):
+        def go(zz, below, above):
+            for m in range(nb):
+                rest_to_core(m, zz, 1 - c).wait_recv()
+                rest_cast(m, zz, 1 - c)
+
+        if spread:
+            each(k, go)
+
+    def gather_sent(k):
+        def go(zz, below, above):
+            onward(zz, below, above, lambda copy: copy.wait_send())
+            for m in direct:
+                to_peer(m, zz, k).wait_send()
+                if square:
+                    half(m, zz, 2 - m, 3 - m, k).wait_send()
+            for m in range(nb):
+                to_other_core(m, zz, c, k).wait_send()
+                if spread and k:
+                    rest_out(m, zz).wait_send()
+                    rest_to_core(m, zz, c).wait_send()
+
+        each(k, go)
 
     def find(part, parts):
         tiles = total // 1024
@@ -407,14 +468,15 @@
 
         def some(g, acc):
             for u in range(unit):
-                start = part * (total // parts) + g * unit
+                start = g * unit
                 s = start + u
                 p = S.idx[start // 128, lax.rem(start, 128) + u]
                 acc = [jnp.where(spot == p, s, a) for spot, a in zip(spots, acc)]
             return acc
 
         acc = [S.inv[k * 8 : k * 8 + 8, :] if part else jnp.zeros((8, 128), jnp.int32) for k in range(tiles)]
-        acc = lax.fori_loop(0, total // parts // unit, some, acc)
+        groups = total // unit
+        acc = lax.fori_loop(groups * part // parts, groups * (part + 1) // parts, some, acc)
         for k in range(tiles):
             S.inv[k * 8 : k * 8 + 8, :] = acc[k]
 
@@ -447,28 +509,35 @@
         to_scalar.wait()
         ld_x.wait()
         share_send(0, 0, jnp.concatenate(local(lambda s: S.x[s, :], n), axis=0))
-        steps = max(nz - 1, 1)
+        steps = 3 * max(nz - 1, 1)
         for k in range(1, nz):
-            find(k - 1, steps)
+            find(3 * k - 3, steps)
             own_column(k)
-            each(k - 1, pass_on)
+            find(3 * k - 2, steps)
+            pass_on(k - 1)
+            find(3 * k - 1, steps)
             if k > 1:
-                each(k - 2, corner)
+                corner(k - 2)
             if k > 2:
-                each(k - 3, other_core)
+                other_core(k - 3)
             if k == 1:
                 share_send(0, 1, share_wait(0, 0, merge_stats(1)))
         if nz == 1:
-            find(0, 1)
+            for part in range(3):
+                find(part, 3)
             share_send(0, 1, share_wait(0, 0, merge_stats(1)))
         to_scalar = pltpu.make_async_copy(S.inv, S.inv_at, S.load_sem.at[6])
         to_scalar.start()
-        each(nz - 1, pass_on)
-        if nz > 1:
-            each(nz - 2, corner)
-        each(nz - 1, corner)
+        pass_on(nz - 1)
+        for k in range(max(nz - 2, 0), nz - 1):
+            corner(k)
+        for k in range(1, nz):
+            rest_here(k)
+        corner(nz - 1)
         for k in range(max(nz - 3, 0), nz):
-            each(k, other_core)
+            other_core(k)
+        for k in range(1, nz):
+            rest_there(k)
         tot = share_wait(0, 1, merge_stats(1))
         m_x, q_x = tot[0:1], tot[1:2] * (1.0 / every)
         inv_x = lax.rsqrt(q_x + norm_eps)
@@ -478,25 +547,8 @@
         order(0, C // 128)
         order(tiles - 2, tiles)
 
-        for m in range(nb):
-
-            @pl.loop(0, nz)
-            def _(zz):
-                to_other_core(m, zz, c).wait_send()
-                if m and not (square and m == 3):
-                    to_peer(m, zz).wait_send()
-                if square and m in (1, 2):
-                    half(m, zz, 2 - m, 3 - m).wait_send()
-
         for k in range(nz):
-
-            @pl.when((z >= k) & (z < nz - 1))
-            def _():
-                along_z(z - k, True).wait_send()
-
-            @pl.when((z + k < nz) & (z > 0))
-            def _():
-                along_z(z + k, False).wait_send()
+            gather_sent(k)
 
         small = S.tab[pl.ds(BASE, 48), :].astype(f32)
         S.small[...] = small
@@ -1145,7 +1197,8 @@
     scratch.update(
         load_sem=dma(9), stat_send=dma(len(WIDTHS), 2), stat_recv=dma(len(WIDTHS), 2), halo_send=dma(4), halo_recv=dma(4),
         z_send=dma(nz), z_recv=dma(nz), b_send=dma(nb, nz), b_recv=dma(nb, nz), half_send=dma(2, nz), half_recv=dma(2, nz),
-        core_send=dma(nb, nz), core_recv=dma(nb, nz), sib_send=dma(nz, nb), sib_recv=dma(nz, nb),
+        core_send=dma(nb, nz), core_recv=dma(nb, nz), rest_send=dma(nb, nz), rest_recv=dma(nb, nz),
+        rest_core_send=dma(nb, nz), rest_core_recv=dma(nb, nz), sib_send=dma(nz, nb), sib_recv=dma(nz, nb),
         hop_send=dma(nz, parts, parts), hop_recv=dma(nz, parts, parts), own_send=dma(nz), own_recv=dma(nz),
     )
     return pl.pallas_call(

time: 149 us -> 147 us (0.987)
  Pallas kernels: 148 us -> 146 us
    pallas_call x1, Pallas kernels: 145 us -> 142 us  [step(): pl.pallas_call(functools.partial(step_kernel, nb, nr, [*ins, *outs, *scra...]
where the time goes in v9:
time: 147 us
  Pallas kernels  146 us (99%)
    pallas_call x1, Pallas kernels, step(): pl.pallas_call(functools.partial(step_kernel, nb, nr, [*ins, *outs, *scra...  142 us
    pallas_call x1, Pallas kernels, finish(): pl.pallas_call(finish_kernel, out_shape=outs, in_specs=[anywhere] * 7, ou...  3.28 us

profile of v9, /device:TPU:0, one launch (start us, length us, event | category | flops | bytes accessed | tf_op | source)
XLA Modules:
  0.0 146.6 jit_solution(16834251789874444520)
XLA Ops:
  0.6 142.5 %shard_map.189 = (f32[256,512]{1,0:T(8,128)}, f32[256,512]{1,0:T(8,128)}, f32[192,512]{1,0:T(8,128)}, f32[192,128]{1,0:T(8,128)}) custom-call(s32[48,128]{1,0:T(8,128)} %bitcast.7, f32[256,512]{1,0:T(8,128)} %bitcast.5, f32[256,512]{1,0:T(8,128)} %bitcast.6, f32[192,512]{1,0:T(8,128)} %refs_4_.2, bf16[1536,768]{1,0:T(8,128)(2,1)} %constant.16.clone.refs_4_, ...), custom_call_target="tpu_custom_call" | custom-call | tf_op jit(solution)/shard_map/pallas_call | solution.py:1204
  143.1 3.3 %shard_map.190 = (f32[256,512]{1,0:T(8,128)}, f32[256,512]{1,0:T(8,128)}, f32[192,512]{1,0:T(8,128)}, f32[192,512]{1,0:T(8,128)}, f32[192,512]{1,0:T(8,128)}, /*...) custom-call(f32[192,512]{1,0:T(8,128)} %get-tuple-element.18.refs_0_, f32[192,128]{1,0:T(8,128)} %get-tuple-element.19.refs_1_, ...), custom_call_target="tpu_custom_call" | custom-call | tf_op jit(solution)/shard_map/pallas_call | solution.py:1262

commit v10 on v9

--- a/solution.py
+++ b/solution.py
@@ -516,8 +516,8 @@
             find(3 * k - 2, steps)
             pass_on(k - 1)
             find(3 * k - 1, steps)
-            if k > 1:
-                corner(k - 2)
+            if k == 2:
+                corner(0)
             if k > 2:
                 other_core(k - 3)
             if k == 1:
@@ -529,7 +529,7 @@
         to_scalar = pltpu.make_async_copy(S.inv, S.inv_at, S.load_sem.at[6])
         to_scalar.start()
         pass_on(nz - 1)
-        for k in range(max(nz - 2, 0), nz - 1):
+        for k in range(1 if nz > 2 else 0, nz - 1):
             corner(k)
         for k in range(1, nz):
             rest_here(k)

time: 147 us -> 147 us (level)
  no operation moved by 1% of the time
where the time goes in v10:
time: 147 us
  Pallas kernels  146 us (99%)
    pallas_call x1, Pallas kernels, step(): pl.pallas_call(functools.partial(step_kernel, nb, nr, [*ins, *outs, *scra...  142 us
    pallas_call x1, Pallas kernels, finish(): pl.pallas_call(finish_kernel, out_shape=outs, in_specs=[anywhere] * 7, ou...  3.28 us

profile of v10, /device:TPU:0, one launch (start us, length us, event | category | flops | bytes accessed | tf_op | source)
XLA Modules:
  0.0 146.6 jit_solution(13851611229782277134)
XLA Ops:
  0.6 142.5 %shard_map.189 = (f32[256,512]{1,0:T(8,128)}, f32[256,512]{1,0:T(8,128)}, f32[192,512]{1,0:T(8,128)}, f32[192,128]{1,0:T(8,128)}) custom-call(s32[48,128]{1,0:T(8,128)} %bitcast.7, f32[256,512]{1,0:T(8,128)} %bitcast.5, f32[256,512]{1,0:T(8,128)} %bitcast.6, f32[192,512]{1,0:T(8,128)} %refs_4_.2, bf16[1536,768]{1,0:T(8,128)(2,1)} %constant.16.clone.refs_4_, ...), custom_call_target="tpu_custom_call" | custom-call | tf_op jit(solution)/shard_map/pallas_call | solution.py:1204
  143.1 3.3 %shard_map.190 = (f32[256,512]{1,0:T(8,128)}, f32[256,512]{1,0:T(8,128)}, f32[192,512]{1,0:T(8,128)}, f32[192,512]{1,0:T(8,128)}, f32[192,512]{1,0:T(8,128)}, /*...) custom-call(f32[192,512]{1,0:T(8,128)} %get-tuple-element.18.refs_0_, f32[192,128]{1,0:T(8,128)} %get-tuple-element.19.refs_1_, ...), custom_call_target="tpu_custom_call" | custom-call | tf_op jit(solution)/shard_map/pallas_call | solution.py:1262

commit v11 on v10

--- a/solution.py
+++ b/solution.py
@@ -289,7 +289,7 @@
     def place(m, zz, core):
         return flip(b, m) * nr + 2 * zz + core
 
-    spread = first_along_z(nb, lines)
+    spread = first_along_z(nb, lines) * 3 // 4
     rest = pl.ds(lines - spread, spread)
 
     def lines_of(k):
@@ -349,7 +349,7 @@
 
     def rest_cast(m, zz, core):
         d = place(m, zz, core)
-        S.flat[pl.ds(pl.multiple_of(d * lines + lines - spread, 64), spread), :] = rows_in[d, rest].astype(f32)
+        S.flat[pl.ds(pl.multiple_of(d * lines + lines - spread, 32), spread), :] = rows_in[d, rest].astype(f32)
 
     direct = [m for m in range(1, nb) if not (square and m == 3)]
 

time: 147 us -> 146 us (level)
  no operation moved by 1% of the time
where the time goes in v11:
time: 146 us
  Pallas kernels  145 us (99%)
    pallas_call x1, Pallas kernels, step(): pl.pallas_call(functools.partial(step_kernel, nb, nr, [*ins, *outs, *scra...  142 us
    pallas_call x1, Pallas kernels, finish(): pl.pallas_call(finish_kernel, out_shape=outs, in_specs=[anywhere] * 7, ou...  3.28 us

profile of v11, /device:TPU:0, one launch (start us, length us, event | category | flops | bytes accessed | tf_op | source)
XLA Modules:
  0.0 145.6 jit_solution(14477651825425569518)
XLA Ops:
  0.6 141.5 %shard_map.189 = (f32[256,512]{1,0:T(8,128)}, f32[256,512]{1,0:T(8,128)}, f32[192,512]{1,0:T(8,128)}, f32[192,128]{1,0:T(8,128)}) custom-call(s32[48,128]{1,0:T(8,128)} %bitcast.7, f32[256,512]{1,0:T(8,128)} %bitcast.5, f32[256,512]{1,0:T(8,128)} %bitcast.6, f32[192,512]{1,0:T(8,128)} %refs_4_.2, bf16[1536,768]{1,0:T(8,128)(2,1)} %constant.16.clone.refs_4_, ...), custom_call_target="tpu_custom_call" | custom-call | tf_op jit(solution)/shard_map/pallas_call | solution.py:1204
  142.2 3.3 %shard_map.190 = (f32[256,512]{1,0:T(8,128)}, f32[256,512]{1,0:T(8,128)}, f32[192,512]{1,0:T(8,128)}, f32[192,512]{1,0:T(8,128)}, f32[192,512]{1,0:T(8,128)}, /*...) custom-call(f32[192,512]{1,0:T(8,128)} %get-tuple-element.18.refs_0_, f32[192,128]{1,0:T(8,128)} %get-tuple-element.19.refs_1_, ...), custom_call_target="tpu_custom_call" | custom-call | tf_op jit(solution)/shard_map/pallas_call | solution.py:1262
